TPU v7x, 256 devices: a whole 4x4x8 slice. The times are simulated.
256 devices in a mesh: row: 32 (over x_lo, z, core), col: 8 (over x_hi, y).
Axes of the slice: x: 4 (x_hi: 2, x_lo: 2; x = x_hi * 2 + x_lo), y: 4, z: 8, core: 2. Of those that a mesh axis runs over, the one named last changes fastest.
Arguments:
- ham: bfloat16 [8192, 8192], P('row'), may hold values from -0.2 to 1.7, as said below
- coeff: bfloat16 [8192, 8192], P('row', 'col'), may hold values from -40 to 40, as said below
- tile_mask: int32 [256, 256], P('row'), may hold values from 0 to 1, as said below
- occupation: int32 [16, 8192], replicated, may hold values from 0 to 1, as said below
- orbital_energy: float32 [16], replicated, may hold values from -0.4 to 0.6
- coulomb: float32 [16, 16], replicated, may hold values from 0.005 to 0.04
Outputs:
- correction: float32 [8192, 8192], P('row', 'col')
- stats: float32 [2], replicated
Inputs may be any that keep to these rules, and one draw needn't show every extreme that they name: ham is symmetric. coeff is symmetric. tile_mask is symmetric with ones on its diagonal. `occupation`: every column holds exactly 6 ones.
All inputs are finite; a program needn't handle non-finite values.
Results may differ from a plain program's by a relative error of at most 0.0003.
Values may be sent and summed in bfloat16 or wider, within the bound.
No kernel may reach another device: no remote copies, remote signals or barrier semaphores. Data moves between devices by JAX's collectives and lax.ppermute only.
A program may use at most 128 MiB of HBM per device.

v0:
```python
import jax
import jax.numpy as jnp
from jax import lax
from jax.sharding import PartitionSpec as P

NS = 8192


def turn_tiles(product):
    tile_rows, tile_cols = product.shape
    row_count = lax.axis_size("row")
    col_count = lax.axis_size("col")
    fold_count = row_count // col_count
    sub_rows = tile_rows // row_count
    sectioned = product.reshape(row_count, sub_rows, tile_cols)
    sectioned = lax.all_to_all(
        lax.all_to_all(sectioned, "row", split_axis=0, concat_axis=0, tiled=True),
        "col",
        split_axis=0,
        concat_axis=0,
        tiled=True,
    )
    sectioned = sectioned.reshape(col_count, fold_count, sub_rows, fold_count, tile_rows)
    sectioned = jnp.transpose(sectioned, (0, 3, 1, 2, 4)).reshape(
        row_count, fold_count * sub_rows, tile_rows
    )
    sectioned = lax.all_to_all(sectioned, "row", split_axis=0, concat_axis=0, tiled=True)
    sectioned = sectioned.reshape(row_count, fold_count, sub_rows, tile_rows)
    turned = jnp.transpose(sectioned, (3, 1, 0, 2)).reshape(tile_rows, tile_cols)
    return turned


def body(ham, coeff, tile_mask, occupation, orbital_energy, coulomb):
    tile_rows, strings = ham.shape
    tile_cols = coeff.shape[1]
    mask_cols = tile_mask.shape[1]
    block_size = strings // mask_cols
    mask_rows = tile_rows // block_size
    weights = tile_mask.astype(jnp.bfloat16)[:, None, :, None]
    masked = (ham.reshape(mask_rows, block_size, mask_cols, block_size) * weights).reshape(
        tile_rows, strings
    )
    occ_float = occupation.astype(jnp.float32)
    occ_alpha = lax.dynamic_slice_in_dim(occ_float, lax.axis_index("row") * tile_rows, tile_rows, 1)
    occ_beta = lax.dynamic_slice_in_dim(occ_float, lax.axis_index("col") * tile_cols, tile_cols, 1)
    energy_alpha = jnp.dot(orbital_energy, occ_alpha, precision=lax.Precision.HIGHEST)
    energy_beta = jnp.dot(orbital_energy, occ_beta, precision=lax.Precision.HIGHEST)
    coupling = jnp.dot(
        jnp.dot(occ_alpha.T, coulomb, precision=lax.Precision.HIGHEST),
        occ_beta,
        precision=lax.Precision.HIGHEST,
    )
    diagonal = energy_alpha[:, None] + energy_beta[None, :] + coupling
    product = jnp.dot(
        masked, lax.all_gather(coeff, "row", axis=0, tiled=True), preferred_element_type=jnp.float32
    )
    coeff_float = coeff.astype(jnp.float32)
    sigma = product + turn_tiles(product)
    late = lax.psum(
        (jnp.sum(coeff_float * sigma), jnp.sum(coeff_float * coeff_float)), ("row", "col")
    )
    projection = late[0]
    weight_sum = late[1]
    theta = projection / weight_sum
    residual = sigma - theta * coeff_float
    update = residual / jnp.maximum(jnp.abs(diagonal - theta), 1.0)
    totals = lax.psum((jnp.sum(residual * residual), jnp.sum(update * update)), ("row", "col"))
    correction = update * lax.rsqrt(totals[1] / (NS * NS) + 1e-06)
    stats = jnp.stack([theta, jnp.sqrt(totals[0] / (NS * NS))])
    return (correction, stats)


def solution(mesh):
    in_specs = (P("row", None), P("row", "col"), P("row", None), P(), P(), P())
    out_specs = (P("row", "col"), P())
    return jax.shard_map(body, mesh=mesh, in_specs=in_specs, out_specs=out_specs, check_vma=False)
```

profile of v0, /device:TPU:1, one launch (start us, length us, event | category | flops | bytes accessed | tf_op | source)
XLA Modules:
  0.0 381.5 jit_solution(8685659466072624419)
XLA Ops:
  7.2 0.0 copy-start
  7.2 0.0 all-gather.2.cloned.1.call-start
  7.2 0.7 all-gather.2.cloned.1.call-update
  7.9 0.7 convert_element_type.9
  8.6 6.4 %mul.41 = bf16[8,32,256,32]{3,2,1,0:T(8,128)(2,1)} broadcast(bf16[8,256]{1,0:T(8,128)(2,1)S(1)} %convert_element_type.9), dimensions={0,2} | broadcast | bytes 4198400 | tf_op jit(solution)/shard_map/mul | solution.py:40
  15.0 21.9 %mul.42 = bf16[256,8192]{1,0:T(8,128)(2,1)} reshape(bf16[8,32,256,32]{3,2,1,0:T(8,128)(2,1)} %mul.41) | data formatting | bytes 8388608 | tf_op jit(solution)/shard_map/mul | solution.py:40
  36.9 77.0 %all-gather.2.cloned.1.call-done = bf16[8192,1024]{1,0:T(8,128)(2,1)} async-done(((bf16[256,1024]{1,0:T(8,128)(2,1)}), bf16[8192,1024]{1,0:T(8,128)(2,1)}) %all-gather.2.cloned.1.call-update) | async-done | bytes 16777232 | tf_op jit(solution)/shard_map/all_gather | solution.py:55
  113.9 10.5 %fusion = f32[256,1024]{1,0:T(8,128)S(1)} fusion(bf16[8192,1024]{1,0:T(8,128)(2,1)} %all-gather.2.cloned.1.call-done, bf16[256,8192]{1,0:T(8,128)(2,1)} %param.6, bf16[256,8192]{1,0:T(8,128)(2,1)} %mul.42), kind=kOutput, calls=%fused_computation | convolution fusion | flops 4297064448 | bytes 26214400 | tf_op jit(solution)/shard_map/dot_general | solution.py:54
  124.4 0.0 copy-start.2
  124.4 33.6 %all_to_all.15 = f32[32,8,1024]{2,1,0:T(8,128)S(1)} all-to-all(f32[32,8,1024]{2,1,0:T(8,128)S(1)} %bitcast.25), channel_id=1, replica_groups=mesh['row'=32,'col'=8] {'row'}, dimensions={0} | all-to-all | bytes 2097152 | tf_op jit(solution)/shard_map/all_to_all | solution.py:17
  158.0 0.0 copy-done.2
  158.0 20.1 %all_to_all.16 = f32[32,8,1024]{2,1,0:T(8,128)S(1)} all-to-all(f32[32,8,1024]{2,1,0:T(8,128)S(1)} %all_to_all.15), channel_id=1, replica_groups=mesh['row'=32,'col'=8] {'col'}, dimensions={0} | all-to-all | bytes 2097152 | tf_op jit(solution)/shard_map/all_to_all | solution.py:16
  178.2 0.5 reshape.26
  178.7 1.2 copy.10
  179.8 9.1 %all-to-all-start.2 = ((f32[32,32,256]{2,1,0:T(8,128)}), f32[32,32,256]{2,1,0:T(8,128)S(1)}, u32[]{:S(2)}, u32[]{:S(2)}) async-start(f32[32,32,256]{2,1,0:T(8,128)} %bitcast.2), calls=%async_computation.2 | async-start | bytes 2097152 | tf_op jit(solution)/shard_map/all_to_all | solution.py:27
  188.9 0.0 copy-done.3
  189.0 0.0 copy-done.4
  189.0 0.1 fusion.14
  189.1 0.2 fusion.10
  189.3 0.0 copy-done
  189.3 0.2 fusion.12
  189.5 25.9 %all-to-all-done.2 = f32[32,32,256]{2,1,0:T(8,128)S(1)} async-done(((f32[32,32,256]{2,1,0:T(8,128)}), f32[32,32,256]{2,1,0:T(8,128)S(1)}, u32[]{:S(2)}, u32[]{:S(2)}) %all-to-all-start.2) | async-done | bytes 1048608 | tf_op jit(solution)/shard_map/all_to_all | solution.py:27
  215.4 0.1 copy.11
  215.5 1.3 copy.12
  216.8 0.0 copy-done.1
  216.8 2.6 fusion.7
  219.4 74.3 %all-reduce.1 = (f32[]{:T(128)}, f32[]{:T(128)}) all-reduce(f32[]{:T(128)} %get-tuple-element.3, f32[]{:T(128)} %get-tuple-element.2), channel_id=1, replica_groups=mesh['row'=32,'col'=8] {'row','col'}, use_global_device_ids=true, to_apply=%region_1.0 | all-reduce | flops 2 | bytes 16 | tf_op jit(solution)/shard_map/psum | solution.py:59
  295.1 1.0 multiply_reduce_fusion
  296.0 2.1 multiply_reduce_fusion.1
  298.1 73.5 %all-reduce = (f32[]{:T(128)}, f32[]{:T(128)}) all-reduce(f32[]{:T(128)} %get-tuple-element.9, f32[]{:T(128)} %multiply_reduce_fusion), channel_id=1, replica_groups=mesh['row'=32,'col'=8] {'row','col'}, use_global_device_ids=true, to_apply=%region_5.0 | all-reduce | flops 2 | bytes 16 | tf_op jit(solution)/shard_map/psum | solution.py:67
  373.0 0.6 pad_maximum_fusion
  373.6 1.0 broadcast_multiply_fusion
  (4 shorter events, 0.0 us)
Async XLA Ops:
  7.2 182.1 %copy-start = (f32[16,16]{1,0:T(8,128)S(1)}, f32[16,16]{1,0:T(8,128)}, u32[]{:S(2)}) copy-start(f32[16,16]{1,0:T(8,128)} %param.11) | copy-start | bytes 3076
  7.2 106.7 %all-gather.2.cloned.1.call-start = ((), (), s32[]{:S(2)}) async-start(), calls=%async_computation.3 | async-start | bytes 17301504 | tf_op jit(solution)/shard_map/all_gather | solution.py:55
  124.4 33.6 %copy-start.2 = (f32[256,1024]{1,0:T(8,128)}, f32[256,1024]{1,0:T(8,128)S(1)}, u32[]{:S(2)}) copy-start(f32[256,1024]{1,0:T(8,128)S(1)} %fusion) | copy-start | bytes 3145732
  158.0 30.9 %copy-start.3 = (s32[16,8192]{1,0:T(8,128)S(1)}, s32[16,8192]{1,0:T(8,128)}, u32[]{:S(2)}) copy-start(s32[16,8192]{1,0:T(8,128)} %param.9) | copy-start | bytes 1572868
  178.2 10.8 %copy-start.4 = (f32[16]{0:T(128)S(1)}, f32[16]{0:T(128)}, u32[]{:S(2)}) copy-start(f32[16]{0:T(128)} %param.10) | copy-start | bytes 196
  179.8 37.0 %copy-start.1 = (bf16[256,1024]{1,0:T(8,128)(2,1)S(1)}, bf16[256,1024]{1,0:T(8,128)(2,1)}, u32[]{:S(2)}) copy-start(bf16[256,1024]{1,0:T(8,128)(2,1)} %param.7) | copy-start | bytes 1572868
  179.8 35.5 %all-to-all-start.2 = ((f32[32,32,256]{2,1,0:T(8,128)}), f32[32,32,256]{2,1,0:T(8,128)S(1)}, u32[]{:S(2)}, u32[]{:S(2)}) async-start(f32[32,32,256]{2,1,0:T(8,128)} %bitcast.2), calls=%async_computation.2 | async-start | bytes 2097152 | tf_op jit(solution)/shard_map/all_to_all | solution.py:27
Sparse Core Ops, SparseCore 0:
  9.9 103.9 all-gather.1
where the time goes:
time: 382 us; the launch traced here: 381 us
  blocking collectives  202 us (53%)
  waiting for transfers between devices  104 us (27%)
  local copies, waits for them, and re-layouts  31.4 us (8%)
  between operations  16.9 us (4%)
  matrix products  13.1 us (3%)
  starting transfers between devices  9.11 us (2%)
  other arithmetic  5.93 us (2%)
    all_gather x1, waiting for transfers between devices, body(): lax.all_gather(coeff, 'row', axis=0, tiled=True)  77 us
    psum x1, blocking collectives, body(): lax.psum((jnp.sum(coeff_float * sigma), jnp.sum(coeff_float * coeff_float...  74.3 us
    psum x1, blocking collectives, body(): lax.psum((jnp.sum(residual * residual), jnp.sum(update * update)), ('row'...  73.5 us
    all_to_all x1, blocking collectives, turn_tiles(): lax.all_to_all(sectioned, 'row', split_axis=0, concat_axis=0, tiled=True)  33.6 us
    mul x2, local copies, waits for them, and re-layouts, body(): ham.reshape(mask_rows, block_size, mask_cols, block_size) * weights  28.3 us
    all_to_all x1, waiting for transfers between devices, turn_tiles(): lax.all_to_all(sectioned, 'row', split_axis=0, concat_axis=0, tiled=True)  25.9 us
    all_to_all x1, blocking collectives, turn_tiles(): lax.all_to_all(lax.all_to_all(sectioned, 'row', split_axis=0, concat_axis...  20.1 us
    dot_general x1, matrix products, body(): jnp.dot(masked, lax.all_gather(coeff, 'row', axis=0, tiled=True), preferr...  10.5 us
  transfers between devices with their start and end apart: 2, of which 2 were waited for; matrix products, arithmetic and copies ran while one was open for 8% of the time, Pallas kernels for 0%

commit v1 on v0

v1 whole, which is shorter than its diff:
```python
import jax
import jax.numpy as jnp
from jax import lax
from jax.experimental import pallas as pl
from jax.experimental.pallas import tpu as pltpu
from jax.sharding import Mesh, PartitionSpec as P

NS = 8192
AXES = ("xlo", "z", "core", "xhi", "y")
SIZES = (2, 8, 2, 2, 4)
ROW = ("xlo", "z", "core")
COL = ("xhi", "y")
LANES = 128


def mask_kernel(own_ref, pair_ref, mask_own_ref, mask_pair_ref, out_ref):
    rows, cols = own_ref.shape
    mask_rows, mask_cols = mask_own_ref.shape
    size = cols // mask_cols
    tile = rows // mask_rows
    spread = (
        lax.broadcasted_iota(jnp.int32, (mask_cols, cols), 1) // size
        == lax.broadcasted_iota(jnp.int32, (mask_cols, cols), 0)
    ).astype(jnp.bfloat16)
    for panel, (ham_ref, mask_ref) in enumerate(
        ((own_ref, mask_own_ref), (pair_ref, mask_pair_ref))
    ):
        mask = mask_ref[...].astype(jnp.float32).astype(jnp.bfloat16)
        wide = jnp.dot(mask, spread, preferred_element_type=jnp.float32)
        for index in range(mask_rows):
            at = index * tile
            values = ham_ref[at : at + tile, :].astype(jnp.float32) * wide[index : index + 1, :]
            out_ref[panel * rows + at : panel * rows + at + tile, :] = values.astype(jnp.bfloat16)


def mask_panels(own, pair, mask_own, mask_pair):
    rows, cols = own.shape
    mask_rows, mask_cols = mask_own.shape
    parts = 2
    width = cols // parts
    ham_spec = pl.BlockSpec((rows, width), lambda j: (0, j))
    mask_spec = pl.BlockSpec((mask_rows, mask_cols // parts), lambda j: (0, j))
    return pl.pallas_call(
        mask_kernel,
        grid=(parts,),
        in_specs=[ham_spec, ham_spec, mask_spec, mask_spec],
        out_specs=pl.BlockSpec((2 * rows, width), lambda j: (0, j)),
        out_shape=jax.ShapeDtypeStruct((2 * rows, cols), jnp.bfloat16),
        compiler_params=pltpu.CompilerParams(vmem_limit_bytes=48 * 1024 * 1024),
        cost_estimate=pl.CostEstimate(
            flops=2 * rows * cols, bytes_accessed=8 * rows * cols, transcendentals=0
        ),
    )(own, pair, mask_own, mask_pair)


def swap(value, axis):
    return lax.ppermute(value, axis, [(0, 1), (1, 0)])


def shift(value, step):
    count = lax.axis_size("z")
    return lax.ppermute(value, "z", [(i, (i + step) % count) for i in range(count)])


def exchange(value, axes):
    return lax.all_to_all(value, axes, split_axis=0, concat_axis=0, tiled=True)


def scalar_tile(first, second):
    lane = lax.broadcasted_iota(jnp.int32, (8, LANES), 1)
    row = lax.broadcasted_iota(jnp.int32, (8, LANES), 0)
    return jnp.where(
        row == 0, jnp.where(lane == 0, first, jnp.where(lane == 1, second, 0.0)), 0.0
    )


def gather_blocks(block):
    near = {0: block}
    far = {}
    near[-1], near[1], far[0] = shift(near[0], 1), shift(near[0], -1), swap(near[0], "xlo")
    near[-2], near[2], far[-1] = shift(near[-1], 1), shift(near[1], -1), swap(near[-1], "xlo")
    near[-3], near[3], far[1] = shift(near[-2], 1), shift(near[2], -1), swap(near[1], "xlo")
    near[-4], far[2], far[-2] = shift(near[-3], 1), shift(far[1], -1), swap(near[-2], "xlo")
    far[-3], far[3], far[-4] = shift(far[-2], 1), shift(far[2], -1), swap(near[-4], "xlo")
    order = [(0, 0), (0, -1), (0, 1), (1, 0), (0, -2), (0, 2), (1, -1), (0, -3), (0, 3), (1, 1)]
    order += [(0, -4), (1, 2), (1, -2), (1, -3), (1, 3), (1, -4)]
    return [(side, offset, (far if side else near)[offset]) for side, offset in order]


def body(ham, coeff, tile_mask, occupation, orbital_energy, coulomb):
    rows, strings = ham.shape
    cols = coeff.shape[1]
    half = cols // 2
    core = lax.axis_index("core")
    xlo = lax.axis_index("xlo")
    z = lax.axis_index("z")
    row_index = (xlo * 8 + z) * 2 + core
    col_index = lax.axis_index("xhi") * 4 + lax.axis_index("y")

    first = core == 0
    left, right = coeff[:, :half], coeff[:, half:]
    mine = jnp.where(first, left, right)
    theirs = swap(jnp.where(first, right, left), "core")
    block = jnp.where(
        first,
        jnp.concatenate([mine, theirs], axis=0),
        jnp.concatenate([theirs, mine], axis=0),
    )
    panels = mask_panels(ham, swap(ham, "core"), tile_mask, swap(tile_mask, "core"))
    depth = block.shape[0]

    product = None
    for side, offset, piece in gather_blocks(block):
        owner = (xlo + side) % 2 * 8 + (z + offset) % 8
        columns = lax.dynamic_slice_in_dim(panels, owner * depth, depth, 1)
        term = jnp.dot(columns, piece, preferred_element_type=jnp.float32)
        product = term if product is None else product + term
    kept, sent = product[:rows], product[rows:]
    got = swap(sent, "core")
    product = jnp.where(
        first,
        jnp.concatenate([kept, got], axis=1),
        jnp.concatenate([got, kept], axis=1),
    )

    coeff_float = coeff.astype(jnp.float32)
    sums = scalar_tile(2.0 * jnp.sum(coeff_float * product), jnp.sum(coeff_float * coeff_float))

    sub = rows // 8
    pieces = product.reshape(8, sub, 8, LANES).transpose(0, 2, 1, 3).reshape(8, rows, LANES)
    pieces = jnp.concatenate([pieces, jnp.broadcast_to(sums, (8, 8, LANES))], axis=1)
    pieces = exchange(pieces, COL)
    sums = jnp.sum(pieces[:, rows:], axis=0)
    pieces = pieces[:, :rows].reshape(32, 2 * sub, LANES)
    pieces = jnp.concatenate([pieces, jnp.broadcast_to(sums, (32, 8, LANES))], axis=1)
    pieces = exchange(pieces, ROW)
    sums = jnp.sum(pieces[:, 2 * sub :], axis=0)
    pieces = exchange(pieces[:, : 2 * sub].reshape(8, 4 * 2 * sub, LANES), COL)
    turned = pieces.reshape(8, 4, 2, sub, LANES).transpose(2, 4, 1, 0, 3).reshape(rows, cols)

    occ_float = occupation.astype(jnp.float32)
    occ_alpha = lax.dynamic_slice_in_dim(occ_float, row_index * rows, rows, 1)
    occ_beta = lax.dynamic_slice_in_dim(occ_float, col_index * cols, cols, 1)
    energy_alpha = jnp.dot(orbital_energy, occ_alpha, precision=lax.Precision.HIGHEST)
    energy_beta = jnp.dot(orbital_energy, occ_beta, precision=lax.Precision.HIGHEST)
    coupling = jnp.dot(
        jnp.dot(occ_alpha.T, coulomb, precision=lax.Precision.HIGHEST),
        occ_beta,
        precision=lax.Precision.HIGHEST,
    )
    diagonal = energy_alpha[:, None] + energy_beta[None, :] + coupling

    theta = sums[0, 0] / sums[0, 1]
    residual = product + turned - theta * coeff_float
    update = residual / jnp.maximum(jnp.abs(diagonal - theta), 1.0)
    totals = scalar_tile(jnp.sum(residual * residual), jnp.sum(update * update))[0]
    totals = jnp.sum(exchange(jnp.broadcast_to(totals, (256, LANES)), AXES), axis=0)
    correction = update * lax.rsqrt(totals[1] / (NS * NS) + 1e-06)
    stats = jnp.stack([theta, jnp.sqrt(totals[0] / (NS * NS))])
    return (correction, stats)


def solution(mesh):
    fine = Mesh(mesh.devices.reshape(SIZES), AXES)
    in_specs = (P(ROW, None), P(ROW, COL), P(ROW, None), P(), P(), P())
    out_specs = (P(ROW, COL), P())
    return jax.shard_map(body, mesh=fine, in_specs=in_specs, out_specs=out_specs, check_vma=False)
```

time: 382 us -> 226 us (0.59)
  blocking collectives: 202 us -> 84.5 us
  waiting for transfers between devices: 104 us -> 66 us
  starting transfers between devices: 9.11 us -> 32 us
  local copies, waits for them, and re-layouts: 31.4 us -> 9.77 us
  between operations: 16.9 us -> 4.34 us
  Pallas kernels: 0 us -> 6.13 us
    psum x2 -> x0, blocking collectives: 148 us -> none  [the longest x1 74.3 us: body(): lax.psum((jnp.sum(coeff_float * sigma), jnp.sum(coeff_float * coeff_float...]
    all_gather x1 -> x0, waiting for transfers between devices: 77 us -> none  [body(): lax.all_gather(coeff, 'row', axis=0, tiled=True)]
    ppermute x0 -> x19, waiting for transfers between devices: none -> 56 us  [the longest x10 34.1 us: shift(): lax.ppermute(value, 'z', [(i, (i + step) % count) for i in range(count)])]
    all_to_all x2 -> x3, blocking collectives: 53.8 us -> 84.5 us  [exchange(): return lax.all_to_all(value, axes, split_axis=0, concat_axis=0, tiled=True)]
    mul x2 -> x0, local copies, waits for them, and re-layouts: 28.3 us -> none  [body(): ham.reshape(mask_rows, block_size, mask_cols, block_size) * weights]
    ppermute x0 -> x19, starting transfers between devices: none -> 27.7 us  [the longest x10 16.2 us: shift(): lax.ppermute(value, 'z', [(i, (i + step) % count) for i in range(count)])]
    all_to_all x1, waiting for transfers between devices: 25.9 us -> 10 us  [exchange(): return lax.all_to_all(value, axes, split_axis=0, concat_axis=0, tiled=True)]
    pallas_call x0 -> x1, Pallas kernels: none -> 6.13 us  [mask_panels(): pl.pallas_call(mask_kernel, grid=(parts,), in_specs=[ham_spec, ham_spec,...]
  transfers between devices with their start and end apart: 2 -> 20, of which waited for: 2 -> 9; matrix products, arithmetic and copies ran while one was open for 8% -> 7% of each run, Pallas kernels for 0% -> 3%
where the time goes in v1:
time: 226 us; the launch traced here: 225 us
  blocking collectives  84.5 us (37%)
  waiting for transfers between devices  66 us (29%)
  starting transfers between devices  32 us (14%)
  matrix products  15.1 us (7%)
  local copies, waits for them, and re-layouts  9.77 us (4%)
  other arithmetic  7.28 us (3%)
  Pallas kernels  6.13 us (3%)
  between operations  4.34 us (2%)
    all_to_all x3, blocking collectives, exchange(): return lax.all_to_all(value, axes, split_axis=0, concat_axis=0, tiled=True)  84.5 us
    ppermute x10, waiting for transfers between devices, shift(): lax.ppermute(value, 'z', [(i, (i + step) % count) for i in range(count)])  34.1 us
    ppermute x9, waiting for transfers between devices, swap(): return lax.ppermute(value, axis, [(0, 1), (1, 0)])  21.9 us
    ppermute x10, starting transfers between devices, shift(): lax.ppermute(value, 'z', [(i, (i + step) % count) for i in range(count)])  16.2 us
    dot_general x16, matrix products, body(): term = jnp.dot(columns, piece, preferred_element_type=jnp.float32)  12.6 us
    ppermute x9, starting transfers between devices, swap(): return lax.ppermute(value, axis, [(0, 1), (1, 0)])  11.6 us
    all_to_all x1, waiting for transfers between devices, exchange(): return lax.all_to_all(value, axes, split_axis=0, concat_axis=0, tiled=True)  10 us
    pallas_call x1, Pallas kernels, mask_panels(): pl.pallas_call(mask_kernel, grid=(parts,), in_specs=[ham_spec, ham_spec,...  6.13 us
  transfers between devices with their start and end apart: 20, of which 9 were waited for; matrix products, arithmetic and copies ran while one was open for 7% of the time, Pallas kernels for 3%

profile of v1, /device:TPU:1, one launch (start us, length us, event | category | flops | bytes accessed | tf_op | source)
XLA Modules:
  0.0 225.1 jit_solution(15069099456721835653)
XLA Ops:
  0.6 3.3 %collective-permute-start = (bf16[256,8192]{1,0:T(8,128)(2,1)}, bf16[256,8192]{1,0:T(8,128)(2,1)}, u32[]{:S(2)}, u32[]{:S(2)}) collective-permute-start(bf16[256,8192]{1,0:T(8,128)(2,1)} %own_ref.1), channel_id=1, source_target_pairs={{0,8},{8,0},{1,9},{9,1},{2,10},{10,2},{3,11},{11,3},{4,12},{12,4},... | collective-permute-start | bytes 12582920 | tf_op jit(solution)/shard_map/ppermute | solution.py:57
  5.2 6.0 %collective-permute-done.2 = bf16[256,512]{1,0:T(8,128)(2,1)S(1)} collective-permute-done((bf16[256,512]{1,0:T(8,128)(2,1)S(1)}, bf16[256,512]{1,0:T(8,128)(2,1)S(1)}, u32[]{:S(2)}, u32[]{:S(2)}) %collective-permute-start.2) | collective-permute-done | bytes 262176 | tf_op jit(solution)/shard_map/ppermute | solution.py:57
  11.4 3.9 %collective-permute-start.4 = (bf16[512,512]{1,0:T(8,128)(2,1)S(1)}, bf16[512,512]{1,0:T(8,128)(2,1)S(1)}, u32[]{:S(2)}, u32[]{:S(2)}) collective-permute-start(bf16[512,512]{1,0:T(8,128)(2,1)S(1)} %maximum_select_fusion.1), channel_id=1, source_target_pairs={{0,112},{16,0},{32,16},{48,32},{64,48},{80,64},{96,80},{112,96},{1... | collective-permute-start | bytes 1572872 | tf_op jit(solution)/shard_map/ppermute | solution.py:62
  15.4 11.9 %collective-permute-done.3 = bf16[512,512]{1,0:T(8,128)(2,1)S(1)} collective-permute-done((bf16[512,512]{1,0:T(8,128)(2,1)S(1)}, bf16[512,512]{1,0:T(8,128)(2,1)S(1)}, u32[]{:S(2)}, u32[]{:S(2)}) %collective-permute-start.3) | collective-permute-done | bytes 524320 | tf_op jit(solution)/shard_map/ppermute | solution.py:62
  28.1 1.2 collective-permute-start.5
  30.4 3.0 %collective-permute-start.7 = (bf16[512,512]{1,0:T(8,128)(2,1)S(1)}, bf16[512,512]{1,0:T(8,128)(2,1)S(1)}, u32[]{:S(2)}, u32[]{:S(2)}) collective-permute-start(bf16[512,512]{1,0:T(8,128)(2,1)S(1)} %collective-permute-done.4), channel_id=1, source_target_pairs={{0,112},{16,0},{32,16},{48,32},{64,48},{80,64},{96,80},{112,96},{1... | collective-permute-start | bytes 1572872 | tf_op jit(solution)/shard_map/ppermute | solution.py:62
  33.4 7.7 %collective-permute-done.6 = bf16[512,512]{1,0:T(8,128)(2,1)S(1)} collective-permute-done((bf16[512,512]{1,0:T(8,128)(2,1)S(1)}, bf16[512,512]{1,0:T(8,128)(2,1)S(1)}, u32[]{:S(2)}, u32[]{:S(2)}) %collective-permute-start.6) | collective-permute-done | bytes 524320 | tf_op jit(solution)/shard_map/ppermute | solution.py:62
  41.0 1.2 collective-permute-start.11
  42.3 2.2 copy-done.1
  45.1 6.1 %shard_map.77 = bf16[512,8192]{1,0:T(8,128)(2,1)} custom-call(bf16[256,8192]{1,0:T(8,128)(2,1)S(1)} %copy-done.1, bf16[256,8192]{1,0:T(8,128)(2,1)} %collective-permute-done.pair_ref, s32[8,256]{1,0:T(8,128)S(1)} %copy-done.2, s32[8,256]{1,0:T(8,128)S(1)} %collective-permute-done.1.mask_pair_ref), custom_call_target="tpu_custom_call" | custom-call | flops 4194304 | bytes 16777216 | tf_op jit(solution)/shard_map/pallas_call | solution.py:43
  51.3 1.7 fusion.37
  52.9 1.9 fusion.39
  54.9 9.3 %collective-permute-done.11 = bf16[512,512]{1,0:T(8,128)(2,1)S(1)} collective-permute-done((bf16[512,512]{1,0:T(8,128)(2,1)S(1)}, bf16[512,512]{1,0:T(8,128)(2,1)S(1)}, u32[]{:S(2)}, u32[]{:S(2)}) %collective-permute-start.11) | collective-permute-done | bytes 524320 | tf_op jit(solution)/shard_map/ppermute | solution.py:57
  64.2 1.2 collective-permute-start.14
  65.4 1.5 fusion.25
  66.9 3.0 %collective-permute-start.13 = (bf16[512,512]{1,0:T(8,128)(2,1)S(1)}, bf16[512,512]{1,0:T(8,128)(2,1)S(1)}, u32[]{:S(2)}, u32[]{:S(2)}) collective-permute-start(bf16[512,512]{1,0:T(8,128)(2,1)S(1)} %collective-permute-done.11), channel_id=1, source_target_pairs={{0,112},{16,0},{32,16},{48,32},{64,48},{80,64},{96,80},{112,96},{1... | collective-permute-start | bytes 1572872 | tf_op jit(solution)/shard_map/ppermute | solution.py:62
  70.0 1.5 fusion.32
  71.5 5.4 %collective-permute-done.14 = bf16[512,512]{1,0:T(8,128)(2,1)S(1)} collective-permute-done((bf16[512,512]{1,0:T(8,128)(2,1)S(1)}, bf16[512,512]{1,0:T(8,128)(2,1)S(1)}, u32[]{:S(2)}, u32[]{:S(2)}) %collective-permute-start.14) | collective-permute-done | bytes 524320 | tf_op jit(solution)/shard_map/ppermute | solution.py:57
  76.8 3.0 %collective-permute-start.10 = (bf16[512,512]{1,0:T(8,128)(2,1)S(1)}, bf16[512,512]{1,0:T(8,128)(2,1)S(1)}, u32[]{:S(2)}, u32[]{:S(2)}) collective-permute-start(bf16[512,512]{1,0:T(8,128)(2,1)S(1)} %collective-permute-done.7), channel_id=1, source_target_pairs={{0,112},{16,0},{32,16},{48,32},{64,48},{80,64},{96,80},{112,96},{1... | collective-permute-start | bytes 1572872 | tf_op jit(solution)/shard_map/ppermute | solution.py:62
  80.4 3.1 %collective-permute-start.16 = (bf16[512,512]{1,0:T(8,128)(2,1)S(1)}, bf16[512,512]{1,0:T(8,128)(2,1)S(1)}, u32[]{:S(2)}, u32[]{:S(2)}) collective-permute-start(bf16[512,512]{1,0:T(8,128)(2,1)S(1)} %collective-permute-done.13), channel_id=1, source_target_pairs={{0,112},{16,0},{32,16},{48,32},{64,48},{80,64},{96,80},{112,96},{1... | collective-permute-start | bytes 1572872 | tf_op jit(solution)/shard_map/ppermute | solution.py:62
  85.8 5.8 %collective-permute-done.10 = bf16[512,512]{1,0:T(8,128)(2,1)S(1)} collective-permute-done((bf16[512,512]{1,0:T(8,128)(2,1)S(1)}, bf16[512,512]{1,0:T(8,128)(2,1)S(1)}, u32[]{:S(2)}, u32[]{:S(2)}) %collective-permute-start.10) | collective-permute-done | bytes 524320 | tf_op jit(solution)/shard_map/ppermute | solution.py:62
  94.2 8.7 %collective-permute-done.16 = bf16[512,512]{1,0:T(8,128)(2,1)S(1)} collective-permute-done((bf16[512,512]{1,0:T(8,128)(2,1)S(1)}, bf16[512,512]{1,0:T(8,128)(2,1)S(1)}, u32[]{:S(2)}, u32[]{:S(2)}) %collective-permute-start.16) | collective-permute-done | bytes 524320 | tf_op jit(solution)/shard_map/ppermute | solution.py:62
  104.4 1.8 collective-permute-start.18
  106.5 1.3 collective-permute-done.18
  111.0 23.3 %all_to_all.21 = f32[8,264,128]{2,1,0:T(8,128)S(1)} all-to-all(f32[8,264,128]{2,1,0:T(8,128)S(1)} %pad_maximum_fusion.1), channel_id=1, replica_groups=mesh['xlo'=2,'z'=8,'core'=2,'xhi'=2,'y'=4] {'xhi','y'}, dimensions={0} | all-to-all | bytes 2162688 | tf_op jit(solution)/shard_map/all_to_all | solution.py:66
  134.5 39.7 %all_to_all.22 = f32[32,72,128]{2,1,0:T(8,128)S(1)} all-to-all(f32[32,72,128]{2,1,0:T(8,128)S(1)} %pad_maximum_fusion), channel_id=1, replica_groups=mesh['xlo'=2,'z'=8,'core'=2,'xhi'=2,'y'=4] {'xlo','z','core'}, dimensions={0} | all-to-all | bytes 2359296 | tf_op jit(solution)/shard_map/all_to_all | solution.py:66
  175.3 4.2 %all-to-all-start.2 = ((f32[8,256,128]{2,1,0:T(8,128)}), f32[8,256,128]{2,1,0:T(8,128)}, u32[]{:S(2)}, u32[]{:S(2)}) async-start(f32[8,256,128]{2,1,0:T(8,128)} %bitcast.59), calls=%async_computation.2 | async-start | bytes 2097152 | tf_op jit(solution)/shard_map/all_to_all | solution.py:66
  183.1 10.0 %all-to-all-done.2 = f32[8,256,128]{2,1,0:T(8,128)} async-done(((f32[8,256,128]{2,1,0:T(8,128)}), f32[8,256,128]{2,1,0:T(8,128)}, u32[]{:S(2)}, u32[]{:S(2)}) %all-to-all-start.2) | async-done | bytes 1048608 | tf_op jit(solution)/shard_map/all_to_all | solution.py:66
  193.1 2.1 copy.26
  196.1 2.1 multiply_reduce_fusion
  199.6 21.5 %all_to_all.23 = f32[256,1,128]{2,1,0:T(1,128)S(1)} all-to-all(f32[256,1,128]{2,1,0:T(1,128)S(1)} %broadcast_in_dim.43), channel_id=1, replica_groups=mesh['xlo'=2,'z'=8,'core'=2,'xhi'=2,'y'=4] {'xlo','z','core','xhi','y'}, dimensions={0} | all-to-all | bytes 262144 | tf_op jit(solution)/shard_map/all_to_all | solution.py:66
  223.2 1.3 copy.29
  (78 shorter events, 20.9 us)
Async XLA Ops:
  0.6 180.4 %copy-start = (f32[16,16]{1,0:T(8,128)S(1)}, f32[16,16]{1,0:T(8,128)}, u32[]{:S(2)}) copy-start(f32[16,16]{1,0:T(8,128)} %param.11) | copy-start | bytes 3076
  0.6 41.6 %collective-permute-start = (bf16[256,8192]{1,0:T(8,128)(2,1)}, bf16[256,8192]{1,0:T(8,128)(2,1)}, u32[]{:S(2)}, u32[]{:S(2)}) collective-permute-start(bf16[256,8192]{1,0:T(8,128)(2,1)} %own_ref.1), channel_id=1, source_target_pairs={{0,8},{8,0},{1,9},{9,1},{2,10},{10,2},{3,11},{11,3},{4,12},{12,4},... | collective-permute-start | bytes 12582920 | tf_op jit(solution)/shard_map/ppermute | solution.py:57
  5.0 6.1 %collective-permute-start.2 = (bf16[256,512]{1,0:T(8,128)(2,1)S(1)}, bf16[256,512]{1,0:T(8,128)(2,1)S(1)}, u32[]{:S(2)}, u32[]{:S(2)}) collective-permute-start(bf16[256,512]{1,0:T(8,128)(2,1)S(1)} %get-tuple-element.16), channel_id=1, source_target_pairs={{0,8},{8,0},{1,9},{9,1},{2,10},{10,2},{3,11},{11,3},{4,12},{12,4},... | collective-permute-start | bytes 786440 | tf_op jit(solution)/shard_map/ppermute | solution.py:57
  11.3 15.9 %collective-permute-start.3 = (bf16[512,512]{1,0:T(8,128)(2,1)S(1)}, bf16[512,512]{1,0:T(8,128)(2,1)S(1)}, u32[]{:S(2)}, u32[]{:S(2)}) collective-permute-start(bf16[512,512]{1,0:T(8,128)(2,1)S(1)} %maximum_select_fusion.1), channel_id=1, source_target_pairs={{0,16},{16,32},{32,48},{48,64},{64,80},{80,96},{96,112},{112,0},{1... | collective-permute-start | bytes 1572872 | tf_op jit(solution)/shard_map/ppermute | solution.py:62
  11.4 19.0 %collective-permute-start.4 = (bf16[512,512]{1,0:T(8,128)(2,1)S(1)}, bf16[512,512]{1,0:T(8,128)(2,1)S(1)}, u32[]{:S(2)}, u32[]{:S(2)}) collective-permute-start(bf16[512,512]{1,0:T(8,128)(2,1)S(1)} %maximum_select_fusion.1), channel_id=1, source_target_pairs={{0,112},{16,0},{32,16},{48,32},{64,48},{80,64},{96,80},{112,96},{1... | collective-permute-start | bytes 1572872 | tf_op jit(solution)/shard_map/ppermute | solution.py:62
  27.3 13.8 %collective-permute-start.6 = (bf16[512,512]{1,0:T(8,128)(2,1)S(1)}, bf16[512,512]{1,0:T(8,128)(2,1)S(1)}, u32[]{:S(2)}, u32[]{:S(2)}) collective-permute-start(bf16[512,512]{1,0:T(8,128)(2,1)S(1)} %collective-permute-done.3), channel_id=1, source_target_pairs={{0,16},{16,32},{32,48},{48,64},{64,80},{80,96},{96,112},{112,0},{1... | collective-permute-start | bytes 1572872 | tf_op jit(solution)/shard_map/ppermute | solution.py:62
  27.3 2.1 collective-permute-start.1
  28.1 52.1 %collective-permute-start.5 = (bf16[512,512]{1,0:T(8,128)(2,1)S(1)}, bf16[512,512]{1,0:T(8,128)(2,1)S(1)}, u32[]{:S(2)}, u32[]{:S(2)}) collective-permute-start(bf16[512,512]{1,0:T(8,128)(2,1)S(1)} %maximum_select_fusion.1), channel_id=1, source_target_pairs={{0,128},{128,0},{1,129},{129,1},{2,130},{130,2},{3,131},{131,3},{4... | collective-permute-start | bytes 1572872 | tf_op jit(solution)/shard_map/ppermute | solution.py:57
  29.4 55.4 %collective-permute-start.8 = (bf16[512,512]{1,0:T(8,128)(2,1)S(1)}, bf16[512,512]{1,0:T(8,128)(2,1)S(1)}, u32[]{:S(2)}, u32[]{:S(2)}) collective-permute-start(bf16[512,512]{1,0:T(8,128)(2,1)S(1)} %collective-permute-done.3), channel_id=1, source_target_pairs={{0,128},{128,0},{1,129},{129,1},{2,130},{130,2},{3,131},{131,3},{4... | collective-permute-start | bytes 1572872 | tf_op jit(solution)/shard_map/ppermute | solution.py:57
  30.4 36.5 %collective-permute-start.7 = (bf16[512,512]{1,0:T(8,128)(2,1)S(1)}, bf16[512,512]{1,0:T(8,128)(2,1)S(1)}, u32[]{:S(2)}, u32[]{:S(2)}) collective-permute-start(bf16[512,512]{1,0:T(8,128)(2,1)S(1)} %collective-permute-done.4), channel_id=1, source_target_pairs={{0,112},{16,0},{32,16},{48,32},{64,48},{80,64},{96,80},{112,96},{1... | collective-permute-start | bytes 1572872 | tf_op jit(solution)/shard_map/ppermute | solution.py:62
  41.0 23.1 %collective-permute-start.11 = (bf16[512,512]{1,0:T(8,128)(2,1)S(1)}, bf16[512,512]{1,0:T(8,128)(2,1)S(1)}, u32[]{:S(2)}, u32[]{:S(2)}) collective-permute-start(bf16[512,512]{1,0:T(8,128)(2,1)S(1)} %collective-permute-done.4), channel_id=1, source_target_pairs={{0,128},{128,0},{1,129},{129,1},{2,130},{130,2},{3,131},{131,3},{4... | collective-permute-start | bytes 1572872 | tf_op jit(solution)/shard_map/ppermute | solution.py:57
  42.2 27.7 %collective-permute-start.9 = (bf16[512,512]{1,0:T(8,128)(2,1)S(1)}, bf16[512,512]{1,0:T(8,128)(2,1)S(1)}, u32[]{:S(2)}, u32[]{:S(2)}) collective-permute-start(bf16[512,512]{1,0:T(8,128)(2,1)S(1)} %collective-permute-done.6), channel_id=1, source_target_pairs={{0,16},{16,32},{32,48},{48,64},{64,80},{80,96},{96,112},{112,0},{1... | collective-permute-start | bytes 1572872 | tf_op jit(solution)/shard_map/ppermute | solution.py:62
  42.2 2.2 copy-start.1
  44.4 0.7 copy-start.2
  51.3 28.5 %copy-start.3 = (bf16[512,8192]{1,0:T(8,128)(2,1)S(1)}, bf16[512,8192]{1,0:T(8,128)(2,1)}, u32[]{:S(2)}) copy-start(bf16[512,8192]{1,0:T(8,128)(2,1)} %shard_map.77) | copy-start | bytes 25165828
  64.2 12.7 %collective-permute-start.14 = (bf16[512,512]{1,0:T(8,128)(2,1)S(1)}, bf16[512,512]{1,0:T(8,128)(2,1)S(1)}, u32[]{:S(2)}, u32[]{:S(2)}) collective-permute-start(bf16[512,512]{1,0:T(8,128)(2,1)S(1)} %collective-permute-done.6), channel_id=1, source_target_pairs={{0,128},{128,0},{1,129},{129,1},{2,130},{130,2},{3,131},{131,3},{4... | collective-permute-start | bytes 1572872 | tf_op jit(solution)/shard_map/ppermute | solution.py:57
  66.9 13.5 %collective-permute-start.13 = (bf16[512,512]{1,0:T(8,128)(2,1)S(1)}, bf16[512,512]{1,0:T(8,128)(2,1)S(1)}, u32[]{:S(2)}, u32[]{:S(2)}) collective-permute-start(bf16[512,512]{1,0:T(8,128)(2,1)S(1)} %collective-permute-done.11), channel_id=1, source_target_pairs={{0,112},{16,0},{32,16},{48,32},{64,48},{80,64},{96,80},{112,96},{1... | collective-permute-start | bytes 1572872 | tf_op jit(solution)/shard_map/ppermute | solution.py:62
  70.0 13.6 %collective-permute-start.12 = (bf16[512,512]{1,0:T(8,128)(2,1)S(1)}, bf16[512,512]{1,0:T(8,128)(2,1)S(1)}, u32[]{:S(2)}, u32[]{:S(2)}) collective-permute-start(bf16[512,512]{1,0:T(8,128)(2,1)S(1)} %collective-permute-done.9), channel_id=1, source_target_pairs={{0,16},{16,32},{32,48},{48,64},{64,80},{80,96},{96,112},{112,0},{1... | collective-permute-start | bytes 1572872 | tf_op jit(solution)/shard_map/ppermute | solution.py:62
  76.8 14.8 %collective-permute-start.10 = (bf16[512,512]{1,0:T(8,128)(2,1)S(1)}, bf16[512,512]{1,0:T(8,128)(2,1)S(1)}, u32[]{:S(2)}, u32[]{:S(2)}) collective-permute-start(bf16[512,512]{1,0:T(8,128)(2,1)S(1)} %collective-permute-done.7), channel_id=1, source_target_pairs={{0,112},{16,0},{32,16},{48,32},{64,48},{80,64},{96,80},{112,96},{1... | collective-permute-start | bytes 1572872 | tf_op jit(solution)/shard_map/ppermute | solution.py:62
  80.3 23.0 %collective-permute-start.15 = (bf16[512,512]{1,0:T(8,128)(2,1)S(1)}, bf16[512,512]{1,0:T(8,128)(2,1)S(1)}, u32[]{:S(2)}, u32[]{:S(2)}) collective-permute-start(bf16[512,512]{1,0:T(8,128)(2,1)S(1)} %collective-permute-done.14), channel_id=1, source_target_pairs={{0,16},{16,32},{32,48},{48,64},{64,80},{80,96},{96,112},{112,0},{1... | collective-permute-start | bytes 1572872 | tf_op jit(solution)/shard_map/ppermute | solution.py:62
  80.4 22.4 %collective-permute-start.16 = (bf16[512,512]{1,0:T(8,128)(2,1)S(1)}, bf16[512,512]{1,0:T(8,128)(2,1)S(1)}, u32[]{:S(2)}, u32[]{:S(2)}) collective-permute-start(bf16[512,512]{1,0:T(8,128)(2,1)S(1)} %collective-permute-done.13), channel_id=1, source_target_pairs={{0,112},{16,0},{32,16},{48,32},{64,48},{80,64},{96,80},{112,96},{1... | collective-permute-start | bytes 1572872 | tf_op jit(solution)/shard_map/ppermute | solution.py:62
  83.5 20.3 %collective-permute-start.17 = (bf16[512,512]{1,0:T(8,128)(2,1)S(1)}, bf16[512,512]{1,0:T(8,128)(2,1)S(1)}, u32[]{:S(2)}, u32[]{:S(2)}) collective-permute-start(bf16[512,512]{1,0:T(8,128)(2,1)S(1)} %collective-permute-done.12), channel_id=1, source_target_pairs={{0,128},{128,0},{1,129},{129,1},{2,130},{130,2},{3,131},{131,3},{4... | collective-permute-start | bytes 1572872 | tf_op jit(solution)/shard_map/ppermute | solution.py:57
  93.7 12.6 %copy-start.4 = (bf16[256,1024]{1,0:T(8,128)(2,1)S(1)}, bf16[256,1024]{1,0:T(8,128)(2,1)}, u32[]{:S(2)}) copy-start(bf16[256,1024]{1,0:T(8,128)(2,1)} %param.7) | copy-start | bytes 1572868
  104.4 3.4 %collective-permute-start.18 = (f32[256,512]{0,1:T(8,128)S(1)}, f32[256,512]{0,1:T(8,128)S(1)}, u32[]{:S(2)}, u32[]{:S(2)}) collective-permute-start(f32[256,512]{0,1:T(8,128)S(1)} %get-tuple-element.13), channel_id=1, source_target_pairs={{0,8},{8,0},{1,9},{9,1},{2,10},{10,2},{3,11},{11,3},{4,12},{12,4},... | collective-permute-start | bytes 1572872 | tf_op jit(solution)/shard_map/ppermute | solution.py:57
  109.6 71.1 %copy-start.5 = (f32[16]{0:T(128)S(1)}, f32[16]{0:T(128)}, u32[]{:S(2)}) copy-start(f32[16]{0:T(128)} %param.10) | copy-start | bytes 196
  175.3 17.8 %all-to-all-start.2 = ((f32[8,256,128]{2,1,0:T(8,128)}), f32[8,256,128]{2,1,0:T(8,128)}, u32[]{:S(2)}, u32[]{:S(2)}) async-start(f32[8,256,128]{2,1,0:T(8,128)} %bitcast.59), calls=%async_computation.2 | async-start | bytes 2097152 | tf_op jit(solution)/shard_map/all_to_all | solution.py:66

commit v2 on v0

v2 whole, which is shorter than its diff:
```python
import jax
import jax.numpy as jnp
from jax import lax
from jax.experimental import pallas as pl
from jax.experimental.pallas import tpu as pltpu
from jax.sharding import Mesh, PartitionSpec as P

NS = 8192
AXES = ("xlo", "z", "core", "xhi", "y")
SIZES = (2, 8, 2, 2, 4)
ROW = ("xlo", "z", "core")
COL = ("xhi", "y")
PLANE = ("xlo", "core", "xhi", "y")
LANES = 128
CHUNK = 1024
MIB = 1024 * 1024


def mask_kernel(ham_ref, mask_ref, out_ref):
    rows, cols = ham_ref.shape
    mask_rows, mask_cols = mask_ref.shape
    size = cols // mask_cols
    tile = rows // mask_rows
    spread = (
        lax.broadcasted_iota(jnp.int32, (mask_cols, cols), 1) // size
        == lax.broadcasted_iota(jnp.int32, (mask_cols, cols), 0)
    ).astype(jnp.bfloat16)
    mask = mask_ref[...].astype(jnp.float32).astype(jnp.bfloat16)
    wide = jnp.dot(mask, spread, preferred_element_type=jnp.float32)
    for index in range(mask_rows):
        at = index * tile
        values = ham_ref[at : at + tile, :].astype(jnp.float32) * wide[index : index + 1, :]
        out_ref[at : at + tile, :] = values.astype(jnp.bfloat16)


def mask_half(ham, tile_mask, half):
    rows, cols = ham.shape
    mask_rows, mask_cols = tile_mask.shape
    return pl.pallas_call(
        mask_kernel,
        grid=(1,),
        in_specs=[
            pl.BlockSpec((rows, cols // 2), lambda j: (0, half)),
            pl.BlockSpec((mask_rows, mask_cols // 2), lambda j: (0, half)),
        ],
        out_specs=pl.BlockSpec((rows, cols // 2), lambda j: (0, 0)),
        out_shape=jax.ShapeDtypeStruct((rows, cols // 2), jnp.bfloat16),
        compiler_params=pltpu.CompilerParams(vmem_limit_bytes=32 * MIB),
        cost_estimate=pl.CostEstimate(
            flops=rows * cols, bytes_accessed=2 * rows * cols, transcendentals=0
        ),
    )(ham, tile_mask)


def product_kernel(
    place_ref, c0, p1, p2, p3, m1, m2, m3, top, low,
    own_a, own_b, pair_a, pair_b, far_a, far_b, cross_a, cross_b,
    turn_ref, home_ref, lhs, acc, local,
):
    step = pl.program_id(0)
    steps = pl.num_programs(0)
    xlo, z, core = place_ref[0], place_ref[1], place_ref[2]

    for offset, ref in ((0, c0), (-1, p1), (-2, p2), (-3, p3), (1, m1), (2, m2), (3, m3)):
        at = pl.multiple_of(lax.rem(z + offset + 8, 8) * 32, 32)
        lhs[pl.ds(at, 32), :] = ref[...]
    at = pl.multiple_of(lax.rem(z + 4, 8) * 32, 32)
    lhs[pl.ds(at, 16), :] = top[...]
    lhs[pl.ds(pl.multiple_of(at + 16, 16), 16), :] = low[...]

    @pl.when(step == 0)
    def _():
        acc[...] = jnp.zeros_like(acc)

    def add(panels):
        for index, ref in enumerate(panels):
            side = xlo if index < 2 else 1 - xlo
            other = core if index % 2 == 0 else 1 - core
            columns = pl.ds(pl.multiple_of((side * 2 + other) * 256, 256), 256)
            acc[:, columns] += lax.dot_general(
                lhs[...], ref[...], (((1,), (1,)), ((), ())), preferred_element_type=jnp.float32
            )

    @pl.when(step < steps // 2)
    def _():
        add((own_a, pair_a, far_a, cross_a))

    @pl.when(step >= steps // 2)
    def _():
        add((own_b, pair_b, far_b, cross_b))

    for side in range(2):

        @pl.when(step == side * (steps // 2) + z // 2)
        def _():
            source = pl.ds(pl.multiple_of(lax.rem(z, 2) * 512, 512), 512)
            local[:, side * 512 : side * 512 + 512] = lhs[:, source]

    @pl.when(step == steps - 1)
    def _():
        coeff = local[...].astype(jnp.float32)
        projection = jnp.sum(2.0 * coeff * acc[...])
        weight = jnp.sum(coeff * coeff)
        lane = lax.broadcasted_iota(jnp.int32, (8, LANES), 1)
        row = lax.broadcasted_iota(jnp.int32, (8, LANES), 0)
        sums = jnp.where(lane == 0, projection, jnp.where(lane == 1, weight, 0.0))
        sums = jnp.where(row == 0, sums, 0.0)
        for there in range(8):
            for part in range(8):
                turn_ref[there, part * 32 : part * 32 + 32, :] = acc[
                    there * 32 : there * 32 + 32, part * LANES : part * LANES + LANES
                ]
            turn_ref[there, 256:264, :] = sums
        for target in range(32):
            quarter, col = target // 8, target % 8
            for part in range(2):
                lanes = quarter * 256 + part * LANES
                for below in range(2):
                    at = (2 * (col % 4) + below) * 32 + col // 4 * 16
                    home_ref[target, part * 32 + below * 16 : part * 32 + below * 16 + 16, :] = acc[
                        at : at + 16, lanes : lanes + LANES
                    ]


def multiply(place, blocks, halves):
    strings = blocks[0].shape[1]
    steps = strings // CHUNK
    half_steps = steps // 2
    block_specs = [pl.BlockSpec((b.shape[0], CHUNK), lambda j, place: (0, j)) for b in blocks]
    low_spec = pl.BlockSpec((256, CHUNK), lambda j, place: (0, jnp.minimum(j, half_steps - 1)))
    high_spec = pl.BlockSpec((256, CHUNK), lambda j, place: (0, jnp.maximum(j - half_steps, 0)))
    return pl.pallas_call(
        product_kernel,
        grid_spec=pltpu.PrefetchScalarGridSpec(
            num_scalar_prefetch=1,
            grid=(steps,),
            in_specs=block_specs + [low_spec, high_spec] * 4,
            out_specs=[
                pl.BlockSpec((8, 264, LANES), lambda j, place: (0, 0, 0)),
                pl.BlockSpec((32, 64, LANES), lambda j, place: (0, 0, 0)),
            ],
            scratch_shapes=[
                pltpu.VMEM((256, CHUNK), jnp.bfloat16),
                pltpu.VMEM((256, 1024), jnp.float32),
                pltpu.VMEM((256, 1024), jnp.bfloat16),
            ],
        ),
        out_shape=[
            jax.ShapeDtypeStruct((8, 264, LANES), jnp.float32),
            jax.ShapeDtypeStruct((32, 64, LANES), jnp.float32),
        ],
        compiler_params=pltpu.CompilerParams(vmem_limit_bytes=40 * MIB),
        cost_estimate=pl.CostEstimate(
            flops=2 * 256 * 1024 * strings, bytes_accessed=24 * MIB, transcendentals=0
        ),
    )(place, *blocks, *halves)


def update_kernel(home_ref, turn_ref, coeff_ref, diag_ref, update_ref, sums_ref):
    totals = jnp.sum(turn_ref[:, 64:72, :], axis=0)
    lane = lax.broadcasted_iota(jnp.int32, (8, LANES), 1)
    row = lax.broadcasted_iota(jnp.int32, (8, LANES), 0)
    projection = jnp.sum(jnp.where(lane == 0, totals, 0.0))
    weight = jnp.sum(jnp.where(lane == 1, totals, 0.0))
    theta = jnp.full((1, 1), projection) / jnp.full((1, 1), weight)
    squares = jnp.zeros((8, LANES), jnp.float32)
    spread = jnp.zeros((8, LANES), jnp.float32)
    for part in range(2):
        rows = slice(part * LANES, part * LANES + LANES)
        for index in range(8):
            cols = slice(index * LANES, index * LANES + LANES)
            quarter, group = index // 2, index % 2
            at = part * 32 + quarter * 8
            straight = home_ref[group * 16 : group * 16 + 16, at : at + 8, :]
            straight = straight.reshape(LANES, LANES).T
            turned = turn_ref[part * 16 : part * 16 + 16, index * 8 : index * 8 + 8, :]
            turned = turned.reshape(LANES, LANES)
            coeff = coeff_ref[rows, cols].astype(jnp.float32)
            residual = straight + turned - theta * coeff
            update = residual / jnp.maximum(jnp.abs(diag_ref[rows, cols] - theta), 1.0)
            update_ref[rows, cols] = update
            squares += jnp.sum((residual * residual).reshape(16, 8, LANES), axis=0)
            spread += jnp.sum((update * update).reshape(16, 8, LANES), axis=0)
    values = jnp.where(lane == 0, jnp.sum(squares), jnp.where(lane == 1, jnp.sum(spread), 0.0))
    values = jnp.where(lane == 2, theta, values)
    sums_ref[...] = jnp.where(row == 0, values, 0.0)


def make_update(home, turn, coeff, diagonal):
    return pl.pallas_call(
        update_kernel,
        out_shape=[
            jax.ShapeDtypeStruct(coeff.shape, jnp.float32),
            jax.ShapeDtypeStruct((8, LANES), jnp.float32),
        ],
        compiler_params=pltpu.CompilerParams(vmem_limit_bytes=32 * MIB),
        cost_estimate=pl.CostEstimate(
            flops=10 * coeff.size, bytes_accessed=5 * MIB, transcendentals=0
        ),
    )(home, turn, coeff, diagonal)


def swap(value):
    return lax.ppermute(value, "core", [(0, 1), (1, 0)])


def shift(value, step):
    count = lax.axis_size("z")
    return lax.ppermute(value, "z", [(i, (i + step) % count) for i in range(count)])


def shift_x(value, step):
    def index(x):
        return x % 2 * 2 + x // 2

    pairs = [(index(x), index((x + step) % 4)) for x in range(4)]
    return lax.ppermute(value, ("xlo", "xhi"), pairs)


def exchange(value, axes):
    return lax.all_to_all(value, axes, split_axis=0, concat_axis=0, tiled=True)


def body(ham, coeff, tile_mask, occupation, orbital_energy, coulomb):
    rows, strings = ham.shape
    cols = coeff.shape[1]
    core = lax.axis_index("core")
    xlo = lax.axis_index("xlo")
    z = lax.axis_index("z")
    row_index = (xlo * 8 + z) * 2 + core
    col_index = lax.axis_index("xhi") * 4 + lax.axis_index("y")

    own_a = mask_half(ham, tile_mask, 0)
    own_b = mask_half(ham, tile_mask, 1)
    far_a, far_b = shift_x(own_a, 1), shift_x(own_b, -1)
    pair_a, pair_b = swap(own_a), swap(own_b)
    cross_a, cross_b = swap(far_a), swap(far_b)

    coeff_in, own_a, own_b = lax.optimization_barrier((coeff, own_a, own_b))
    block = exchange(coeff_in.reshape(32, 8, cols), PLANE)
    block = block.reshape(4, 8, 8, cols).transpose(0, 2, 1, 3).reshape(32, strings)
    p1, m1 = shift(block, 1), shift(block, -1)
    p2, m2 = shift(p1, 1), shift(m1, -1)
    p3, m3 = shift(p2, 1), shift(m2, -1)
    top, low = shift(p3[:16], 1), shift(m3[16:], -1)

    place = jnp.stack([xlo, z, core]).astype(jnp.int32)
    turn, home = multiply(
        place,
        (block, p1, p2, p3, m1, m2, m3, top, low),
        (own_a, own_b, pair_a, pair_b, far_a, far_b, cross_a, cross_b),
    )

    home = exchange(home, PLANE)
    turn = exchange(turn, "z")
    sums = jnp.sum(turn[:, 256:], axis=0)
    turn = turn[:, :256].reshape(4, 2, 2, 2, 2, 2, 2, 8, LANES)
    turn = turn.transpose(5, 6, 2, 0, 1, 3, 4, 7, 8).reshape(32, 64, LANES)
    turn = jnp.concatenate([turn, jnp.broadcast_to(sums, (32, 8, LANES))], axis=1)
    turn = exchange(turn, PLANE)

    occ_float = occupation.astype(jnp.float32)
    occ_alpha = lax.dynamic_slice_in_dim(occ_float, row_index * rows, rows, 1)
    occ_beta = lax.dynamic_slice_in_dim(occ_float, col_index * cols, cols, 1)
    energy_alpha = jnp.dot(orbital_energy, occ_alpha, precision=lax.Precision.HIGHEST)
    energy_beta = jnp.dot(orbital_energy, occ_beta, precision=lax.Precision.HIGHEST)
    coupling = jnp.dot(
        jnp.dot(occ_alpha.T, coulomb, precision=lax.Precision.HIGHEST),
        occ_beta,
        precision=lax.Precision.HIGHEST,
    )
    diagonal = energy_alpha[:, None] + energy_beta[None, :] + coupling

    update, sums = make_update(home, turn, coeff, diagonal)
    theta = sums[0, 2]
    totals = exchange(jnp.broadcast_to(sums[0], (256, LANES)), AXES)
    totals = jnp.sum(totals, axis=0)
    correction = update * lax.rsqrt(totals[1] / (NS * NS) + 1e-06)
    stats = jnp.stack([theta, jnp.sqrt(totals[0] / (NS * NS))])
    return (correction, stats)


def solution(mesh):
    fine = Mesh(mesh.devices.reshape(SIZES), AXES)
    in_specs = (P(ROW, None), P(ROW, COL), P(ROW, None), P(), P(), P())
    out_specs = (P(ROW, COL), P())
    return jax.shard_map(body, mesh=fine, in_specs=in_specs, out_specs=out_specs, check_vma=False)
```

time: 382 us -> 266 us (0.70)
  blocking collectives: 202 us -> 80.3 us
  starting transfers between devices: 9.11 us -> 41.3 us
  Pallas kernels: 0 us -> 15.7 us
  between operations: 16.9 us -> 2.23 us
  local copies, waits for them, and re-layouts: 31.4 us -> 20.2 us
  matrix products: 13.1 us -> 2.39 us
  waiting for transfers between devices: 104 us -> 98.6 us
    psum x2 -> x0, blocking collectives: 148 us -> none  [the longest x1 74.3 us: body(): lax.psum((jnp.sum(coeff_float * sigma), jnp.sum(coeff_float * coeff_float...]
    all_gather x1 -> x0, waiting for transfers between devices: 77 us -> none  [body(): lax.all_gather(coeff, 'row', axis=0, tiled=True)]
    ppermute x0 -> x14, waiting for transfers between devices: none -> 56.9 us  [the longest x8 56.9 us: shift(): lax.ppermute(value, 'z', [(i, (i + step) % count) for i in range(count)])]
    mul x2 -> x0, local copies, waits for them, and re-layouts: 28.3 us -> none  [body(): ham.reshape(mask_rows, block_size, mask_cols, block_size) * weights]
    all_to_all x2, blocking collectives: 53.8 us -> 80.3 us  [exchange(): return lax.all_to_all(value, axes, split_axis=0, concat_axis=0, tiled=True)]
    all_to_all x1 -> x3, starting transfers between devices: 9.07 us -> 28.1 us  [exchange(): return lax.all_to_all(value, axes, split_axis=0, concat_axis=0, tiled=True)]
    unnamed x10 -> x46, local copies, waits for them, and re-layouts: 0.03 us -> 16.6 us
    all_to_all x1 -> x3, waiting for transfers between devices: 25.9 us -> 41.6 us  [exchange(): return lax.all_to_all(value, axes, split_axis=0, concat_axis=0, tiled=True)]
  transfers between devices with their start and end apart: 2 -> 17, of which waited for: 2 -> 10; matrix products, arithmetic and copies ran while one was open for 8% -> 2% of each run, Pallas kernels for 0% -> 1%
where the time goes in v2:
time: 266 us; the launch traced here: 265 us
  waiting for transfers between devices  98.6 us (37%)
  blocking collectives  80.3 us (30%)
  starting transfers between devices  41.3 us (16%)
  local copies, waits for them, and re-layouts  20.2 us (8%)
  Pallas kernels  15.7 us (6%)
  other arithmetic  4.74 us (2%)
    all_to_all x2, blocking collectives, exchange(): return lax.all_to_all(value, axes, split_axis=0, concat_axis=0, tiled=True)  80.3 us
    ppermute x8, waiting for transfers between devices, shift(): lax.ppermute(value, 'z', [(i, (i + step) % count) for i in range(count)])  56.9 us
    all_to_all x3, waiting for transfers between devices, exchange(): return lax.all_to_all(value, axes, split_axis=0, concat_axis=0, tiled=True)  41.6 us
    all_to_all x3, starting transfers between devices, exchange(): return lax.all_to_all(value, axes, split_axis=0, concat_axis=0, tiled=True)  28.1 us
    unnamed x46, local copies, waits for them, and re-layouts  16.6 us
    pallas_call x1, Pallas kernels, multiply(): pl.pallas_call(product_kernel, grid_spec=pltpu.PrefetchScalarGridSpec(num...  12.4 us
    ppermute x8, starting transfers between devices, shift(): lax.ppermute(value, 'z', [(i, (i + step) % count) for i in range(count)])  8.25 us
  transfers between devices with their start and end apart: 17, of which 10 were waited for; matrix products, arithmetic and copies ran while one was open for 2% of the time, Pallas kernels for 1%

profile of v2, /device:TPU:1, one launch (start us, length us, event | category | flops | bytes accessed | tf_op | source)
XLA Modules:
  0.0 265.4 jit_solution(5438094442591189071)
XLA Ops:
  0.7 2.2 copy-done.1
  4.2 2.1 collective-permute-start.10
  6.3 2.0 shard_map.78.own_b
  8.2 1.3 collective-permute-start.11
  9.5 54.1 %all_to_all.26 = bf16[32,8,1024]{2,1,0:T(8,128)(2,1)S(1)} all-to-all(bf16[32,8,1024]{2,1,0:T(8,128)(2,1)S(1)} %bitcast.31), channel_id=1, replica_groups=mesh['xlo'=2,'z'=8,'core'=2,'xhi'=2,'y'=4] {'xlo','core','xhi','y'}, dimensions={0} | all-to-all | bytes 1048576 | tf_op jit(solution)/shard_map/all_to_all | solution.py:221
  63.6 1.6 collective-permute-start
  65.3 3.9 %collective-permute-start.3 = (bf16[32,8192]{1,0:T(8,128)(2,1)S(1)}, bf16[32,8192]{1,0:T(8,128)(2,1)S(1)}, u32[]{:S(2)}, u32[]{:S(2)}) collective-permute-start(bf16[32,8192]{1,0:T(8,128)(2,1)S(1)} %bitcast.29), channel_id=1, source_target_pairs={{0,112},{16,0},{32,16},{48,32},{64,48},{80,64},{96,80},{112,96},{1... | collective-permute-start | bytes 1572872 | tf_op jit(solution)/shard_map/ppermute | solution.py:209
  69.2 12.0 %collective-permute-done.p1 = bf16[32,8192]{1,0:T(8,128)(2,1)S(1)} collective-permute-done((bf16[32,8192]{1,0:T(8,128)(2,1)S(1)}, bf16[32,8192]{1,0:T(8,128)(2,1)S(1)}, u32[]{:S(2)}, u32[]{:S(2)}) %collective-permute-start) | collective-permute-done | bytes 524320 | tf_op jit(solution)/shard_map/ppermute | solution.py:209
  83.5 11.4 %collective-permute-done.1.p2 = bf16[32,8192]{1,0:T(8,128)(2,1)S(1)} collective-permute-done((bf16[32,8192]{1,0:T(8,128)(2,1)S(1)}, bf16[32,8192]{1,0:T(8,128)(2,1)S(1)}, u32[]{:S(2)}, u32[]{:S(2)}) %collective-permute-start.1) | collective-permute-done | bytes 524320 | tf_op jit(solution)/shard_map/ppermute | solution.py:209
  95.7 10.8 %collective-permute-done.4.m2 = bf16[32,8192]{1,0:T(8,128)(2,1)S(1)} collective-permute-done((bf16[32,8192]{1,0:T(8,128)(2,1)S(1)}, bf16[32,8192]{1,0:T(8,128)(2,1)S(1)}, u32[]{:S(2)}, u32[]{:S(2)}) %collective-permute-start.4) | collective-permute-done | bytes 524320 | tf_op jit(solution)/shard_map/ppermute | solution.py:209
  107.3 11.1 %collective-permute-done.2.p3 = bf16[32,8192]{1,0:T(8,128)(2,1)S(1)} collective-permute-done((bf16[32,8192]{1,0:T(8,128)(2,1)S(1)}, bf16[32,8192]{1,0:T(8,128)(2,1)S(1)}, u32[]{:S(2)}, u32[]{:S(2)}) %collective-permute-start.2) | collective-permute-done | bytes 524320 | tf_op jit(solution)/shard_map/ppermute | solution.py:209
  120.1 8.1 %collective-permute-done.5.m3 = bf16[32,8192]{1,0:T(8,128)(2,1)S(1)} collective-permute-done((bf16[32,8192]{1,0:T(8,128)(2,1)S(1)}, bf16[32,8192]{1,0:T(8,128)(2,1)S(1)}, u32[]{:S(2)}, u32[]{:S(2)}) %collective-permute-start.5) | collective-permute-done | bytes 524320 | tf_op jit(solution)/shard_map/ppermute | solution.py:209
  129.1 1.3 copy-done.2
  130.4 2.5 collective-permute-start.7
  133.0 1.8 collective-permute-done.6.top
  134.8 1.7 collective-permute-done.7.low
  136.5 1.6 copy-done.3
  138.1 1.0 copy-done.7
  140.2 1.0 copy-done.13
  143.3 12.4 %shard_map.79 = (f32[8,264,128]{2,1,0:T(8,128)S(1)}, f32[32,64,128]{2,1,0:T(8,128)S(1)}) custom-call(s32[3]{0:T(128)S(1)} %pad_add_fusion.place_ref, bf16[32,8192]{1,0:T(8,128)(2,1)S(1)} %bitcast.30, bf16[32,8192]{1,0:T(8,128)(2,1)S(1)} %copy-done.11, bf16[32,8192]{1,0:T(8,128)(2,1)S(1)} %copy-done.15, bf16[32,8192]{1,0:T(8,128)(2,1)S(1)} %collective-permute-done.2.p3, ...), custom_call_target="tpu_custom_call" | custom-call | flops 4294967296 | bytes 25165824 | tf_op jit(solution)/shard_map/pallas_call | solution.py:132
  155.8 26.2 %all_to_all.27 = f32[8,264,128]{2,1,0:T(8,128)S(1)} all-to-all(f32[8,264,128]{2,1,0:T(8,128)S(1)} %get-tuple-element.13), channel_id=1, replica_groups=mesh['xlo'=2,'z'=8,'core'=2,'xhi'=2,'y'=4] {'z'}, dimensions={0} | all-to-all | bytes 2162688 | tf_op jit(solution)/shard_map/all_to_all | solution.py:221
  181.9 16.9 %all-to-all-start.1 = ((f32[32,64,128]{2,1,0:T(8,128)}), f32[32,64,128]{2,1,0:T(8,128)S(1)}, u32[]{:S(2)}, u32[]{:S(2)}) async-start(f32[32,64,128]{2,1,0:T(8,128)} %copy-done.9), calls=%async_computation.1 | async-start | bytes 2097152 | tf_op jit(solution)/shard_map/all_to_all | solution.py:221
  199.1 1.1 pad_maximum_fusion
  200.2 14.7 %all-to-all-done.1.home_ref = f32[32,64,128]{2,1,0:T(8,128)S(1)} async-done(((f32[32,64,128]{2,1,0:T(8,128)}), f32[32,64,128]{2,1,0:T(8,128)S(1)}, u32[]{:S(2)}, u32[]{:S(2)}) %all-to-all-start.1) | async-done | bytes 1048608 | tf_op jit(solution)/shard_map/all_to_all | solution.py:221
  214.9 5.1 %all-to-all-start.3 = ((f32[32,72,128]{2,1,0:T(8,128)}), f32[32,72,128]{2,1,0:T(8,128)S(1)}, u32[]{:S(2)}, u32[]{:S(2)}) async-start(f32[32,72,128]{2,1,0:T(8,128)} %pad_maximum_fusion), calls=%async_computation.3 | async-start | bytes 2359296 | tf_op jit(solution)/shard_map/all_to_all | solution.py:221
  220.8 1.9 convolution_add_fusion.diag_ref
  222.7 14.7 %all-to-all-done.3.turn_ref = f32[32,72,128]{2,1,0:T(8,128)S(1)} async-done(((f32[32,72,128]{2,1,0:T(8,128)}), f32[32,72,128]{2,1,0:T(8,128)S(1)}, u32[]{:S(2)}, u32[]{:S(2)}) %all-to-all-start.3) | async-done | bytes 1179680 | tf_op jit(solution)/shard_map/all_to_all | solution.py:221
  237.4 1.0 copy-done.5
  240.9 6.2 %all-to-all-start.4 = ((f32[256,1,128]{2,1,0:T(1,128)}), f32[256,1,128]{2,1,0:T(1,128)S(1)}, u32[]{:S(2)}, u32[]{:S(2)}) async-start(f32[256,1,128]{2,1,0:T(1,128)} %broadcast_in_dim.9), calls=%async_computation.4 | async-start | bytes 262144 | tf_op jit(solution)/shard_map/all_to_all | solution.py:221
  247.6 12.3 %all-to-all-done.4 = f32[256,1,128]{2,1,0:T(1,128)S(1)} async-done(((f32[256,1,128]{2,1,0:T(1,128)}), f32[256,1,128]{2,1,0:T(1,128)S(1)}, u32[]{:S(2)}, u32[]{:S(2)}) %all-to-all-start.4) | async-done | bytes 131104 | tf_op jit(solution)/shard_map/all_to_all | solution.py:221
  262.0 1.1 pad_maximum_fusion.1
  263.1 2.3 broadcast_multiply_fusion
  (74 shorter events, 15.7 us)
Async XLA Ops:
  0.6 219.8 %copy-start = (f32[16,16]{1,0:T(8,128)S(1)}, f32[16,16]{1,0:T(8,128)}, u32[]{:S(2)}) copy-start(f32[16,16]{1,0:T(8,128)} %param.11) | copy-start | bytes 3076
  0.6 2.2 copy-start.1
  3.5 2.7 %copy-start.19 = (s32[8,256]{1,0:T(8,128)S(1)}, s32[8,256]{1,0:T(8,128)}, u32[]{:S(2)}) copy-start(s32[8,256]{1,0:T(8,128)} %mask_ref.3) | copy-start | bytes 24580
  4.1 5.4 %copy-start.4 = (bf16[256,1024]{1,0:T(8,128)(2,1)S(1)}, bf16[256,1024]{1,0:T(8,128)(2,1)}, u32[]{:S(2)}) copy-start(bf16[256,1024]{1,0:T(8,128)(2,1)} %coeff_ref.1) | copy-start | bytes 1572868
  4.2 78.7 %collective-permute-start.10 = (bf16[256,4096]{1,0:T(8,128)(2,1)S(1)}, bf16[256,4096]{1,0:T(8,128)(2,1)}, u32[]{:S(2)}, u32[]{:S(2)}) collective-permute-start(bf16[256,4096]{1,0:T(8,128)(2,1)S(1)} %shard_map.77.own_a), channel_id=1, source_target_pairs={{0,128},{128,4},{4,132},{132,0},{1,129},{129,5},{5,133},{133,1},{2... | collective-permute-start | bytes 6291464 | tf_op jit(solution)/shard_map/ppermute | solution.py:217
  8.2 75.2 %collective-permute-start.11 = (bf16[256,4096]{1,0:T(8,128)(2,1)}, bf16[256,4096]{1,0:T(8,128)(2,1)}, u32[]{:S(2)}, u32[]{:S(2)}) collective-permute-start(bf16[256,4096]{1,0:T(8,128)(2,1)} %shard_map.78.own_b), channel_id=1, source_target_pairs={{0,132},{128,0},{4,128},{132,4},{1,133},{129,1},{5,129},{133,5},{2... | collective-permute-start | bytes 6291464 | tf_op jit(solution)/shard_map/ppermute | solution.py:217
  63.6 17.5 %collective-permute-start = (bf16[32,8192]{1,0:T(8,128)(2,1)S(1)}, bf16[32,8192]{1,0:T(8,128)(2,1)S(1)}, u32[]{:S(2)}, u32[]{:S(2)}) collective-permute-start(bf16[32,8192]{1,0:T(8,128)(2,1)S(1)} %bitcast.28), channel_id=1, source_target_pairs={{0,16},{16,32},{32,48},{48,64},{64,80},{80,96},{96,112},{112,0},{1... | collective-permute-start | bytes 1572872 | tf_op jit(solution)/shard_map/ppermute | solution.py:209
  65.3 17.6 %collective-permute-start.3 = (bf16[32,8192]{1,0:T(8,128)(2,1)S(1)}, bf16[32,8192]{1,0:T(8,128)(2,1)S(1)}, u32[]{:S(2)}, u32[]{:S(2)}) collective-permute-start(bf16[32,8192]{1,0:T(8,128)(2,1)S(1)} %bitcast.29), channel_id=1, source_target_pairs={{0,112},{16,0},{32,16},{48,32},{64,48},{80,64},{96,80},{112,96},{1... | collective-permute-start | bytes 1572872 | tf_op jit(solution)/shard_map/ppermute | solution.py:209
  81.2 13.7 %collective-permute-start.1 = (bf16[32,8192]{1,0:T(8,128)(2,1)S(1)}, bf16[32,8192]{1,0:T(8,128)(2,1)S(1)}, u32[]{:S(2)}, u32[]{:S(2)}) collective-permute-start(bf16[32,8192]{1,0:T(8,128)(2,1)S(1)} %collective-permute-done.p1), channel_id=1, source_target_pairs={{0,16},{16,32},{32,48},{48,64},{64,80},{80,96},{96,112},{112,0},{1... | collective-permute-start | bytes 1572872 | tf_op jit(solution)/shard_map/ppermute | solution.py:209
  82.0 47.0 %collective-permute-start.8 = (bf16[256,4096]{1,0:T(8,128)(2,1)S(1)}, bf16[256,4096]{1,0:T(8,128)(2,1)S(1)}, u32[]{:S(2)}, u32[]{:S(2)}) collective-permute-start(bf16[256,4096]{1,0:T(8,128)(2,1)S(1)} %shard_map.77.own_a), channel_id=1, source_target_pairs={{0,8},{8,0},{1,9},{9,1},{2,10},{10,2},{3,11},{11,3},{4,12},{12,4},... | collective-permute-start | bytes 6291464 | tf_op jit(solution)/shard_map/ppermute | solution.py:204
  82.9 50.1 %collective-permute-start.9 = (bf16[256,4096]{1,0:T(8,128)(2,1)}, bf16[256,4096]{1,0:T(8,128)(2,1)}, u32[]{:S(2)}, u32[]{:S(2)}) collective-permute-start(bf16[256,4096]{1,0:T(8,128)(2,1)} %shard_map.78.own_b), channel_id=1, source_target_pairs={{0,8},{8,0},{1,9},{9,1},{2,10},{10,2},{3,11},{11,3},{4,12},{12,4},... | collective-permute-start | bytes 6291464 | tf_op jit(solution)/shard_map/ppermute | solution.py:204
  82.9 53.6 %collective-permute-start.12 = (bf16[256,4096]{1,0:T(8,128)(2,1)}, bf16[256,4096]{1,0:T(8,128)(2,1)}, u32[]{:S(2)}, u32[]{:S(2)}) collective-permute-start(bf16[256,4096]{1,0:T(8,128)(2,1)} %collective-permute-done.10.far_a), channel_id=1, source_target_pairs={{0,8},{8,0},{1,9},{9,1},{2,10},{10,2},{3,11},{11,3},{4,12},{12,4},... | collective-permute-start | bytes 6291464 | tf_op jit(solution)/shard_map/ppermute | solution.py:204
  83.4 53.1 %collective-permute-start.13 = (bf16[256,4096]{1,0:T(8,128)(2,1)}, bf16[256,4096]{1,0:T(8,128)(2,1)}, u32[]{:S(2)}, u32[]{:S(2)}) collective-permute-start(bf16[256,4096]{1,0:T(8,128)(2,1)} %collective-permute-done.11.far_b), channel_id=1, source_target_pairs={{0,8},{8,0},{1,9},{9,1},{2,10},{10,2},{3,11},{11,3},{4,12},{12,4},... | collective-permute-start | bytes 6291464 | tf_op jit(solution)/shard_map/ppermute | solution.py:204
  94.9 11.6 %collective-permute-start.4 = (bf16[32,8192]{1,0:T(8,128)(2,1)S(1)}, bf16[32,8192]{1,0:T(8,128)(2,1)S(1)}, u32[]{:S(2)}, u32[]{:S(2)}) collective-permute-start(bf16[32,8192]{1,0:T(8,128)(2,1)S(1)} %collective-permute-done.3.m1), channel_id=1, source_target_pairs={{0,112},{16,0},{32,16},{48,32},{64,48},{80,64},{96,80},{112,96},{1... | collective-permute-start | bytes 1572872 | tf_op jit(solution)/shard_map/ppermute | solution.py:209
  106.5 11.9 %collective-permute-start.2 = (bf16[32,8192]{1,0:T(8,128)(2,1)S(1)}, bf16[32,8192]{1,0:T(8,128)(2,1)S(1)}, u32[]{:S(2)}, u32[]{:S(2)}) collective-permute-start(bf16[32,8192]{1,0:T(8,128)(2,1)S(1)} %collective-permute-done.1.p2), channel_id=1, source_target_pairs={{0,16},{16,32},{32,48},{48,64},{64,80},{80,96},{96,112},{112,0},{1... | collective-permute-start | bytes 1572872 | tf_op jit(solution)/shard_map/ppermute | solution.py:209
  118.4 9.8 %collective-permute-start.5 = (bf16[32,8192]{1,0:T(8,128)(2,1)S(1)}, bf16[32,8192]{1,0:T(8,128)(2,1)S(1)}, u32[]{:S(2)}, u32[]{:S(2)}) collective-permute-start(bf16[32,8192]{1,0:T(8,128)(2,1)S(1)} %collective-permute-done.4.m2), channel_id=1, source_target_pairs={{0,112},{16,0},{32,16},{48,32},{64,48},{80,64},{96,80},{112,96},{1... | collective-permute-start | bytes 1572872 | tf_op jit(solution)/shard_map/ppermute | solution.py:209
  128.2 6.6 %collective-permute-start.6 = (bf16[16,8192]{1,0:T(8,128)(2,1)}, bf16[16,8192]{1,0:T(8,128)(2,1)S(1)}, u32[]{:S(2)}, u32[]{:S(2)}) collective-permute-start(bf16[16,8192]{1,0:T(8,128)(2,1)} %slice.35), channel_id=1, source_target_pairs={{0,16},{16,32},{32,48},{48,64},{64,80},{80,96},{96,112},{112,0},{1... | collective-permute-start | bytes 786440 | tf_op jit(solution)/shard_map/ppermute | solution.py:209
  129.1 1.3 copy-start.2
  130.4 6.2 %collective-permute-start.7 = (bf16[16,8192]{1,0:T(8,128)(2,1)}, bf16[16,8192]{1,0:T(8,128)(2,1)}, u32[]{:S(2)}, u32[]{:S(2)}) collective-permute-start(bf16[16,8192]{1,0:T(8,128)(2,1)} %slice.36), channel_id=1, source_target_pairs={{0,112},{16,0},{32,16},{48,32},{64,48},{80,64},{96,80},{112,96},{1... | collective-permute-start | bytes 786440 | tf_op jit(solution)/shard_map/ppermute | solution.py:209
  136.5 1.6 copy-start.3
  138.1 1.0 copy-start.7
  139.2 1.0 copy-start.11
  140.2 1.0 copy-start.13
  141.3 1.0 copy-start.15
  142.3 1.0 copy-start.17
  155.8 26.2 %copy-start.9 = (f32[32,64,128]{2,1,0:T(8,128)}, f32[32,64,128]{2,1,0:T(8,128)S(1)}, u32[]{:S(2)}) copy-start(f32[32,64,128]{2,1,0:T(8,128)S(1)} %get-tuple-element.12) | copy-start | bytes 3145732
  181.9 32.9 %all-to-all-start.1 = ((f32[32,64,128]{2,1,0:T(8,128)}), f32[32,64,128]{2,1,0:T(8,128)S(1)}, u32[]{:S(2)}, u32[]{:S(2)}) async-start(f32[32,64,128]{2,1,0:T(8,128)} %copy-done.9), calls=%async_computation.1 | async-start | bytes 2097152 | tf_op jit(solution)/shard_map/all_to_all | solution.py:221
  199.1 20.9 %copy-start.21 = (s32[16,8192]{1,0:T(8,128)S(1)}, s32[16,8192]{1,0:T(8,128)}, u32[]{:S(2)}) copy-start(s32[16,8192]{1,0:T(8,128)} %param.9) | copy-start | bytes 1572868
  200.2 19.9 %copy-start.22 = (f32[16]{0:T(128)S(1)}, f32[16]{0:T(128)}, u32[]{:S(2)}) copy-start(f32[16]{0:T(128)} %param.10) | copy-start | bytes 196
  214.9 22.5 %all-to-all-start.3 = ((f32[32,72,128]{2,1,0:T(8,128)}), f32[32,72,128]{2,1,0:T(8,128)S(1)}, u32[]{:S(2)}, u32[]{:S(2)}) async-start(f32[32,72,128]{2,1,0:T(8,128)} %pad_maximum_fusion), calls=%async_computation.3 | async-start | bytes 2359296 | tf_op jit(solution)/shard_map/all_to_all | solution.py:221
  237.4 1.0 copy-start.5
  240.9 19.0 %all-to-all-start.4 = ((f32[256,1,128]{2,1,0:T(1,128)}), f32[256,1,128]{2,1,0:T(1,128)S(1)}, u32[]{:S(2)}, u32[]{:S(2)}) async-start(f32[256,1,128]{2,1,0:T(1,128)} %broadcast_in_dim.9), calls=%async_computation.4 | async-start | bytes 262144 | tf_op jit(solution)/shard_map/all_to_all | solution.py:221
  (8 other events, 6.5 us)

commit v3 on v2

--- a/solution.py
+++ b/solution.py
@@ -19,10 +19,9 @@
 def mask_kernel(ham_ref, mask_ref, out_ref):
     rows, cols = ham_ref.shape
     mask_rows, mask_cols = mask_ref.shape
-    size = cols // mask_cols
-    tile = rows // mask_rows
+    tile = size = rows // mask_rows
     spread = (
-        lax.broadcasted_iota(jnp.int32, (mask_cols, cols), 1) // size
+        lax.broadcasted_iota(jnp.int32, (mask_cols, cols), 1) // size + pl.program_id(0) * (cols // size)
         == lax.broadcasted_iota(jnp.int32, (mask_cols, cols), 0)
     ).astype(jnp.bfloat16)
     mask = mask_ref[...].astype(jnp.float32).astype(jnp.bfloat16)
@@ -38,14 +37,14 @@
     mask_rows, mask_cols = tile_mask.shape
     return pl.pallas_call(
         mask_kernel,
-        grid=(1,),
+        grid=(4,),
         in_specs=[
-            pl.BlockSpec((rows, cols // 2), lambda j: (0, half)),
+            pl.BlockSpec((rows, cols // 8), lambda j: (0, half * 4 + j)),
             pl.BlockSpec((mask_rows, mask_cols // 2), lambda j: (0, half)),
         ],
-        out_specs=pl.BlockSpec((rows, cols // 2), lambda j: (0, 0)),
+        out_specs=pl.BlockSpec((rows, cols // 8), lambda j: (0, j)),
         out_shape=jax.ShapeDtypeStruct((rows, cols // 2), jnp.bfloat16),
-        compiler_params=pltpu.CompilerParams(vmem_limit_bytes=32 * MIB),
+        compiler_params=pltpu.CompilerParams(vmem_limit_bytes=60 * MIB),
         cost_estimate=pl.CostEstimate(
             flops=rows * cols, bytes_accessed=2 * rows * cols, transcendentals=0
         ),
@@ -149,15 +148,15 @@
             jax.ShapeDtypeStruct((8, 264, LANES), jnp.float32),
             jax.ShapeDtypeStruct((32, 64, LANES), jnp.float32),
         ],
-        compiler_params=pltpu.CompilerParams(vmem_limit_bytes=40 * MIB),
+        compiler_params=pltpu.CompilerParams(vmem_limit_bytes=60 * MIB),
         cost_estimate=pl.CostEstimate(
             flops=2 * 256 * 1024 * strings, bytes_accessed=24 * MIB, transcendentals=0
         ),
     )(place, *blocks, *halves)
 
 
-def update_kernel(home_ref, turn_ref, coeff_ref, diag_ref, update_ref, sums_ref):
-    totals = jnp.sum(turn_ref[:, 64:72, :], axis=0)
+def update_kernel(tiles_ref, coeff_ref, diag_ref, update_ref, sums_ref):
+    totals = jnp.sum(tiles_ref[:, 128:136, :], axis=0)
     lane = lax.broadcasted_iota(jnp.int32, (8, LANES), 1)
     row = lax.broadcasted_iota(jnp.int32, (8, LANES), 0)
     projection = jnp.sum(jnp.where(lane == 0, totals, 0.0))
@@ -171,9 +170,9 @@
             cols = slice(index * LANES, index * LANES + LANES)
             quarter, group = index // 2, index % 2
             at = part * 32 + quarter * 8
-            straight = home_ref[group * 16 : group * 16 + 16, at : at + 8, :]
+            straight = tiles_ref[group * 16 : group * 16 + 16, at : at + 8, :]
             straight = straight.reshape(LANES, LANES).T
-            turned = turn_ref[part * 16 : part * 16 + 16, index * 8 : index * 8 + 8, :]
+            turned = tiles_ref[part * 16 : part * 16 + 16, 64 + index * 8 : 72 + index * 8, :]
             turned = turned.reshape(LANES, LANES)
             coeff = coeff_ref[rows, cols].astype(jnp.float32)
             residual = straight + turned - theta * coeff
@@ -186,18 +185,18 @@
     sums_ref[...] = jnp.where(row == 0, values, 0.0)
 
 
-def make_update(home, turn, coeff, diagonal):
+def make_update(tiles, coeff, diagonal):
     return pl.pallas_call(
         update_kernel,
         out_shape=[
             jax.ShapeDtypeStruct(coeff.shape, jnp.float32),
             jax.ShapeDtypeStruct((8, LANES), jnp.float32),
         ],
-        compiler_params=pltpu.CompilerParams(vmem_limit_bytes=32 * MIB),
+        compiler_params=pltpu.CompilerParams(vmem_limit_bytes=16 * MIB),
         cost_estimate=pl.CostEstimate(
             flops=10 * coeff.size, bytes_accessed=5 * MIB, transcendentals=0
         ),
-    )(home, turn, coeff, diagonal)
+    )(tiles, coeff, diagonal)
 
 
 def swap(value):
@@ -232,16 +231,18 @@
 
     own_a = mask_half(ham, tile_mask, 0)
     own_b = mask_half(ham, tile_mask, 1)
+    pair_a, pair_b = swap(own_a), swap(own_b)
+
+    block = exchange(coeff.reshape(32, 8, cols), PLANE)
+    block, own_a, own_b, pair_a, pair_b = lax.optimization_barrier(
+        (block, own_a, own_b, pair_a, pair_b)
+    )
     far_a, far_b = shift_x(own_a, 1), shift_x(own_b, -1)
-    pair_a, pair_b = swap(own_a), swap(own_b)
+    block = block.reshape(4, 8, 8, cols).transpose(0, 2, 1, 3).reshape(32, strings)
+    p1, m1 = lax.optimization_barrier((shift(block, 1), shift(block, -1)))
+    p2, m2 = lax.optimization_barrier((shift(p1, 1), shift(m1, -1)))
+    p3, m3, far_a, far_b = lax.optimization_barrier((shift(p2, 1), shift(m2, -1), far_a, far_b))
     cross_a, cross_b = swap(far_a), swap(far_b)
-
-    coeff_in, own_a, own_b = lax.optimization_barrier((coeff, own_a, own_b))
-    block = exchange(coeff_in.reshape(32, 8, cols), PLANE)
-    block = block.reshape(4, 8, 8, cols).transpose(0, 2, 1, 3).reshape(32, strings)
-    p1, m1 = shift(block, 1), shift(block, -1)
-    p2, m2 = shift(p1, 1), shift(m1, -1)
-    p3, m3 = shift(p2, 1), shift(m2, -1)
     top, low = shift(p3[:16], 1), shift(m3[16:], -1)
 
     place = jnp.stack([xlo, z, core]).astype(jnp.int32)
@@ -251,13 +252,12 @@
         (own_a, own_b, pair_a, pair_b, far_a, far_b, cross_a, cross_b),
     )
 
-    home = exchange(home, PLANE)
     turn = exchange(turn, "z")
     sums = jnp.sum(turn[:, 256:], axis=0)
     turn = turn[:, :256].reshape(4, 2, 2, 2, 2, 2, 2, 8, LANES)
     turn = turn.transpose(5, 6, 2, 0, 1, 3, 4, 7, 8).reshape(32, 64, LANES)
-    turn = jnp.concatenate([turn, jnp.broadcast_to(sums, (32, 8, LANES))], axis=1)
-    turn = exchange(turn, PLANE)
+    tiles = jnp.concatenate([home, turn, jnp.broadcast_to(sums, (32, 8, LANES))], axis=1)
+    tiles = exchange(tiles, PLANE)
 
     occ_float = occupation.astype(jnp.float32)
     occ_alpha = lax.dynamic_slice_in_dim(occ_float, row_index * rows, rows, 1)
@@ -271,7 +271,7 @@
     )
     diagonal = energy_alpha[:, None] + energy_beta[None, :] + coupling
 
-    update, sums = make_update(home, turn, coeff, diagonal)
+    update, sums = make_update(tiles, coeff, diagonal)
     theta = sums[0, 2]
     totals = exchange(jnp.broadcast_to(sums[0], (256, LANES)), AXES)
     totals = jnp.sum(totals, axis=0)

time: 266 us -> 211 us (0.79)
  blocking collectives: 80.3 us -> 48.3 us
  waiting for transfers between devices: 98.6 us -> 75.4 us
  local copies, waits for them, and re-layouts: 20.2 us -> 8.21 us
  Pallas kernels: 15.7 us -> 24.2 us
    all_to_all x2, blocking collectives: 80.3 us -> 48.3 us  [exchange(): return lax.all_to_all(value, axes, split_axis=0, concat_axis=0, tiled=True)]
    ppermute x8, waiting for transfers between devices: 56.9 us -> 32.7 us  [shift(): lax.ppermute(value, 'z', [(i, (i + step) % count) for i in range(count)])]
    unnamed x46 -> x38, local copies, waits for them, and re-layouts: 16.6 us -> 4.63 us
    all_to_all x3 -> x2, starting transfers between devices: 28.1 us -> 17.6 us  [exchange(): return lax.all_to_all(value, axes, split_axis=0, concat_axis=0, tiled=True)]
    ppermute x8, starting transfers between devices: 8.25 us -> 16.7 us  [shift(): lax.ppermute(value, 'z', [(i, (i + step) % count) for i in range(count)])]
    pallas_call x2, Pallas kernels: 2.55 us -> 8.56 us  [mask_half(): pl.pallas_call(mask_kernel, grid=(4,), in_specs=[pl.BlockSpec((rows, cols...]
    ppermute x2, waiting for transfers between devices: 0.01 us -> 5.37 us  [shift_x(): return lax.ppermute(value, ('xlo', 'xhi'), pairs)]
    ppermute x4, starting transfers between devices: 1.51 us -> 6.34 us  [swap(): return lax.ppermute(value, 'core', [(0, 1), (1, 0)])]
  transfers between devices with their start and end apart: 17 -> 16, of which waited for: 10 -> 7; matrix products, arithmetic and copies ran while one was open for 2% -> 2% of each run, Pallas kernels for 1% -> 2%
where the time goes in v3:
time: 211 us; the launch traced here: 210 us
  waiting for transfers between devices  75.4 us (36%)
  blocking collectives  48.3 us (23%)
  starting transfers between devices  43.3 us (21%)
  Pallas kernels  24.2 us (11%)
  local copies, waits for them, and re-layouts  8.21 us (4%)
  other arithmetic  5.78 us (3%)
  matrix products  2.39 us (1%)
  between operations  2.22 us (1%)
    all_to_all x2, blocking collectives, exchange(): return lax.all_to_all(value, axes, split_axis=0, concat_axis=0, tiled=True)  48.3 us
    all_to_all x2, waiting for transfers between devices, exchange(): return lax.all_to_all(value, axes, split_axis=0, concat_axis=0, tiled=True)  37.4 us
    ppermute x8, waiting for transfers between devices, shift(): lax.ppermute(value, 'z', [(i, (i + step) % count) for i in range(count)])  32.7 us
    all_to_all x2, starting transfers between devices, exchange(): return lax.all_to_all(value, axes, split_axis=0, concat_axis=0, tiled=True)  17.6 us
    ppermute x8, starting transfers between devices, shift(): lax.ppermute(value, 'z', [(i, (i + step) % count) for i in range(count)])  16.7 us
    pallas_call x1, Pallas kernels, multiply(): pl.pallas_call(product_kernel, grid_spec=pltpu.PrefetchScalarGridSpec(num...  14.9 us
    pallas_call x2, Pallas kernels, mask_half(): pl.pallas_call(mask_kernel, grid=(4,), in_specs=[pl.BlockSpec((rows, cols...  8.56 us
    ppermute x4, starting transfers between devices, swap(): return lax.ppermute(value, 'core', [(0, 1), (1, 0)])  6.34 us
  transfers between devices with their start and end apart: 16, of which 7 were waited for; matrix products, arithmetic and copies ran while one was open for 2% of the time, Pallas kernels for 2%

profile of v3, /device:TPU:1, one launch (start us, length us, event | category | flops | bytes accessed | tf_op | source)
XLA Modules:
  0.0 209.8 jit_solution(16739107986696201690)
XLA Ops:
  0.6 4.3 %shard_map.77.own_a = bf16[256,4096]{1,0:T(8,128)(2,1)} custom-call(bf16[256,8192]{1,0:T(8,128)(2,1)} %ham_ref.3, s32[8,256]{1,0:T(8,128)} %mask_ref.3), custom_call_target="tpu_custom_call" | custom-call | flops 2097152 | bytes 4194304 | tf_op jit(solution)/shard_map/pallas_call | solution.py:38
  4.9 3.2 %collective-permute-start = (bf16[256,4096]{1,0:T(8,128)(2,1)}, bf16[256,4096]{1,0:T(8,128)(2,1)}, u32[]{:S(2)}, u32[]{:S(2)}) collective-permute-start(bf16[256,4096]{1,0:T(8,128)(2,1)} %shard_map.77.own_a), channel_id=1, source_target_pairs={{0,8},{8,0},{1,9},{9,1},{2,10},{10,2},{3,11},{11,3},{4,12},{12,4},... | collective-permute-start | bytes 6291464 | tf_op jit(solution)/shard_map/ppermute | solution.py:203
  8.2 4.3 %shard_map.78.own_b = bf16[256,4096]{1,0:T(8,128)(2,1)} custom-call(bf16[256,8192]{1,0:T(8,128)(2,1)} %ham_ref.3, s32[8,256]{1,0:T(8,128)} %mask_ref.3), custom_call_target="tpu_custom_call" | custom-call | flops 2097152 | bytes 4194304 | tf_op jit(solution)/shard_map/pallas_call | solution.py:38
  12.6 16.1 %all_to_all.21 = bf16[32,8,1024]{2,1,0:T(8,128)(2,1)S(1)} all-to-all(bf16[32,8,1024]{2,1,0:T(8,128)(2,1)S(1)} %bitcast.28), channel_id=1, replica_groups=mesh['xlo'=2,'z'=8,'core'=2,'xhi'=2,'y'=4] {'xlo','core','xhi','y'}, dimensions={0} | all-to-all | bytes 1048576 | tf_op jit(solution)/shard_map/all_to_all | solution.py:220
  29.1 2.4 %collective-permute-start.9 = (bf16[256,4096]{1,0:T(8,128)(2,1)}, bf16[256,4096]{1,0:T(8,128)(2,1)}, u32[]{:S(2)}, u32[]{:S(2)}) collective-permute-start(bf16[256,4096]{1,0:T(8,128)(2,1)} %shard_map.78.own_b), channel_id=1, source_target_pairs={{0,132},{128,0},{4,128},{132,4},{1,133},{129,1},{5,129},{133,5},{2... | collective-permute-start | bytes 6291464 | tf_op jit(solution)/shard_map/ppermute | solution.py:216
  31.5 1.6 collective-permute-start.2
  33.1 3.9 %collective-permute-start.3 = (bf16[32,8192]{1,0:T(8,128)(2,1)S(1)}, bf16[32,8192]{1,0:T(8,128)(2,1)S(1)}, u32[]{:S(2)}, u32[]{:S(2)}) collective-permute-start(bf16[32,8192]{1,0:T(8,128)(2,1)S(1)} %bitcast.32), channel_id=1, source_target_pairs={{0,112},{16,0},{32,16},{48,32},{64,48},{80,64},{96,80},{112,96},{1... | collective-permute-start | bytes 1572872 | tf_op jit(solution)/shard_map/ppermute | solution.py:208
  37.1 10.0 %collective-permute-done.2.p1 = bf16[32,8192]{1,0:T(8,128)(2,1)S(1)} collective-permute-done((bf16[32,8192]{1,0:T(8,128)(2,1)S(1)}, bf16[32,8192]{1,0:T(8,128)(2,1)S(1)}, u32[]{:S(2)}, u32[]{:S(2)}) %collective-permute-start.2) | collective-permute-done | bytes 524320 | tf_op jit(solution)/shard_map/ppermute | solution.py:208
  47.1 2.7 %collective-permute-start.5 = (bf16[32,8192]{1,0:T(8,128)(2,1)S(1)}, bf16[32,8192]{1,0:T(8,128)(2,1)S(1)}, u32[]{:S(2)}, u32[]{:S(2)}) collective-permute-start(bf16[32,8192]{1,0:T(8,128)(2,1)S(1)} %collective-permute-done.3.m1), channel_id=1, source_target_pairs={{0,112},{16,0},{32,16},{48,32},{64,48},{80,64},{96,80},{112,96},{1... | collective-permute-start | bytes 1572872 | tf_op jit(solution)/shard_map/ppermute | solution.py:208
  49.8 9.2 %collective-permute-done.4.p2 = bf16[32,8192]{1,0:T(8,128)(2,1)S(1)} collective-permute-done((bf16[32,8192]{1,0:T(8,128)(2,1)S(1)}, bf16[32,8192]{1,0:T(8,128)(2,1)S(1)}, u32[]{:S(2)}, u32[]{:S(2)}) %collective-permute-start.4) | collective-permute-done | bytes 524320 | tf_op jit(solution)/shard_map/ppermute | solution.py:208
  59.0 1.0 collective-permute-start.6
  60.0 1.8 collective-permute-start.7
  61.7 8.3 %collective-permute-done.6.p3 = bf16[32,8192]{1,0:T(8,128)(2,1)S(1)} collective-permute-done((bf16[32,8192]{1,0:T(8,128)(2,1)S(1)}, bf16[32,8192]{1,0:T(8,128)(2,1)S(1)}, u32[]{:S(2)}, u32[]{:S(2)}) %collective-permute-start.6) | collective-permute-done | bytes 524320 | tf_op jit(solution)/shard_map/ppermute | solution.py:208
  70.1 5.4 %collective-permute-done.8.far_a = bf16[256,4096]{1,0:T(8,128)(2,1)} collective-permute-done((bf16[256,4096]{1,0:T(8,128)(2,1)S(1)}, bf16[256,4096]{1,0:T(8,128)(2,1)}, u32[]{:S(2)}, u32[]{:S(2)}) %collective-permute-start.8) | collective-permute-done | bytes 2097184 | tf_op jit(solution)/shard_map/ppermute | solution.py:216
  75.5 2.8 %collective-permute-start.12 = (bf16[256,4096]{1,0:T(8,128)(2,1)}, bf16[256,4096]{1,0:T(8,128)(2,1)S(1)}, u32[]{:S(2)}, u32[]{:S(2)}) collective-permute-start(bf16[256,4096]{1,0:T(8,128)(2,1)} %collective-permute-done.8.far_a), channel_id=1, source_target_pairs={{0,8},{8,0},{1,9},{9,1},{2,10},{10,2},{3,11},{11,3},{4,12},{12,4},... | collective-permute-start | bytes 6291464 | tf_op jit(solution)/shard_map/ppermute | solution.py:203
  79.1 1.6 collective-permute-start.10
  81.5 3.9 %collective-permute-start.11 = (bf16[16,8192]{1,0:T(8,128)(2,1)}, bf16[16,8192]{1,0:T(8,128)(2,1)}, u32[]{:S(2)}, u32[]{:S(2)}) collective-permute-start(bf16[16,8192]{1,0:T(8,128)(2,1)} %slice.27), channel_id=1, source_target_pairs={{0,112},{16,0},{32,16},{48,32},{64,48},{80,64},{96,80},{112,96},{1... | collective-permute-start | bytes 786440 | tf_op jit(solution)/shard_map/ppermute | solution.py:208
  86.1 5.2 %collective-permute-done.10.top = bf16[16,8192]{1,0:T(8,128)(2,1)S(1)} collective-permute-done((bf16[16,8192]{1,0:T(8,128)(2,1)}, bf16[16,8192]{1,0:T(8,128)(2,1)S(1)}, u32[]{:S(2)}, u32[]{:S(2)}) %collective-permute-start.10) | collective-permute-done | bytes 262176 | tf_op jit(solution)/shard_map/ppermute | solution.py:208
  92.6 14.9 %shard_map.79 = (f32[8,264,128]{2,1,0:T(8,128)}, f32[32,64,128]{2,1,0:T(8,128)}) custom-call(s32[3]{0:T(128)} %pad_add_fusion.place_ref, bf16[32,8192]{1,0:T(8,128)(2,1)} %bitcast.33, bf16[32,8192]{1,0:T(8,128)(2,1)} %copy-done.12, bf16[32,8192]{1,0:T(8,128)(2,1)} %copy-done.14, bf16[32,8192]{1,0:T(8,128)(2,1)} %copy-done.8, bf16[32,8192]{1,0:T(8,128)(2,1)} %copy-done.13, ...), custom_call_target="tpu_custom_call" | custom-call | flops 4294967296 | bytes 25165824 | tf_op jit(solution)/shard_map/pallas_call | solution.py:131
  107.5 32.2 %all_to_all.22 = f32[8,264,128]{2,1,0:T(8,128)S(1)} all-to-all(f32[8,264,128]{2,1,0:T(8,128)} %get-tuple-element.33), channel_id=1, replica_groups=mesh['xlo'=2,'z'=8,'core'=2,'xhi'=2,'y'=4] {'z'}, dimensions={0} | all-to-all | bytes 2162688 | tf_op jit(solution)/shard_map/all_to_all | solution.py:220
  139.9 1.0 copy-done.10
  140.9 1.6 pad_maximum_fusion
  142.5 10.4 %all-to-all-start.2 = ((f32[32,136,128]{2,1,0:T(8,128)}), f32[32,136,128]{2,1,0:T(8,128)S(1)}, u32[]{:S(2)}, u32[]{:S(2)}) async-start(f32[32,136,128]{2,1,0:T(8,128)} %pad_maximum_fusion), calls=%async_computation.2 | async-start | bytes 4456448 | tf_op jit(solution)/shard_map/all_to_all | solution.py:220
  153.8 1.9 convolution_add_fusion.diag_ref
  155.7 25.3 %all-to-all-done.2.tiles_ref = f32[32,136,128]{2,1,0:T(8,128)S(1)} async-done(((f32[32,136,128]{2,1,0:T(8,128)}), f32[32,136,128]{2,1,0:T(8,128)S(1)}, u32[]{:S(2)}, u32[]{:S(2)}) %all-to-all-start.2) | async-done | bytes 2228256 | tf_op jit(solution)/shard_map/all_to_all | solution.py:220
  180.9 1.0 copy-done.2
  182.0 0.8 shard_map.80
  182.8 1.0 copy-done.3
  184.5 7.2 %all-to-all-start.3 = ((f32[256,1,128]{2,1,0:T(1,128)}), f32[256,1,128]{2,1,0:T(1,128)S(1)}, u32[]{:S(2)}, u32[]{:S(2)}) async-start(f32[256,1,128]{2,1,0:T(1,128)} %broadcast_in_dim.9), calls=%async_computation.3 | async-start | bytes 262144 | tf_op jit(solution)/shard_map/all_to_all | solution.py:220
  192.2 12.1 %all-to-all-done.3 = f32[256,1,128]{2,1,0:T(1,128)S(1)} async-done(((f32[256,1,128]{2,1,0:T(1,128)}), f32[256,1,128]{2,1,0:T(1,128)S(1)}, u32[]{:S(2)}, u32[]{:S(2)}) %all-to-all-start.3) | async-done | bytes 131104 | tf_op jit(solution)/shard_map/all_to_all | solution.py:220
  206.3 1.2 pad_maximum_fusion.1
  207.5 2.3 %broadcast_multiply_fusion = f32[256,1024]{1,0:T(8,128)} fusion(f32[256,1024]{1,0:T(8,128)} %copy-done.3, f32[]{:T(128)} %bitcast.18), kind=kLoop, calls=%fused_computation.2 | loop fusion | flops 262144 | bytes 2097156 | tf_op jit(solution)/shard_map/mul | solution.py:278
  (64 shorter events, 7.2 us)
Async XLA Ops:
  0.6 152.7 %copy-start = (f32[16,16]{1,0:T(8,128)S(1)}, f32[16,16]{1,0:T(8,128)}, u32[]{:S(2)}) copy-start(f32[16,16]{1,0:T(8,128)} %param.11) | copy-start | bytes 3076
  4.9 7.7 %copy-start.1 = (bf16[256,1024]{1,0:T(8,128)(2,1)S(1)}, bf16[256,1024]{1,0:T(8,128)(2,1)}, u32[]{:S(2)}) copy-start(bf16[256,1024]{1,0:T(8,128)(2,1)} %coeff_ref.1) | copy-start | bytes 1572868
  4.9 23.8 %copy-start.4 = (bf16[256,4096]{1,0:T(8,128)(2,1)S(1)}, bf16[256,4096]{1,0:T(8,128)(2,1)}, u32[]{:S(2)}) copy-start(bf16[256,4096]{1,0:T(8,128)(2,1)} %shard_map.77.own_a) | copy-start | bytes 6291460
  4.9 23.8 %collective-permute-start = (bf16[256,4096]{1,0:T(8,128)(2,1)}, bf16[256,4096]{1,0:T(8,128)(2,1)}, u32[]{:S(2)}, u32[]{:S(2)}) collective-permute-start(bf16[256,4096]{1,0:T(8,128)(2,1)} %shard_map.77.own_a), channel_id=1, source_target_pairs={{0,8},{8,0},{1,9},{9,1},{2,10},{10,2},{3,11},{11,3},{4,12},{12,4},... | collective-permute-start | bytes 6291464 | tf_op jit(solution)/shard_map/ppermute | solution.py:203
  12.5 16.3 %collective-permute-start.1 = (bf16[256,4096]{1,0:T(8,128)(2,1)}, bf16[256,4096]{1,0:T(8,128)(2,1)S(1)}, u32[]{:S(2)}, u32[]{:S(2)}) collective-permute-start(bf16[256,4096]{1,0:T(8,128)(2,1)} %shard_map.78.own_b), channel_id=1, source_target_pairs={{0,8},{8,0},{1,9},{9,1},{2,10},{10,2},{3,11},{11,3},{4,12},{12,4},... | collective-permute-start | bytes 6291464 | tf_op jit(solution)/shard_map/ppermute | solution.py:203
  28.7 62.6 %copy-start.7 = (bf16[32,8,1024]{2,1,0:T(8,128)(2,1)}, bf16[32,8,1024]{2,1,0:T(8,128)(2,1)S(1)}, u32[]{:S(2)}) copy-start(bf16[32,8,1024]{2,1,0:T(8,128)(2,1)S(1)} %all_to_all.21) | copy-start | bytes 1572868
  28.7 46.7 %copy-start.5 = (bf16[256,4096]{1,0:T(8,128)(2,1)}, bf16[256,4096]{1,0:T(8,128)(2,1)S(1)}, u32[]{:S(2)}) copy-start(bf16[256,4096]{1,0:T(8,128)(2,1)S(1)} %collective-permute-done.1.pair_b) | copy-start | bytes 6291460
  28.7 46.7 %collective-permute-start.8 = (bf16[256,4096]{1,0:T(8,128)(2,1)S(1)}, bf16[256,4096]{1,0:T(8,128)(2,1)}, u32[]{:S(2)}, u32[]{:S(2)}) collective-permute-start(bf16[256,4096]{1,0:T(8,128)(2,1)S(1)} %copy-done.4), channel_id=1, source_target_pairs={{0,128},{128,4},{4,132},{132,0},{1,129},{129,5},{5,133},{133,1},{2... | collective-permute-start | bytes 6291464 | tf_op jit(solution)/shard_map/ppermute | solution.py:216
  29.1 46.4 %collective-permute-start.9 = (bf16[256,4096]{1,0:T(8,128)(2,1)}, bf16[256,4096]{1,0:T(8,128)(2,1)}, u32[]{:S(2)}, u32[]{:S(2)}) collective-permute-start(bf16[256,4096]{1,0:T(8,128)(2,1)} %shard_map.78.own_b), channel_id=1, source_target_pairs={{0,132},{128,0},{4,128},{132,4},{1,133},{129,1},{5,129},{133,5},{2... | collective-permute-start | bytes 6291464 | tf_op jit(solution)/shard_map/ppermute | solution.py:216
  31.5 15.6 %collective-permute-start.2 = (bf16[32,8192]{1,0:T(8,128)(2,1)S(1)}, bf16[32,8192]{1,0:T(8,128)(2,1)S(1)}, u32[]{:S(2)}, u32[]{:S(2)}) collective-permute-start(bf16[32,8192]{1,0:T(8,128)(2,1)S(1)} %bitcast.31), channel_id=1, source_target_pairs={{0,16},{16,32},{32,48},{48,64},{64,80},{80,96},{96,112},{112,0},{1... | collective-permute-start | bytes 1572872 | tf_op jit(solution)/shard_map/ppermute | solution.py:208
  33.1 13.9 %collective-permute-start.3 = (bf16[32,8192]{1,0:T(8,128)(2,1)S(1)}, bf16[32,8192]{1,0:T(8,128)(2,1)S(1)}, u32[]{:S(2)}, u32[]{:S(2)}) collective-permute-start(bf16[32,8192]{1,0:T(8,128)(2,1)S(1)} %bitcast.32), channel_id=1, source_target_pairs={{0,112},{16,0},{32,16},{48,32},{64,48},{80,64},{96,80},{112,96},{1... | collective-permute-start | bytes 1572872 | tf_op jit(solution)/shard_map/ppermute | solution.py:208
  47.0 11.9 %copy-start.12 = (bf16[32,8192]{1,0:T(8,128)(2,1)}, bf16[32,8192]{1,0:T(8,128)(2,1)S(1)}, u32[]{:S(2)}) copy-start(bf16[32,8192]{1,0:T(8,128)(2,1)S(1)} %collective-permute-done.2.p1) | copy-start | bytes 1572868
  47.1 28.4 %copy-start.13 = (bf16[32,8192]{1,0:T(8,128)(2,1)}, bf16[32,8192]{1,0:T(8,128)(2,1)S(1)}, u32[]{:S(2)}) copy-start(bf16[32,8192]{1,0:T(8,128)(2,1)S(1)} %collective-permute-done.3.m1) | copy-start | bytes 1572868
  47.1 11.9 %collective-permute-start.4 = (bf16[32,8192]{1,0:T(8,128)(2,1)S(1)}, bf16[32,8192]{1,0:T(8,128)(2,1)S(1)}, u32[]{:S(2)}, u32[]{:S(2)}) collective-permute-start(bf16[32,8192]{1,0:T(8,128)(2,1)S(1)} %collective-permute-done.2.p1), channel_id=1, source_target_pairs={{0,16},{16,32},{32,48},{48,64},{64,80},{80,96},{96,112},{112,0},{1... | collective-permute-start | bytes 1572872 | tf_op jit(solution)/shard_map/ppermute | solution.py:208
  47.1 11.8 %collective-permute-start.5 = (bf16[32,8192]{1,0:T(8,128)(2,1)S(1)}, bf16[32,8192]{1,0:T(8,128)(2,1)S(1)}, u32[]{:S(2)}, u32[]{:S(2)}) collective-permute-start(bf16[32,8192]{1,0:T(8,128)(2,1)S(1)} %collective-permute-done.3.m1), channel_id=1, source_target_pairs={{0,112},{16,0},{32,16},{48,32},{64,48},{80,64},{96,80},{112,96},{1... | collective-permute-start | bytes 1572872 | tf_op jit(solution)/shard_map/ppermute | solution.py:208
  59.0 19.3 %copy-start.14 = (bf16[32,8192]{1,0:T(8,128)(2,1)}, bf16[32,8192]{1,0:T(8,128)(2,1)S(1)}, u32[]{:S(2)}) copy-start(bf16[32,8192]{1,0:T(8,128)(2,1)S(1)} %collective-permute-done.4.p2) | copy-start | bytes 1572868
  59.0 19.3 %copy-start.15 = (bf16[32,8192]{1,0:T(8,128)(2,1)}, bf16[32,8192]{1,0:T(8,128)(2,1)S(1)}, u32[]{:S(2)}) copy-start(bf16[32,8192]{1,0:T(8,128)(2,1)S(1)} %collective-permute-done.5.m2) | copy-start | bytes 1572868
  59.0 11.1 %collective-permute-start.6 = (bf16[32,8192]{1,0:T(8,128)(2,1)S(1)}, bf16[32,8192]{1,0:T(8,128)(2,1)S(1)}, u32[]{:S(2)}, u32[]{:S(2)}) collective-permute-start(bf16[32,8192]{1,0:T(8,128)(2,1)S(1)} %collective-permute-done.4.p2), channel_id=1, source_target_pairs={{0,16},{16,32},{32,48},{48,64},{64,80},{80,96},{96,112},{112,0},{1... | collective-permute-start | bytes 1572872 | tf_op jit(solution)/shard_map/ppermute | solution.py:208
  60.0 10.1 %collective-permute-start.7 = (bf16[32,8192]{1,0:T(8,128)(2,1)S(1)}, bf16[32,8192]{1,0:T(8,128)(2,1)S(1)}, u32[]{:S(2)}, u32[]{:S(2)}) collective-permute-start(bf16[32,8192]{1,0:T(8,128)(2,1)S(1)} %collective-permute-done.5.m2), channel_id=1, source_target_pairs={{0,112},{16,0},{32,16},{48,32},{64,48},{80,64},{96,80},{112,96},{1... | collective-permute-start | bytes 1572872 | tf_op jit(solution)/shard_map/ppermute | solution.py:208
  70.1 21.2 %copy-start.8 = (bf16[32,8192]{1,0:T(8,128)(2,1)}, bf16[32,8192]{1,0:T(8,128)(2,1)S(1)}, u32[]{:S(2)}) copy-start(bf16[32,8192]{1,0:T(8,128)(2,1)S(1)} %collective-permute-done.6.p3) | copy-start | bytes 1572868
  70.1 10.7 %copy-start.9 = (bf16[32,8192]{1,0:T(8,128)(2,1)}, bf16[32,8192]{1,0:T(8,128)(2,1)S(1)}, u32[]{:S(2)}) copy-start(bf16[32,8192]{1,0:T(8,128)(2,1)S(1)} %collective-permute-done.7.m3) | copy-start | bytes 1572868
  75.5 15.8 %collective-permute-start.12 = (bf16[256,4096]{1,0:T(8,128)(2,1)}, bf16[256,4096]{1,0:T(8,128)(2,1)S(1)}, u32[]{:S(2)}, u32[]{:S(2)}) collective-permute-start(bf16[256,4096]{1,0:T(8,128)(2,1)} %collective-permute-done.8.far_a), channel_id=1, source_target_pairs={{0,8},{8,0},{1,9},{9,1},{2,10},{10,2},{3,11},{11,3},{4,12},{12,4},... | collective-permute-start | bytes 6291464 | tf_op jit(solution)/shard_map/ppermute | solution.py:203
  78.3 13.0 %collective-permute-start.13 = (bf16[256,4096]{1,0:T(8,128)(2,1)}, bf16[256,4096]{1,0:T(8,128)(2,1)}, u32[]{:S(2)}, u32[]{:S(2)}) collective-permute-start(bf16[256,4096]{1,0:T(8,128)(2,1)} %collective-permute-done.9.far_b), channel_id=1, source_target_pairs={{0,8},{8,0},{1,9},{9,1},{2,10},{10,2},{3,11},{11,3},{4,12},{12,4},... | collective-permute-start | bytes 6291464 | tf_op jit(solution)/shard_map/ppermute | solution.py:203
  79.1 12.1 %collective-permute-start.10 = (bf16[16,8192]{1,0:T(8,128)(2,1)}, bf16[16,8192]{1,0:T(8,128)(2,1)S(1)}, u32[]{:S(2)}, u32[]{:S(2)}) collective-permute-start(bf16[16,8192]{1,0:T(8,128)(2,1)} %slice.26), channel_id=1, source_target_pairs={{0,16},{16,32},{32,48},{48,64},{64,80},{80,96},{96,112},{112,0},{1... | collective-permute-start | bytes 786440 | tf_op jit(solution)/shard_map/ppermute | solution.py:208
  81.5 9.8 %collective-permute-start.11 = (bf16[16,8192]{1,0:T(8,128)(2,1)}, bf16[16,8192]{1,0:T(8,128)(2,1)}, u32[]{:S(2)}, u32[]{:S(2)}) collective-permute-start(bf16[16,8192]{1,0:T(8,128)(2,1)} %slice.27), channel_id=1, source_target_pairs={{0,112},{16,0},{32,16},{48,32},{64,48},{80,64},{96,80},{112,96},{1... | collective-permute-start | bytes 786440 | tf_op jit(solution)/shard_map/ppermute | solution.py:208
  91.3 1.4 copy-start.6
  139.7 1.2 copy-start.10
  142.5 10.4 %copy-start.16 = (s32[16,8192]{1,0:T(8,128)S(1)}, s32[16,8192]{1,0:T(8,128)}, u32[]{:S(2)}) copy-start(s32[16,8192]{1,0:T(8,128)} %param.9) | copy-start | bytes 1572868
  142.5 10.5 %copy-start.18 = (f32[16]{0:T(128)S(1)}, f32[16]{0:T(128)}, u32[]{:S(2)}) copy-start(f32[16]{0:T(128)} %param.10) | copy-start | bytes 196
  142.5 38.4 %all-to-all-start.2 = ((f32[32,136,128]{2,1,0:T(8,128)}), f32[32,136,128]{2,1,0:T(8,128)S(1)}, u32[]{:S(2)}, u32[]{:S(2)}) async-start(f32[32,136,128]{2,1,0:T(8,128)} %pad_maximum_fusion), calls=%async_computation.2 | async-start | bytes 4456448 | tf_op jit(solution)/shard_map/all_to_all | solution.py:220
  180.9 1.0 copy-start.2
  184.5 19.9 %all-to-all-start.3 = ((f32[256,1,128]{2,1,0:T(1,128)}), f32[256,1,128]{2,1,0:T(1,128)S(1)}, u32[]{:S(2)}, u32[]{:S(2)}) async-start(f32[256,1,128]{2,1,0:T(1,128)} %broadcast_in_dim.9), calls=%async_computation.3 | async-start | bytes 262144 | tf_op jit(solution)/shard_map/all_to_all | solution.py:220
  (3 other events, 2.5 us)

commit v4 on v3

v4 whole, which is shorter than its diff:
```python
import functools

import jax
import jax.numpy as jnp
from jax import lax
from jax.experimental import pallas as pl
from jax.experimental.pallas import tpu as pltpu
from jax.sharding import Mesh, PartitionSpec as P

NS = 8192
AXES = ("xlo", "z", "core", "xhi", "y")
SIZES = (2, 8, 2, 2, 4)
ROW = ("xlo", "z", "core")
COL = ("xhi", "y")
PLANE = ("xlo", "core", "xhi", "y")
LANES = 128
CHUNK = 1024
MIB = 1024 * 1024


def mask_kernel(ham_ref, mask_ref, out_ref):
    rows, cols = ham_ref.shape
    mask_rows, mask_cols = mask_ref.shape
    tile = size = rows // mask_rows
    spread = (
        lax.broadcasted_iota(jnp.int32, (mask_cols, cols), 1) // size + pl.program_id(0) * (cols // size)
        == lax.broadcasted_iota(jnp.int32, (mask_cols, cols), 0)
    ).astype(jnp.bfloat16)
    mask = mask_ref[...].astype(jnp.float32).astype(jnp.bfloat16)
    wide = jnp.dot(mask, spread, preferred_element_type=jnp.float32)
    for index in range(mask_rows):
        at = index * tile
        values = ham_ref[at : at + tile, :].astype(jnp.float32) * wide[index : index + 1, :]
        out_ref[at : at + tile, :] = values.astype(jnp.bfloat16)


def mask_half(ham, tile_mask, half):
    rows, cols = ham.shape
    mask_rows, mask_cols = tile_mask.shape
    return pl.pallas_call(
        mask_kernel,
        grid=(4,),
        in_specs=[
            pl.BlockSpec((rows, cols // 8), lambda j: (0, half * 4 + j)),
            pl.BlockSpec((mask_rows, mask_cols // 2), lambda j: (0, half)),
        ],
        out_specs=pl.BlockSpec((rows, cols // 8), lambda j: (0, j)),
        out_shape=jax.ShapeDtypeStruct((rows, cols // 2), jnp.bfloat16),
        compiler_params=pltpu.CompilerParams(vmem_limit_bytes=8 * MIB),
        cost_estimate=pl.CostEstimate(
            flops=rows * cols, bytes_accessed=2 * rows * cols, transcendentals=0
        ),
    )(ham, tile_mask)


def product_kernel(
    place_ref, c0, p1, p2, p3, m1, m2, m3, top, low,
    own_a, own_b, pair_a, pair_b, far_a, far_b, cross_a, cross_b,
    turn_ref, home_ref, lhs, acc, local,
):
    xlo, z, core = place_ref[0], place_ref[1], place_ref[2]
    strings = c0.shape[1]
    blocks = ((0, c0), (-1, p1), (-2, p2), (-3, p3), (1, m1), (2, m2), (3, m3))
    acc[...] = jnp.zeros_like(acc)

    def gather(at, width, out):
        for offset, ref in blocks:
            row = pl.multiple_of(lax.rem(z + offset + 8, 8) * 32, 32)
            out[pl.ds(row, 32), :] = ref[:, pl.ds(at, width)]
        row = pl.multiple_of(lax.rem(z + 4, 8) * 32, 32)
        out[pl.ds(row, 16), :] = top[:, pl.ds(at, width)]
        out[pl.ds(pl.multiple_of(row + 16, 16), 16), :] = low[:, pl.ds(at, width)]

    for start, panels in (
        (0, (own_a, pair_a, far_a, cross_a)),
        (strings // 2, (own_b, pair_b, far_b, cross_b)),
    ):

        def step(index, carry, start=start, panels=panels):
            at = pl.multiple_of(index * CHUNK, CHUNK)
            gather(pl.multiple_of(start + at, CHUNK), CHUNK, lhs)
            for number, ref in enumerate(panels):
                side = xlo if number < 2 else 1 - xlo
                other = core if number % 2 == 0 else 1 - core
                columns = pl.ds(pl.multiple_of((side * 2 + other) * 256, 256), 256)
                acc[:, columns] += lax.dot_general(
                    lhs[...],
                    ref[:, pl.ds(at, CHUNK)],
                    (((1,), (1,)), ((), ())),
                    preferred_element_type=jnp.float32,
                )
            return carry

        lax.fori_loop(0, strings // 2 // CHUNK, step, 0)

    for side in range(2):
        at = pl.multiple_of(side * (strings // 2) + z * 512, 512)
        gather(at, 512, local.at[:, side * 512 : side * 512 + 512])

    coeff = local[...].astype(jnp.float32)
    projection = jnp.sum(2.0 * coeff * acc[...])
    weight = jnp.sum(coeff * coeff)
    lane = lax.broadcasted_iota(jnp.int32, (8, LANES), 1)
    row = lax.broadcasted_iota(jnp.int32, (8, LANES), 0)
    sums = jnp.where(lane == 0, projection, jnp.where(lane == 1, weight, 0.0))
    sums = jnp.where(row == 0, sums, 0.0)
    for there in range(8):
        for part in range(8):
            turn_ref[there, part * 32 : part * 32 + 32, :] = acc[
                there * 32 : there * 32 + 32, part * LANES : part * LANES + LANES
            ]
        turn_ref[there, 256:264, :] = sums
    for target in range(32):
        quarter, col = target // 8, target % 8
        for part in range(2):
            lanes = quarter * 256 + part * LANES
            for below in range(2):
                at = (2 * (col % 4) + below) * 32 + col // 4 * 16
                home_ref[target, part * 32 + below * 16 : part * 32 + below * 16 + 16, :] = acc[
                    at : at + 16, lanes : lanes + LANES
                ]


def multiply(place, blocks, halves):
    strings = blocks[0].shape[1]
    vmem = pl.BlockSpec(memory_space=pltpu.VMEM)
    return pl.pallas_call(
        product_kernel,
        in_specs=[pl.BlockSpec(memory_space=pltpu.SMEM)] + [vmem] * (len(blocks) + len(halves)),
        out_specs=[vmem, vmem],
        scratch_shapes=[
            pltpu.VMEM((256, CHUNK), jnp.bfloat16),
            pltpu.VMEM((256, 1024), jnp.float32),
            pltpu.VMEM((256, 1024), jnp.bfloat16),
        ],
        out_shape=[
            jax.ShapeDtypeStruct((8, 264, LANES), jnp.float32),
            jax.ShapeDtypeStruct((32, 64, LANES), jnp.float32),
        ],
        compiler_params=pltpu.CompilerParams(vmem_limit_bytes=30 * MIB),
        cost_estimate=pl.CostEstimate(
            flops=2 * 256 * 1024 * strings, bytes_accessed=24 * MIB, transcendentals=0
        ),
    )(place, *blocks, *halves)


def split_kernel(value_ref, out_ref, start):
    out_ref[...] = value_ref[start : start + out_ref.shape[0], :]


def take_rows(value, start):
    rows, cols = value.shape
    return pl.pallas_call(
        functools.partial(split_kernel, start=start),
        out_shape=jax.ShapeDtypeStruct((rows // 2, cols), value.dtype),
        compiler_params=pltpu.CompilerParams(vmem_limit_bytes=3 * MIB),
    )(value)


def pack_kernel(turn_ref, home_ref, out_ref):
    sums = jnp.sum(turn_ref[:, 256:264, :], axis=0)
    for target in range(32):
        row, col = target // 8, target % 8
        out_ref[target, 0:64, :] = home_ref[target, :, :]
        for part in range(8):
            source = ((col // 4) * 4 + part % 4) * 32 + row * 8
            out_ref[target, 64 + part * 8 : 72 + part * 8, :] = turn_ref[
                2 * (col % 4) + part // 4, source : source + 8, :
            ]
        out_ref[target, 128:136, :] = sums


def pack(turn, home):
    return pl.pallas_call(
        pack_kernel,
        out_shape=jax.ShapeDtypeStruct((32, 136, LANES), jnp.float32),
        compiler_params=pltpu.CompilerParams(vmem_limit_bytes=16 * MIB),
        cost_estimate=pl.CostEstimate(flops=0, bytes_accessed=5 * MIB, transcendentals=0),
    )(turn, home)


def finish_kernel(update_ref, totals_ref, own_ref, out_ref, stats_ref):
    totals = jnp.sum(totals_ref[...], axis=0, keepdims=True) * (1.0 / (NS * NS))
    lane = lax.broadcasted_iota(jnp.int32, (1, LANES), 1)
    spread = jnp.sum(jnp.where(lane == 0, totals, 0.0), axis=1, keepdims=True)
    out_ref[...] = update_ref[...] * lax.rsqrt(spread + 1e-06)
    stats_ref[...] = jnp.where(lane == 0, own_ref[0:1, :], jnp.sqrt(totals))


def finish(update, totals, own):
    return pl.pallas_call(
        finish_kernel,
        out_shape=[
            jax.ShapeDtypeStruct(update.shape, jnp.float32),
            jax.ShapeDtypeStruct((1, LANES), jnp.float32),
        ],
        compiler_params=pltpu.CompilerParams(vmem_limit_bytes=16 * MIB),
        cost_estimate=pl.CostEstimate(flops=update.size, bytes_accessed=2 * MIB, transcendentals=0),
    )(update, totals, own)


def update_kernel(tiles_ref, coeff_ref, diag_ref, update_ref, sums_ref, theta_ref):
    totals = jnp.sum(tiles_ref[:, 128:136, :], axis=0)
    lane = lax.broadcasted_iota(jnp.int32, (8, LANES), 1)
    projection = jnp.sum(jnp.where(lane == 0, totals, 0.0))
    weight = jnp.sum(jnp.where(lane == 1, totals, 0.0))
    theta = jnp.full((1, 1), projection) / jnp.full((1, 1), weight)
    squares = jnp.zeros((8, LANES), jnp.float32)
    spread = jnp.zeros((8, LANES), jnp.float32)
    for part in range(2):
        rows = slice(part * LANES, part * LANES + LANES)
        for index in range(8):
            cols = slice(index * LANES, index * LANES + LANES)
            quarter, group = index // 2, index % 2
            at = part * 32 + quarter * 8
            straight = tiles_ref[group * 16 : group * 16 + 16, at : at + 8, :]
            straight = straight.reshape(LANES, LANES).T
            turned = tiles_ref[part * 16 : part * 16 + 16, 64 + index * 8 : 72 + index * 8, :]
            turned = turned.reshape(LANES, LANES)
            coeff = coeff_ref[rows, cols].astype(jnp.float32)
            residual = straight + turned - theta * coeff
            update = residual / jnp.maximum(jnp.abs(diag_ref[rows, cols] - theta), 1.0)
            update_ref[rows, cols] = update
            squares += jnp.sum((residual * residual).reshape(16, 8, LANES), axis=0)
            spread += jnp.sum((update * update).reshape(16, 8, LANES), axis=0)
    theta_ref[...] = jnp.broadcast_to(theta, theta_ref.shape)
    values = jnp.where(lane == 0, jnp.sum(spread), jnp.where(lane == 1, jnp.sum(squares), 0.0))
    sums_ref[...] = jnp.broadcast_to(values[0:1, :], sums_ref.shape)


def make_update(tiles, coeff, diagonal):
    return pl.pallas_call(
        update_kernel,
        out_shape=[
            jax.ShapeDtypeStruct(coeff.shape, jnp.float32),
            jax.ShapeDtypeStruct((256, LANES), jnp.float32),
            jax.ShapeDtypeStruct((8, LANES), jnp.float32),
        ],
        compiler_params=pltpu.CompilerParams(vmem_limit_bytes=16 * MIB),
        cost_estimate=pl.CostEstimate(
            flops=10 * coeff.size, bytes_accessed=5 * MIB, transcendentals=0
        ),
    )(tiles, coeff, diagonal)


def swap(value):
    return lax.ppermute(value, "core", [(0, 1), (1, 0)])


def shift(value, step):
    count = lax.axis_size("z")
    return lax.ppermute(value, "z", [(i, (i + step) % count) for i in range(count)])


def shift_x(value, step):
    def index(x):
        return x % 2 * 2 + x // 2

    pairs = [(index(x), index((x + step) % 4)) for x in range(4)]
    return lax.ppermute(value, ("xlo", "xhi"), pairs)


def exchange(value, axes):
    return lax.all_to_all(value, axes, split_axis=0, concat_axis=0, tiled=True)


def body(ham, coeff, tile_mask, occupation, orbital_energy, coulomb):
    rows, strings = ham.shape
    cols = coeff.shape[1]
    core = lax.axis_index("core")
    xlo = lax.axis_index("xlo")
    z = lax.axis_index("z")
    row_index = (xlo * 8 + z) * 2 + core
    col_index = lax.axis_index("xhi") * 4 + lax.axis_index("y")

    place = jnp.stack([xlo, z, core]).astype(jnp.int32)
    ham, place = lax.optimization_barrier((ham, place))
    pair, pair_mask = swap(ham), swap(tile_mask)
    own_a, own_b = mask_half(ham, tile_mask, 0), mask_half(ham, tile_mask, 1)
    pair_a, pair_b = mask_half(pair, pair_mask, 0), mask_half(pair, pair_mask, 1)

    block = exchange(coeff.reshape(32, 8, cols), PLANE)
    block = block.reshape(4, 8, 8, cols).transpose(0, 2, 1, 3).reshape(32, strings)
    block, own_a, own_b, pair_a, pair_b = lax.optimization_barrier(
        (block, own_a, own_b, pair_a, pair_b)
    )
    far_a, far_b = shift_x(own_a, 1), shift_x(own_b, -1)
    p1, m1 = lax.optimization_barrier((shift(block, 1), shift(block, -1)))
    p2, m2 = lax.optimization_barrier((shift(p1, 1), shift(m1, -1)))
    p3, m3, far_a, far_b = lax.optimization_barrier((shift(p2, 1), shift(m2, -1), far_a, far_b))
    cross_a, cross_b = swap(far_a), swap(far_b)
    top, low = shift(take_rows(p3, 0), 1), shift(take_rows(m3, 16), -1)

    turn, home = multiply(
        place,
        (block, p1, p2, p3, m1, m2, m3, top, low),
        (own_a, own_b, pair_a, pair_b, far_a, far_b, cross_a, cross_b),
    )

    tiles = exchange(pack(exchange(turn, "z"), home), PLANE)

    occ_float = occupation.astype(jnp.float32)
    occ_alpha = lax.dynamic_slice_in_dim(occ_float, row_index * rows, rows, 1)
    occ_beta = lax.dynamic_slice_in_dim(occ_float, col_index * cols, cols, 1)
    energy_alpha = jnp.dot(orbital_energy, occ_alpha, precision=lax.Precision.HIGHEST)
    energy_beta = jnp.dot(orbital_energy, occ_beta, precision=lax.Precision.HIGHEST)
    coupling = jnp.dot(
        jnp.dot(occ_alpha.T, coulomb, precision=lax.Precision.HIGHEST),
        occ_beta,
        precision=lax.Precision.HIGHEST,
    )
    diagonal = energy_alpha[:, None] + energy_beta[None, :] + coupling

    update, sums, theta = make_update(tiles, coeff, diagonal)
    correction, stats = finish(update, exchange(sums, AXES), theta)
    return (correction, stats[0, :2])


def solution(mesh):
    fine = Mesh(mesh.devices.reshape(SIZES), AXES)
    in_specs = (P(ROW, None), P(ROW, COL), P(ROW, None), P(), P(), P())
    out_specs = (P(ROW, COL), P())
    return jax.shard_map(body, mesh=fine, in_specs=in_specs, out_specs=out_specs, check_vma=False)
```

time: 211 us -> 196 us (0.929)
  waiting for transfers between devices: 75.4 us -> 66.1 us
  other arithmetic: 5.78 us -> 0.11 us
  local copies, waits for them, and re-layouts: 8.21 us -> 13.4 us
  Pallas kernels: 24.2 us -> 19.9 us
  blocking collectives: 48.3 us -> 50.9 us
  starting transfers between devices: 43.3 us -> 41.1 us
    all_to_all x2, waiting for transfers between devices: 37.4 us -> 25.4 us  [exchange(): return lax.all_to_all(value, axes, split_axis=0, concat_axis=0, tiled=True)]
    unnamed x38 -> x28, local copies, waits for them, and re-layouts: 4.63 us -> 12.9 us
    ppermute x8, waiting for transfers between devices: 32.7 us -> 37.8 us  [shift(): lax.ppermute(value, 'z', [(i, (i + step) % count) for i in range(count)])]
    pallas_call x1 -> x5, Pallas kernels: 14.9 us -> 10.3 us  [the longest x1 7.54 us: multiply(): pl.pallas_call(product_kernel, in_specs=[pl.BlockSpec(memory_space=pltpu....]
    slice x6 -> x0, local copies, waits for them, and re-layouts: 2.72 us -> none  [the longest x2 1.45 us: body(): top, low = (shift(p3[:16], 1), shift(m3[16:], -1))]
    all_to_all x2, blocking collectives: 48.3 us -> 50.9 us  [exchange(): return lax.all_to_all(value, axes, split_axis=0, concat_axis=0, tiled=True)]
    ppermute x2, waiting for transfers between devices: 5.37 us -> 2.96 us  [shift_x(): return lax.ppermute(value, ('xlo', 'xhi'), pairs)]
    mul x1 -> x0, other arithmetic: 2.3 us -> none  [body(): correction = update * lax.rsqrt(totals[1] / (NS * NS) + 1e-06)]
  transfers between devices with their start and end apart: 16 -> 16, of which waited for: 7 -> 7; matrix products, arithmetic and copies ran while one was open for 2% -> 1% of each run, Pallas kernels for 2% -> 5%
where the time goes in v4:
time: 196 us; the launch traced here: 195 us
  waiting for transfers between devices  66.1 us (34%)
  blocking collectives  50.9 us (26%)
  starting transfers between devices  41.1 us (21%)
  Pallas kernels  19.9 us (10%)
  local copies, waits for them, and re-layouts  13.4 us (7%)
  matrix products  2.52 us (1%)
    all_to_all x2, blocking collectives, exchange(): return lax.all_to_all(value, axes, split_axis=0, concat_axis=0, tiled=True)  50.9 us
    ppermute x8, waiting for transfers between devices, shift(): lax.ppermute(value, 'z', [(i, (i + step) % count) for i in range(count)])  37.8 us
    all_to_all x2, waiting for transfers between devices, exchange(): return lax.all_to_all(value, axes, split_axis=0, concat_axis=0, tiled=True)  25.4 us
    ppermute x8, starting transfers between devices, shift(): lax.ppermute(value, 'z', [(i, (i + step) % count) for i in range(count)])  16.9 us
    all_to_all x2, starting transfers between devices, exchange(): return lax.all_to_all(value, axes, split_axis=0, concat_axis=0, tiled=True)  16.6 us
    unnamed x28, local copies, waits for them, and re-layouts  12.9 us
    pallas_call x4, Pallas kernels, mask_half(): pl.pallas_call(mask_kernel, grid=(4,), in_specs=[pl.BlockSpec((rows, cols...  8.86 us
    pallas_call x1, Pallas kernels, multiply(): pl.pallas_call(product_kernel, in_specs=[pl.BlockSpec(memory_space=pltpu....  7.54 us
  transfers between devices with their start and end apart: 16, of which 7 were waited for; matrix products, arithmetic and copies ran while one was open for 1% of the time, Pallas kernels for 5%

profile of v4, /device:TPU:1, one launch (start us, length us, event | category | flops | bytes accessed | tf_op | source)
XLA Modules:
  0.0 194.9 jit_solution(17268986542746893971)
XLA Ops:
  0.7 3.3 %collective-permute-start = (bf16[256,8192]{1,0:T(8,128)(2,1)}, bf16[256,8192]{1,0:T(8,128)(2,1)}, u32[]{:S(2)}, u32[]{:S(2)}) collective-permute-start(bf16[256,8192]{1,0:T(8,128)(2,1)} %ham_ref.1), channel_id=1, source_target_pairs={{0,8},{8,0},{1,9},{9,1},{2,10},{10,2},{3,11},{11,3},{4,12},{12,4},... | collective-permute-start | bytes 12582920 | tf_op jit(solution)/shard_map/ppermute | solution.py:247
  4.0 5.5 %all-to-all-start = ((bf16[32,8,1024]{2,1,0:T(8,128)(2,1)}), bf16[32,8,1024]{2,1,0:T(8,128)(2,1)S(1)}, u32[]{:S(2)}, u32[]{:S(2)}) async-start(bf16[32,8,1024]{2,1,0:T(8,128)(2,1)} %bitcast.28), calls=%async_computation | async-start | bytes 1048576 | tf_op jit(solution)/shard_map/all_to_all | solution.py:264
  9.8 2.2 %copy-done.1 = bf16[256,8192]{1,0:T(8,128)(2,1)S(1)} copy-done((bf16[256,8192]{1,0:T(8,128)(2,1)S(1)}, bf16[256,8192]{1,0:T(8,128)(2,1)}, u32[]{:S(2)}) %copy-start.1) | copy-done | bytes 4194328
  12.7 1.4 shard_map.77.own_a
  14.1 1.4 shard_map.78.own_b
  15.5 1.4 copy-done.2
  16.9 3.0 %shard_map.79.pair_a = bf16[256,4096]{1,0:T(8,128)(2,1)S(1)} custom-call(bf16[256,8192]{1,0:T(8,128)(2,1)} %collective-permute-done.ham_ref, s32[8,256]{1,0:T(8,128)S(1)} %collective-permute-done.1.mask_ref), custom_call_target="tpu_custom_call" | custom-call | flops 2097152 | bytes 4194304 | tf_op jit(solution)/shard_map/pallas_call | solution.py:40
  19.9 1.4 copy-done.4
  21.3 3.0 %shard_map.80.pair_b = bf16[256,4096]{1,0:T(8,128)(2,1)S(1)} custom-call(bf16[256,8192]{1,0:T(8,128)(2,1)} %collective-permute-done.ham_ref, s32[8,256]{1,0:T(8,128)S(1)} %collective-permute-done.1.mask_ref), custom_call_target="tpu_custom_call" | custom-call | flops 2097152 | bytes 4194304 | tf_op jit(solution)/shard_map/pallas_call | solution.py:40
  24.4 1.3 copy-done.6
  25.7 1.5 collective-permute-start.8
  28.5 1.6 collective-permute-start.2
  30.1 3.9 %collective-permute-start.3 = (bf16[32,8192]{1,0:T(8,128)(2,1)S(1)}, bf16[32,8192]{1,0:T(8,128)(2,1)S(1)}, u32[]{:S(2)}, u32[]{:S(2)}) collective-permute-start(bf16[32,8192]{1,0:T(8,128)(2,1)S(1)} %bitcast.26), channel_id=1, source_target_pairs={{0,112},{16,0},{32,16},{48,32},{64,48},{80,64},{96,80},{112,96},{1... | collective-permute-start | bytes 1572872 | tf_op jit(solution)/shard_map/ppermute | solution.py:252
  34.0 11.5 %collective-permute-done.2.p1 = bf16[32,8192]{1,0:T(8,128)(2,1)S(1)} collective-permute-done((bf16[32,8192]{1,0:T(8,128)(2,1)S(1)}, bf16[32,8192]{1,0:T(8,128)(2,1)S(1)}, u32[]{:S(2)}, u32[]{:S(2)}) %collective-permute-start.2) | collective-permute-done | bytes 524320 | tf_op jit(solution)/shard_map/ppermute | solution.py:252
  45.6 2.7 %collective-permute-start.5 = (bf16[32,8192]{1,0:T(8,128)(2,1)S(1)}, bf16[32,8192]{1,0:T(8,128)(2,1)S(1)}, u32[]{:S(2)}, u32[]{:S(2)}) collective-permute-start(bf16[32,8192]{1,0:T(8,128)(2,1)S(1)} %collective-permute-done.3.m1), channel_id=1, source_target_pairs={{0,112},{16,0},{32,16},{48,32},{64,48},{80,64},{96,80},{112,96},{1... | collective-permute-start | bytes 1572872 | tf_op jit(solution)/shard_map/ppermute | solution.py:252
  48.3 10.6 %collective-permute-done.4.p2 = bf16[32,8192]{1,0:T(8,128)(2,1)S(1)} collective-permute-done((bf16[32,8192]{1,0:T(8,128)(2,1)S(1)}, bf16[32,8192]{1,0:T(8,128)(2,1)S(1)}, u32[]{:S(2)}, u32[]{:S(2)}) %collective-permute-start.4) | collective-permute-done | bytes 524320 | tf_op jit(solution)/shard_map/ppermute | solution.py:252
  59.8 1.8 collective-permute-start.7
  61.5 9.7 %collective-permute-done.6.value_ref.p3 = bf16[32,8192]{1,0:T(8,128)(2,1)S(1)} collective-permute-done((bf16[32,8192]{1,0:T(8,128)(2,1)S(1)}, bf16[32,8192]{1,0:T(8,128)(2,1)S(1)}, u32[]{:S(2)}, u32[]{:S(2)}) %collective-permute-start.6) | collective-permute-done | bytes 524320 | tf_op jit(solution)/shard_map/ppermute | solution.py:252
  71.2 2.8 %collective-permute-done.8.far_a = bf16[256,4096]{1,0:T(8,128)(2,1)S(1)} collective-permute-done((bf16[256,4096]{1,0:T(8,128)(2,1)S(1)}, bf16[256,4096]{1,0:T(8,128)(2,1)S(1)}, u32[]{:S(2)}, u32[]{:S(2)}) %collective-permute-start.8) | collective-permute-done | bytes 2097184 | tf_op jit(solution)/shard_map/ppermute | solution.py:260
  75.5 1.7 collective-permute-start.10
  77.3 4.2 %collective-permute-start.11 = (bf16[16,8192]{1,0:T(8,128)(2,1)S(1)}, bf16[16,8192]{1,0:T(8,128)(2,1)S(1)}, u32[]{:S(2)}, u32[]{:S(2)}) collective-permute-start(bf16[16,8192]{1,0:T(8,128)(2,1)S(1)} %shard_map.82), channel_id=1, source_target_pairs={{0,112},{16,0},{32,16},{48,32},{64,48},{80,64},{96,80},{112,96},{1... | collective-permute-start | bytes 786440 | tf_op jit(solution)/shard_map/ppermute | solution.py:252
  81.5 5.9 %collective-permute-done.10.top = bf16[16,8192]{1,0:T(8,128)(2,1)S(1)} collective-permute-done((bf16[16,8192]{1,0:T(8,128)(2,1)S(1)}, bf16[16,8192]{1,0:T(8,128)(2,1)S(1)}, u32[]{:S(2)}, u32[]{:S(2)}) %collective-permute-start.10) | collective-permute-done | bytes 262176 | tf_op jit(solution)/shard_map/ppermute | solution.py:252
  87.4 1.6 copy-done.3
  89.0 1.6 copy-done.5
  90.6 1.6 copy-done.7
  92.2 7.5 %shard_map.83 = (f32[8,264,128]{2,1,0:T(8,128)S(1)}, f32[32,64,128]{2,1,0:T(8,128)S(1)}) custom-call(s32[3]{0:T(128)S(1)} %pad_add_fusion.place_ref, bf16[32,8192]{1,0:T(8,128)(2,1)S(1)} %bitcast.27, bf16[32,8192]{1,0:T(8,128)(2,1)S(1)} %collective-permute-done.2.p1, bf16[32,8192]{1,0:T(8,128)(2,1)S(1)} %collective-permute-done.4.p2, ...), custom_call_target="tpu_custom_call" | custom-call | flops 4294967296 | bytes 25165824 | tf_op jit(solution)/shard_map/pallas_call | solution.py:127
  99.7 31.2 %all_to_all.26.turn_ref = f32[8,264,128]{2,1,0:T(8,128)S(1)} all-to-all(f32[8,264,128]{2,1,0:T(8,128)S(1)} %get-tuple-element.39), channel_id=1, replica_groups=mesh['xlo'=2,'z'=8,'core'=2,'xhi'=2,'y'=4] {'z'}, dimensions={0} | all-to-all | bytes 2162688 | tf_op jit(solution)/shard_map/all_to_all | solution.py:264
  130.9 1.6 shard_map.84
  132.5 11.1 %all-to-all-start.2 = ((f32[32,136,128]{2,1,0:T(8,128)}), f32[32,136,128]{2,1,0:T(8,128)S(1)}, u32[]{:S(2)}, u32[]{:S(2)}) async-start(f32[32,136,128]{2,1,0:T(8,128)} %shard_map.84), calls=%async_computation.2 | async-start | bytes 4456448 | tf_op jit(solution)/shard_map/all_to_all | solution.py:264
  144.5 1.8 convolution_add_fusion.diag_ref
  146.3 25.4 %all-to-all-done.2.tiles_ref = f32[32,136,128]{2,1,0:T(8,128)S(1)} async-done(((f32[32,136,128]{2,1,0:T(8,128)}), f32[32,136,128]{2,1,0:T(8,128)S(1)}, u32[]{:S(2)}, u32[]{:S(2)}) %all-to-all-start.2) | async-done | bytes 2228256 | tf_op jit(solution)/shard_map/all_to_all | solution.py:264
  173.5 19.7 %all_to_all.27 = f32[256,1,128]{2,1,0:T(1,128)S(1)} all-to-all(f32[256,1,128]{2,1,0:T(1,128)S(1)} %bitcast.30), channel_id=1, replica_groups=mesh['xlo'=2,'z'=8,'core'=2,'xhi'=2,'y'=4] {'xlo','z','core','xhi','y'}, dimensions={0} | all-to-all | bytes 262144 | tf_op jit(solution)/shard_map/all_to_all | solution.py:264
  (47 shorter events, 9.1 us)
Async XLA Ops:
  0.6 143.4 %copy-start = (f32[16,16]{1,0:T(8,128)S(1)}, f32[16,16]{1,0:T(8,128)}, u32[]{:S(2)}) copy-start(f32[16,16]{1,0:T(8,128)} %param.11) | copy-start | bytes 3076
  0.7 16.1 %collective-permute-start = (bf16[256,8192]{1,0:T(8,128)(2,1)}, bf16[256,8192]{1,0:T(8,128)(2,1)}, u32[]{:S(2)}, u32[]{:S(2)}) collective-permute-start(bf16[256,8192]{1,0:T(8,128)(2,1)} %ham_ref.1), channel_id=1, source_target_pairs={{0,8},{8,0},{1,9},{9,1},{2,10},{10,2},{3,11},{11,3},{4,12},{12,4},... | collective-permute-start | bytes 12582920 | tf_op jit(solution)/shard_map/ppermute | solution.py:247
  4.0 21.7 %all-to-all-start = ((bf16[32,8,1024]{2,1,0:T(8,128)(2,1)}), bf16[32,8,1024]{2,1,0:T(8,128)(2,1)S(1)}, u32[]{:S(2)}, u32[]{:S(2)}) async-start(bf16[32,8,1024]{2,1,0:T(8,128)(2,1)} %bitcast.28), calls=%async_computation | async-start | bytes 1048576 | tf_op jit(solution)/shard_map/all_to_all | solution.py:264
  9.5 7.4 %collective-permute-start.1 = (s32[8,256]{1,0:T(8,128)}, s32[8,256]{1,0:T(8,128)S(1)}, u32[]{:S(2)}, u32[]{:S(2)}) collective-permute-start(s32[8,256]{1,0:T(8,128)} %mask_ref.3), channel_id=1, source_target_pairs={{0,8},{8,0},{1,9},{9,1},{2,10},{10,2},{3,11},{11,3},{4,12},{12,4},... | collective-permute-start | bytes 24584 | tf_op jit(solution)/shard_map/ppermute | solution.py:247
  9.8 2.2 %copy-start.1 = (bf16[256,8192]{1,0:T(8,128)(2,1)S(1)}, bf16[256,8192]{1,0:T(8,128)(2,1)}, u32[]{:S(2)}) copy-start(bf16[256,8192]{1,0:T(8,128)(2,1)} %ham_ref.1) | copy-start | bytes 12582916
  12.0 0.7 copy-start.9
  12.7 1.4 copy-start.10
  15.5 1.4 copy-start.2
  19.9 1.4 copy-start.4
  24.4 1.4 copy-start.6
  25.7 48.3 %collective-permute-start.8 = (bf16[256,4096]{1,0:T(8,128)(2,1)S(1)}, bf16[256,4096]{1,0:T(8,128)(2,1)S(1)}, u32[]{:S(2)}, u32[]{:S(2)}) collective-permute-start(bf16[256,4096]{1,0:T(8,128)(2,1)S(1)} %shard_map.77.own_a), channel_id=1, source_target_pairs={{0,128},{128,4},{4,132},{132,0},{1,129},{129,5},{5,133},{133,1},{2... | collective-permute-start | bytes 6291464 | tf_op jit(solution)/shard_map/ppermute | solution.py:260
  27.2 47.0 %collective-permute-start.9 = (bf16[256,4096]{1,0:T(8,128)(2,1)}, bf16[256,4096]{1,0:T(8,128)(2,1)S(1)}, u32[]{:S(2)}, u32[]{:S(2)}) collective-permute-start(bf16[256,4096]{1,0:T(8,128)(2,1)} %copy-done.2), channel_id=1, source_target_pairs={{0,132},{128,0},{4,128},{132,4},{1,133},{129,1},{5,129},{133,5},{2... | collective-permute-start | bytes 6291464 | tf_op jit(solution)/shard_map/ppermute | solution.py:260
  28.5 17.1 %collective-permute-start.2 = (bf16[32,8192]{1,0:T(8,128)(2,1)S(1)}, bf16[32,8192]{1,0:T(8,128)(2,1)S(1)}, u32[]{:S(2)}, u32[]{:S(2)}) collective-permute-start(bf16[32,8192]{1,0:T(8,128)(2,1)S(1)} %bitcast.25), channel_id=1, source_target_pairs={{0,16},{16,32},{32,48},{48,64},{64,80},{80,96},{96,112},{112,0},{1... | collective-permute-start | bytes 1572872 | tf_op jit(solution)/shard_map/ppermute | solution.py:252
  30.1 15.5 %collective-permute-start.3 = (bf16[32,8192]{1,0:T(8,128)(2,1)S(1)}, bf16[32,8192]{1,0:T(8,128)(2,1)S(1)}, u32[]{:S(2)}, u32[]{:S(2)}) collective-permute-start(bf16[32,8192]{1,0:T(8,128)(2,1)S(1)} %bitcast.26), channel_id=1, source_target_pairs={{0,112},{16,0},{32,16},{48,32},{64,48},{80,64},{96,80},{112,96},{1... | collective-permute-start | bytes 1572872 | tf_op jit(solution)/shard_map/ppermute | solution.py:252
  45.6 13.3 %collective-permute-start.4 = (bf16[32,8192]{1,0:T(8,128)(2,1)S(1)}, bf16[32,8192]{1,0:T(8,128)(2,1)S(1)}, u32[]{:S(2)}, u32[]{:S(2)}) collective-permute-start(bf16[32,8192]{1,0:T(8,128)(2,1)S(1)} %collective-permute-done.2.p1), channel_id=1, source_target_pairs={{0,16},{16,32},{32,48},{48,64},{64,80},{80,96},{96,112},{112,0},{1... | collective-permute-start | bytes 1572872 | tf_op jit(solution)/shard_map/ppermute | solution.py:252
  45.6 13.3 %collective-permute-start.5 = (bf16[32,8192]{1,0:T(8,128)(2,1)S(1)}, bf16[32,8192]{1,0:T(8,128)(2,1)S(1)}, u32[]{:S(2)}, u32[]{:S(2)}) collective-permute-start(bf16[32,8192]{1,0:T(8,128)(2,1)S(1)} %collective-permute-done.3.m1), channel_id=1, source_target_pairs={{0,112},{16,0},{32,16},{48,32},{64,48},{80,64},{96,80},{112,96},{1... | collective-permute-start | bytes 1572872 | tf_op jit(solution)/shard_map/ppermute | solution.py:252
  58.9 12.4 %collective-permute-start.6 = (bf16[32,8192]{1,0:T(8,128)(2,1)S(1)}, bf16[32,8192]{1,0:T(8,128)(2,1)S(1)}, u32[]{:S(2)}, u32[]{:S(2)}) collective-permute-start(bf16[32,8192]{1,0:T(8,128)(2,1)S(1)} %collective-permute-done.4.p2), channel_id=1, source_target_pairs={{0,16},{16,32},{32,48},{48,64},{64,80},{80,96},{96,112},{112,0},{1... | collective-permute-start | bytes 1572872 | tf_op jit(solution)/shard_map/ppermute | solution.py:252
  59.8 11.5 %collective-permute-start.7 = (bf16[32,8192]{1,0:T(8,128)(2,1)S(1)}, bf16[32,8192]{1,0:T(8,128)(2,1)S(1)}, u32[]{:S(2)}, u32[]{:S(2)}) collective-permute-start(bf16[32,8192]{1,0:T(8,128)(2,1)S(1)} %collective-permute-done.5.m2), channel_id=1, source_target_pairs={{0,112},{16,0},{32,16},{48,32},{64,48},{80,64},{96,80},{112,96},{1... | collective-permute-start | bytes 1572872 | tf_op jit(solution)/shard_map/ppermute | solution.py:252
  74.2 13.2 %collective-permute-start.12 = (bf16[256,4096]{1,0:T(8,128)(2,1)S(1)}, bf16[256,4096]{1,0:T(8,128)(2,1)S(1)}, u32[]{:S(2)}, u32[]{:S(2)}) collective-permute-start(bf16[256,4096]{1,0:T(8,128)(2,1)S(1)} %collective-permute-done.8.far_a), channel_id=1, source_target_pairs={{0,8},{8,0},{1,9},{9,1},{2,10},{10,2},{3,11},{11,3},{4,12},{12,4},... | collective-permute-start | bytes 6291464 | tf_op jit(solution)/shard_map/ppermute | solution.py:247
  75.5 11.9 %collective-permute-start.13 = (bf16[256,4096]{1,0:T(8,128)(2,1)S(1)}, bf16[256,4096]{1,0:T(8,128)(2,1)S(1)}, u32[]{:S(2)}, u32[]{:S(2)}) collective-permute-start(bf16[256,4096]{1,0:T(8,128)(2,1)S(1)} %collective-permute-done.9.far_b), channel_id=1, source_target_pairs={{0,8},{8,0},{1,9},{9,1},{2,10},{10,2},{3,11},{11,3},{4,12},{12,4},... | collective-permute-start | bytes 6291464 | tf_op jit(solution)/shard_map/ppermute | solution.py:247
  75.5 11.9 %collective-permute-start.10 = (bf16[16,8192]{1,0:T(8,128)(2,1)S(1)}, bf16[16,8192]{1,0:T(8,128)(2,1)S(1)}, u32[]{:S(2)}, u32[]{:S(2)}) collective-permute-start(bf16[16,8192]{1,0:T(8,128)(2,1)S(1)} %shard_map.81), channel_id=1, source_target_pairs={{0,16},{16,32},{32,48},{48,64},{64,80},{80,96},{96,112},{112,0},{1... | collective-permute-start | bytes 786440 | tf_op jit(solution)/shard_map/ppermute | solution.py:252
  77.3 10.1 %collective-permute-start.11 = (bf16[16,8192]{1,0:T(8,128)(2,1)S(1)}, bf16[16,8192]{1,0:T(8,128)(2,1)S(1)}, u32[]{:S(2)}, u32[]{:S(2)}) collective-permute-start(bf16[16,8192]{1,0:T(8,128)(2,1)S(1)} %shard_map.82), channel_id=1, source_target_pairs={{0,112},{16,0},{32,16},{48,32},{64,48},{80,64},{96,80},{112,96},{1... | collective-permute-start | bytes 786440 | tf_op jit(solution)/shard_map/ppermute | solution.py:252
  87.4 1.6 copy-start.3
  89.0 1.6 copy-start.5
  90.6 1.6 copy-start.7
  132.5 11.1 %copy-start.12 = (s32[16,8192]{1,0:T(8,128)S(1)}, s32[16,8192]{1,0:T(8,128)}, u32[]{:S(2)}) copy-start(s32[16,8192]{1,0:T(8,128)} %param.9) | copy-start | bytes 1572868
  132.5 11.2 %copy-start.13 = (f32[16]{0:T(128)S(1)}, f32[16]{0:T(128)}, u32[]{:S(2)}) copy-start(f32[16]{0:T(128)} %param.10) | copy-start | bytes 196
  132.5 39.2 %all-to-all-start.2 = ((f32[32,136,128]{2,1,0:T(8,128)}), f32[32,136,128]{2,1,0:T(8,128)S(1)}, u32[]{:S(2)}, u32[]{:S(2)}) async-start(f32[32,136,128]{2,1,0:T(8,128)} %shard_map.84), calls=%async_computation.2 | async-start | bytes 4456448 | tf_op jit(solution)/shard_map/all_to_all | solution.py:264
  143.7 0.8 copy-start.11
  171.7 1.0 copy-start.8

commit v5 on v4

--- a/solution.py
+++ b/solution.py
@@ -277,19 +277,25 @@
     ham, place = lax.optimization_barrier((ham, place))
     pair, pair_mask = swap(ham), swap(tile_mask)
     own_a, own_b = mask_half(ham, tile_mask, 0), mask_half(ham, tile_mask, 1)
-    pair_a, pair_b = mask_half(pair, pair_mask, 0), mask_half(pair, pair_mask, 1)
 
     block = exchange(coeff.reshape(32, 8, cols), PLANE)
     block = block.reshape(4, 8, 8, cols).transpose(0, 2, 1, 3).reshape(32, strings)
-    block, own_a, own_b, pair_a, pair_b = lax.optimization_barrier(
-        (block, own_a, own_b, pair_a, pair_b)
+    block, own_a, own_b, pair, pair_mask = lax.optimization_barrier(
+        (block, own_a, own_b, pair, pair_mask)
     )
     far_a, far_b = shift_x(own_a, 1), shift_x(own_b, -1)
-    p1, m1 = lax.optimization_barrier((shift(block, 1), shift(block, -1)))
-    p2, m2 = lax.optimization_barrier((shift(p1, 1), shift(m1, -1)))
-    p3, m3, far_a, far_b = lax.optimization_barrier((shift(p2, 1), shift(m2, -1), far_a, far_b))
+    p1, m1, pair, pair_mask = lax.optimization_barrier(
+        (shift(block, 1), shift(block, -1), pair, pair_mask)
+    )
+    pair_a, pair_b = mask_half(pair, pair_mask, 0), mask_half(pair, pair_mask, 1)
+    p2, m2, pair_a, pair_b = lax.optimization_barrier(
+        (shift(p1, 1), shift(m1, -1), pair_a, pair_b)
+    )
+    p3, m3 = shift(p2, 1), shift(m2, -1)
+    top, low = take_rows(p3, 0), take_rows(m3, 16)
+    _, _, far_a, far_b = lax.optimization_barrier((top, low, far_a, far_b))
+    top, low = shift(top, 1), shift(low, -1)
     cross_a, cross_b = swap(far_a), swap(far_b)
-    top, low = shift(take_rows(p3, 0), 1), shift(take_rows(m3, 16), -1)
 
     turn, home = multiply(
         place,

time: 196 us -> 184 us (0.939)
  local copies, waits for them, and re-layouts: 13.4 us -> 5.86 us
  waiting for transfers between devices: 66.1 us -> 61.3 us
    ppermute x8, waiting for transfers between devices: 37.8 us -> 26.8 us  [shift(): lax.ppermute(value, 'z', [(i, (i + step) % count) for i in range(count)])]
    unnamed x28 -> x20, local copies, waits for them, and re-layouts: 12.9 us -> 5.35 us
    all_to_all x2, waiting for transfers between devices: 25.4 us -> 28.5 us  [exchange(): return lax.all_to_all(value, axes, split_axis=0, concat_axis=0, tiled=True)]
    ppermute x2, waiting for transfers between devices: 2.96 us -> 6.01 us  [shift_x(): return lax.ppermute(value, ('xlo', 'xhi'), pairs)]
where the time goes in v5:
time: 184 us; the launch traced here: 183 us
  waiting for transfers between devices  61.3 us (33%)
  blocking collectives  50.8 us (28%)
  starting transfers between devices  41.7 us (23%)
  Pallas kernels  20.1 us (11%)
  local copies, waits for them, and re-layouts  5.86 us (3%)
  matrix products  2.52 us (1%)
    all_to_all x2, blocking collectives, exchange(): return lax.all_to_all(value, axes, split_axis=0, concat_axis=0, tiled=True)  50.8 us
    all_to_all x2, waiting for transfers between devices, exchange(): return lax.all_to_all(value, axes, split_axis=0, concat_axis=0, tiled=True)  28.5 us
    ppermute x8, waiting for transfers between devices, shift(): lax.ppermute(value, 'z', [(i, (i + step) % count) for i in range(count)])  26.8 us
    ppermute x8, starting transfers between devices, shift(): lax.ppermute(value, 'z', [(i, (i + step) % count) for i in range(count)])  16.5 us
    all_to_all x2, starting transfers between devices, exchange(): return lax.all_to_all(value, axes, split_axis=0, concat_axis=0, tiled=True)  16.2 us
    pallas_call x4, Pallas kernels, mask_half(): pl.pallas_call(mask_kernel, grid=(4,), in_specs=[pl.BlockSpec((rows, cols...  9.02 us
    pallas_call x1, Pallas kernels, multiply(): pl.pallas_call(product_kernel, in_specs=[pl.BlockSpec(memory_space=pltpu....  7.56 us
    ppermute x4, starting transfers between devices, swap(): return lax.ppermute(value, 'core', [(0, 1), (1, 0)])  6.31 us
  transfers between devices with their start and end apart: 16, of which 7 were waited for; matrix products, arithmetic and copies ran while one was open for 1% of the time, Pallas kernels for 5%

profile of v5, /device:TPU:1, one launch (start us, length us, event | category | flops | bytes accessed | tf_op | source)
XLA Modules:
  0.0 183.2 jit_solution(1743623038683979200)
XLA Ops:
  0.7 3.3 %collective-permute-start = (bf16[256,8192]{1,0:T(8,128)(2,1)}, bf16[256,8192]{1,0:T(8,128)(2,1)}, u32[]{:S(2)}, u32[]{:S(2)}) collective-permute-start(bf16[256,8192]{1,0:T(8,128)(2,1)} %ham_ref.1), channel_id=1, source_target_pairs={{0,8},{8,0},{1,9},{9,1},{2,10},{10,2},{3,11},{11,3},{4,12},{12,4},... | collective-permute-start | bytes 12582920 | tf_op jit(solution)/shard_map/ppermute | solution.py:247
  4.0 5.5 %all-to-all-start = ((bf16[32,8,1024]{2,1,0:T(8,128)(2,1)}), bf16[32,8,1024]{2,1,0:T(8,128)(2,1)S(1)}, u32[]{:S(2)}, u32[]{:S(2)}) async-start(bf16[32,8,1024]{2,1,0:T(8,128)(2,1)} %bitcast.28), calls=%async_computation | async-start | bytes 1048576 | tf_op jit(solution)/shard_map/all_to_all | solution.py:264
  9.8 2.2 %copy-done.1 = bf16[256,8192]{1,0:T(8,128)(2,1)S(1)} copy-done((bf16[256,8192]{1,0:T(8,128)(2,1)S(1)}, bf16[256,8192]{1,0:T(8,128)(2,1)}, u32[]{:S(2)}) %copy-start.1) | copy-done | bytes 4194328
  12.7 1.4 shard_map.77.own_a
  14.1 1.4 shard_map.78.own_b
  15.5 1.4 copy-done.2
  16.8 3.1 %all-to-all-done = bf16[32,8,1024]{2,1,0:T(8,128)(2,1)S(1)} async-done(((bf16[32,8,1024]{2,1,0:T(8,128)(2,1)}), bf16[32,8,1024]{2,1,0:T(8,128)(2,1)S(1)}, u32[]{:S(2)}, u32[]{:S(2)}) %all-to-all-start) | async-done | bytes 524320 | tf_op jit(solution)/shard_map/all_to_all | solution.py:264
  20.3 2.4 %collective-permute-start.11 = (bf16[256,4096]{1,0:T(8,128)(2,1)}, bf16[256,4096]{1,0:T(8,128)(2,1)S(1)}, u32[]{:S(2)}, u32[]{:S(2)}) collective-permute-start(bf16[256,4096]{1,0:T(8,128)(2,1)} %copy-done.2), channel_id=1, source_target_pairs={{0,132},{128,0},{4,128},{132,4},{1,133},{129,1},{5,129},{133,5},{2... | collective-permute-start | bytes 6291464 | tf_op jit(solution)/shard_map/ppermute | solution.py:260
  22.6 1.6 collective-permute-start.2
  24.3 3.9 %collective-permute-start.3 = (bf16[32,8192]{1,0:T(8,128)(2,1)S(1)}, bf16[32,8192]{1,0:T(8,128)(2,1)S(1)}, u32[]{:S(2)}, u32[]{:S(2)}) collective-permute-start(bf16[32,8192]{1,0:T(8,128)(2,1)S(1)} %bitcast.26), channel_id=1, source_target_pairs={{0,112},{16,0},{32,16},{48,32},{64,48},{80,64},{96,80},{112,96},{1... | collective-permute-start | bytes 1572872 | tf_op jit(solution)/shard_map/ppermute | solution.py:252
  28.2 9.9 %collective-permute-done.2.p1 = bf16[32,8192]{1,0:T(8,128)(2,1)S(1)} collective-permute-done((bf16[32,8192]{1,0:T(8,128)(2,1)S(1)}, bf16[32,8192]{1,0:T(8,128)(2,1)S(1)}, u32[]{:S(2)}, u32[]{:S(2)}) %collective-permute-start.2) | collective-permute-done | bytes 524320 | tf_op jit(solution)/shard_map/ppermute | solution.py:252
  38.1 2.7 %collective-permute-start.5 = (bf16[32,8192]{1,0:T(8,128)(2,1)S(1)}, bf16[32,8192]{1,0:T(8,128)(2,1)S(1)}, u32[]{:S(2)}, u32[]{:S(2)}) collective-permute-start(bf16[32,8192]{1,0:T(8,128)(2,1)S(1)} %collective-permute-done.3.m1), channel_id=1, source_target_pairs={{0,112},{16,0},{32,16},{48,32},{64,48},{80,64},{96,80},{112,96},{1... | collective-permute-start | bytes 1572872 | tf_op jit(solution)/shard_map/ppermute | solution.py:252
  40.8 3.0 %shard_map.80.pair_b = bf16[256,4096]{1,0:T(8,128)(2,1)S(1)} custom-call(bf16[256,8192]{1,0:T(8,128)(2,1)} %collective-permute-done.ham_ref, s32[8,256]{1,0:T(8,128)S(1)} %collective-permute-done.1.mask_ref), custom_call_target="tpu_custom_call" | custom-call | flops 2097152 | bytes 4194304 | tf_op jit(solution)/shard_map/pallas_call | solution.py:40
  43.8 3.2 %shard_map.79.pair_a = bf16[256,4096]{1,0:T(8,128)(2,1)S(1)} custom-call(bf16[256,8192]{1,0:T(8,128)(2,1)} %collective-permute-done.ham_ref, s32[8,256]{1,0:T(8,128)S(1)} %collective-permute-done.1.mask_ref), custom_call_target="tpu_custom_call" | custom-call | flops 2097152 | bytes 4194304 | tf_op jit(solution)/shard_map/pallas_call | solution.py:40
  47.0 2.7 %collective-permute-done.4.p2 = bf16[32,8192]{1,0:T(8,128)(2,1)S(1)} collective-permute-done((bf16[32,8192]{1,0:T(8,128)(2,1)S(1)}, bf16[32,8192]{1,0:T(8,128)(2,1)S(1)}, u32[]{:S(2)}, u32[]{:S(2)}) %collective-permute-start.4) | collective-permute-done | bytes 524320 | tf_op jit(solution)/shard_map/ppermute | solution.py:252
  49.7 1.1 collective-permute-start.6
  50.8 1.6 collective-permute-start.7
  52.4 8.0 %collective-permute-done.6.value_ref.p3 = bf16[32,8192]{1,0:T(8,128)(2,1)S(1)} collective-permute-done((bf16[32,8192]{1,0:T(8,128)(2,1)S(1)}, bf16[32,8192]{1,0:T(8,128)(2,1)S(1)}, u32[]{:S(2)}, u32[]{:S(2)}) %collective-permute-start.6) | collective-permute-done | bytes 524320 | tf_op jit(solution)/shard_map/ppermute | solution.py:252
  60.5 6.0 %collective-permute-done.10.far_a = bf16[256,4096]{1,0:T(8,128)(2,1)S(1)} collective-permute-done((bf16[256,4096]{1,0:T(8,128)(2,1)S(1)}, bf16[256,4096]{1,0:T(8,128)(2,1)S(1)}, u32[]{:S(2)}, u32[]{:S(2)}) %collective-permute-start.10) | collective-permute-done | bytes 2097184 | tf_op jit(solution)/shard_map/ppermute | solution.py:260
  66.5 2.7 %collective-permute-start.12 = (bf16[256,4096]{1,0:T(8,128)(2,1)S(1)}, bf16[256,4096]{1,0:T(8,128)(2,1)S(1)}, u32[]{:S(2)}, u32[]{:S(2)}) collective-permute-start(bf16[256,4096]{1,0:T(8,128)(2,1)S(1)} %collective-permute-done.10.far_a), channel_id=1, source_target_pairs={{0,8},{8,0},{1,9},{9,1},{2,10},{10,2},{3,11},{11,3},{4,12},{12,4},... | collective-permute-start | bytes 6291464 | tf_op jit(solution)/shard_map/ppermute | solution.py:247
  69.2 1.6 collective-permute-start.8
  70.9 3.9 %collective-permute-start.9 = (bf16[16,8192]{1,0:T(8,128)(2,1)S(1)}, bf16[16,8192]{1,0:T(8,128)(2,1)S(1)}, u32[]{:S(2)}, u32[]{:S(2)}) collective-permute-start(bf16[16,8192]{1,0:T(8,128)(2,1)S(1)} %shard_map.82), channel_id=1, source_target_pairs={{0,112},{16,0},{32,16},{48,32},{64,48},{80,64},{96,80},{112,96},{1... | collective-permute-start | bytes 786440 | tf_op jit(solution)/shard_map/ppermute | solution.py:252
  74.8 6.2 %collective-permute-done.8.top = bf16[16,8192]{1,0:T(8,128)(2,1)S(1)} collective-permute-done((bf16[16,8192]{1,0:T(8,128)(2,1)S(1)}, bf16[16,8192]{1,0:T(8,128)(2,1)S(1)}, u32[]{:S(2)}, u32[]{:S(2)}) %collective-permute-start.8) | collective-permute-done | bytes 262176 | tf_op jit(solution)/shard_map/ppermute | solution.py:252
  81.0 7.6 %shard_map.83 = (f32[8,264,128]{2,1,0:T(8,128)S(1)}, f32[32,64,128]{2,1,0:T(8,128)S(1)}) custom-call(s32[3]{0:T(128)S(1)} %pad_add_fusion.place_ref, bf16[32,8192]{1,0:T(8,128)(2,1)S(1)} %bitcast.27, bf16[32,8192]{1,0:T(8,128)(2,1)S(1)} %collective-permute-done.2.p1, bf16[32,8192]{1,0:T(8,128)(2,1)S(1)} %collective-permute-done.4.p2, ...), custom_call_target="tpu_custom_call" | custom-call | flops 4294967296 | bytes 25165824 | tf_op jit(solution)/shard_map/pallas_call | solution.py:127
  88.6 31.1 %all_to_all.26.turn_ref = f32[8,264,128]{2,1,0:T(8,128)S(1)} all-to-all(f32[8,264,128]{2,1,0:T(8,128)S(1)} %get-tuple-element.43), channel_id=1, replica_groups=mesh['xlo'=2,'z'=8,'core'=2,'xhi'=2,'y'=4] {'z'}, dimensions={0} | all-to-all | bytes 2162688 | tf_op jit(solution)/shard_map/all_to_all | solution.py:264
  119.7 1.6 shard_map.84
  121.2 10.7 %all-to-all-start.2 = ((f32[32,136,128]{2,1,0:T(8,128)}), f32[32,136,128]{2,1,0:T(8,128)S(1)}, u32[]{:S(2)}, u32[]{:S(2)}) async-start(f32[32,136,128]{2,1,0:T(8,128)} %shard_map.84), calls=%async_computation.2 | async-start | bytes 4456448 | tf_op jit(solution)/shard_map/all_to_all | solution.py:264
  132.8 1.8 convolution_add_fusion.diag_ref
  134.7 25.4 %all-to-all-done.2.tiles_ref = f32[32,136,128]{2,1,0:T(8,128)S(1)} async-done(((f32[32,136,128]{2,1,0:T(8,128)}), f32[32,136,128]{2,1,0:T(8,128)S(1)}, u32[]{:S(2)}, u32[]{:S(2)}) %all-to-all-start.2) | async-done | bytes 2228256 | tf_op jit(solution)/shard_map/all_to_all | solution.py:264
  160.0 1.0 copy-done.4
  161.8 19.7 %all_to_all.27 = f32[256,1,128]{2,1,0:T(1,128)S(1)} all-to-all(f32[256,1,128]{2,1,0:T(1,128)S(1)} %bitcast.30), channel_id=1, replica_groups=mesh['xlo'=2,'z'=8,'core'=2,'xhi'=2,'y'=4] {'xlo','z','core','xhi','y'}, dimensions={0} | all-to-all | bytes 262144 | tf_op jit(solution)/shard_map/all_to_all | solution.py:264
  181.5 1.2 shard_map.86
  (39 shorter events, 3.6 us)
Async XLA Ops:
  0.6 131.8 %copy-start = (f32[16,16]{1,0:T(8,128)S(1)}, f32[16,16]{1,0:T(8,128)}, u32[]{:S(2)}) copy-start(f32[16,16]{1,0:T(8,128)} %param.11) | copy-start | bytes 3076
  0.7 19.2 %collective-permute-start = (bf16[256,8192]{1,0:T(8,128)(2,1)}, bf16[256,8192]{1,0:T(8,128)(2,1)}, u32[]{:S(2)}, u32[]{:S(2)}) collective-permute-start(bf16[256,8192]{1,0:T(8,128)(2,1)} %ham_ref.1), channel_id=1, source_target_pairs={{0,8},{8,0},{1,9},{9,1},{2,10},{10,2},{3,11},{11,3},{4,12},{12,4},... | collective-permute-start | bytes 12582920 | tf_op jit(solution)/shard_map/ppermute | solution.py:247
  4.0 16.0 %all-to-all-start = ((bf16[32,8,1024]{2,1,0:T(8,128)(2,1)}), bf16[32,8,1024]{2,1,0:T(8,128)(2,1)S(1)}, u32[]{:S(2)}, u32[]{:S(2)}) async-start(bf16[32,8,1024]{2,1,0:T(8,128)(2,1)} %bitcast.28), calls=%async_computation | async-start | bytes 1048576 | tf_op jit(solution)/shard_map/all_to_all | solution.py:264
  9.5 7.4 %collective-permute-start.1 = (s32[8,256]{1,0:T(8,128)}, s32[8,256]{1,0:T(8,128)S(1)}, u32[]{:S(2)}, u32[]{:S(2)}) collective-permute-start(s32[8,256]{1,0:T(8,128)} %mask_ref.3), channel_id=1, source_target_pairs={{0,8},{8,0},{1,9},{9,1},{2,10},{10,2},{3,11},{11,3},{4,12},{12,4},... | collective-permute-start | bytes 24584 | tf_op jit(solution)/shard_map/ppermute | solution.py:247
  9.8 2.2 %copy-start.1 = (bf16[256,8192]{1,0:T(8,128)(2,1)S(1)}, bf16[256,8192]{1,0:T(8,128)(2,1)}, u32[]{:S(2)}) copy-start(bf16[256,8192]{1,0:T(8,128)(2,1)} %ham_ref.1) | copy-start | bytes 12582916
  12.0 0.7 copy-start.5
  12.7 1.4 copy-start.6
  15.5 1.4 copy-start.2
  20.0 46.5 %collective-permute-start.10 = (bf16[256,4096]{1,0:T(8,128)(2,1)S(1)}, bf16[256,4096]{1,0:T(8,128)(2,1)S(1)}, u32[]{:S(2)}, u32[]{:S(2)}) collective-permute-start(bf16[256,4096]{1,0:T(8,128)(2,1)S(1)} %shard_map.77.own_a), channel_id=1, source_target_pairs={{0,128},{128,4},{4,132},{132,0},{1,129},{129,5},{5,133},{133,1},{2... | collective-permute-start | bytes 6291464 | tf_op jit(solution)/shard_map/ppermute | solution.py:260
  20.3 46.2 %collective-permute-start.11 = (bf16[256,4096]{1,0:T(8,128)(2,1)}, bf16[256,4096]{1,0:T(8,128)(2,1)S(1)}, u32[]{:S(2)}, u32[]{:S(2)}) collective-permute-start(bf16[256,4096]{1,0:T(8,128)(2,1)} %copy-done.2), channel_id=1, source_target_pairs={{0,132},{128,0},{4,128},{132,4},{1,133},{129,1},{5,129},{133,5},{2... | collective-permute-start | bytes 6291464 | tf_op jit(solution)/shard_map/ppermute | solution.py:260
  22.6 15.5 %collective-permute-start.2 = (bf16[32,8192]{1,0:T(8,128)(2,1)S(1)}, bf16[32,8192]{1,0:T(8,128)(2,1)S(1)}, u32[]{:S(2)}, u32[]{:S(2)}) collective-permute-start(bf16[32,8192]{1,0:T(8,128)(2,1)S(1)} %bitcast.25), channel_id=1, source_target_pairs={{0,16},{16,32},{32,48},{48,64},{64,80},{80,96},{96,112},{112,0},{1... | collective-permute-start | bytes 1572872 | tf_op jit(solution)/shard_map/ppermute | solution.py:252
  24.3 13.8 %collective-permute-start.3 = (bf16[32,8192]{1,0:T(8,128)(2,1)S(1)}, bf16[32,8192]{1,0:T(8,128)(2,1)S(1)}, u32[]{:S(2)}, u32[]{:S(2)}) collective-permute-start(bf16[32,8192]{1,0:T(8,128)(2,1)S(1)} %bitcast.26), channel_id=1, source_target_pairs={{0,112},{16,0},{32,16},{48,32},{64,48},{80,64},{96,80},{112,96},{1... | collective-permute-start | bytes 1572872 | tf_op jit(solution)/shard_map/ppermute | solution.py:252
  38.1 11.6 %collective-permute-start.4 = (bf16[32,8192]{1,0:T(8,128)(2,1)S(1)}, bf16[32,8192]{1,0:T(8,128)(2,1)S(1)}, u32[]{:S(2)}, u32[]{:S(2)}) collective-permute-start(bf16[32,8192]{1,0:T(8,128)(2,1)S(1)} %collective-permute-done.2.p1), channel_id=1, source_target_pairs={{0,16},{16,32},{32,48},{48,64},{64,80},{80,96},{96,112},{112,0},{1... | collective-permute-start | bytes 1572872 | tf_op jit(solution)/shard_map/ppermute | solution.py:252
  38.1 11.6 %collective-permute-start.5 = (bf16[32,8192]{1,0:T(8,128)(2,1)S(1)}, bf16[32,8192]{1,0:T(8,128)(2,1)S(1)}, u32[]{:S(2)}, u32[]{:S(2)}) collective-permute-start(bf16[32,8192]{1,0:T(8,128)(2,1)S(1)} %collective-permute-done.3.m1), channel_id=1, source_target_pairs={{0,112},{16,0},{32,16},{48,32},{64,48},{80,64},{96,80},{112,96},{1... | collective-permute-start | bytes 1572872 | tf_op jit(solution)/shard_map/ppermute | solution.py:252
  43.8 37.2 %copy-start.3 = (bf16[256,4096]{1,0:T(8,128)(2,1)S(1)}, bf16[256,4096]{1,0:T(8,128)(2,1)}, u32[]{:S(2)}) copy-start(bf16[256,4096]{1,0:T(8,128)(2,1)} %copy-done.2) | copy-start | bytes 6291460
  49.7 10.7 %collective-permute-start.6 = (bf16[32,8192]{1,0:T(8,128)(2,1)S(1)}, bf16[32,8192]{1,0:T(8,128)(2,1)S(1)}, u32[]{:S(2)}, u32[]{:S(2)}) collective-permute-start(bf16[32,8192]{1,0:T(8,128)(2,1)S(1)} %collective-permute-done.4.p2), channel_id=1, source_target_pairs={{0,16},{16,32},{32,48},{48,64},{64,80},{80,96},{96,112},{112,0},{1... | collective-permute-start | bytes 1572872 | tf_op jit(solution)/shard_map/ppermute | solution.py:252
  50.8 9.7 %collective-permute-start.7 = (bf16[32,8192]{1,0:T(8,128)(2,1)S(1)}, bf16[32,8192]{1,0:T(8,128)(2,1)S(1)}, u32[]{:S(2)}, u32[]{:S(2)}) collective-permute-start(bf16[32,8192]{1,0:T(8,128)(2,1)S(1)} %collective-permute-done.5.m2), channel_id=1, source_target_pairs={{0,112},{16,0},{32,16},{48,32},{64,48},{80,64},{96,80},{112,96},{1... | collective-permute-start | bytes 1572872 | tf_op jit(solution)/shard_map/ppermute | solution.py:252
  66.5 14.5 %collective-permute-start.12 = (bf16[256,4096]{1,0:T(8,128)(2,1)S(1)}, bf16[256,4096]{1,0:T(8,128)(2,1)S(1)}, u32[]{:S(2)}, u32[]{:S(2)}) collective-permute-start(bf16[256,4096]{1,0:T(8,128)(2,1)S(1)} %collective-permute-done.10.far_a), channel_id=1, source_target_pairs={{0,8},{8,0},{1,9},{9,1},{2,10},{10,2},{3,11},{11,3},{4,12},{12,4},... | collective-permute-start | bytes 6291464 | tf_op jit(solution)/shard_map/ppermute | solution.py:247
  69.2 11.8 %collective-permute-start.13 = (bf16[256,4096]{1,0:T(8,128)(2,1)S(1)}, bf16[256,4096]{1,0:T(8,128)(2,1)S(1)}, u32[]{:S(2)}, u32[]{:S(2)}) collective-permute-start(bf16[256,4096]{1,0:T(8,128)(2,1)S(1)} %collective-permute-done.11.far_b), channel_id=1, source_target_pairs={{0,8},{8,0},{1,9},{9,1},{2,10},{10,2},{3,11},{11,3},{4,12},{12,4},... | collective-permute-start | bytes 6291464 | tf_op jit(solution)/shard_map/ppermute | solution.py:247
  69.2 11.8 %collective-permute-start.8 = (bf16[16,8192]{1,0:T(8,128)(2,1)S(1)}, bf16[16,8192]{1,0:T(8,128)(2,1)S(1)}, u32[]{:S(2)}, u32[]{:S(2)}) collective-permute-start(bf16[16,8192]{1,0:T(8,128)(2,1)S(1)} %shard_map.81), channel_id=1, source_target_pairs={{0,16},{16,32},{32,48},{48,64},{64,80},{80,96},{96,112},{112,0},{1... | collective-permute-start | bytes 786440 | tf_op jit(solution)/shard_map/ppermute | solution.py:252
  70.9 10.2 %collective-permute-start.9 = (bf16[16,8192]{1,0:T(8,128)(2,1)S(1)}, bf16[16,8192]{1,0:T(8,128)(2,1)S(1)}, u32[]{:S(2)}, u32[]{:S(2)}) collective-permute-start(bf16[16,8192]{1,0:T(8,128)(2,1)S(1)} %shard_map.82), channel_id=1, source_target_pairs={{0,112},{16,0},{32,16},{48,32},{64,48},{80,64},{96,80},{112,96},{1... | collective-permute-start | bytes 786440 | tf_op jit(solution)/shard_map/ppermute | solution.py:252
  121.2 10.8 %copy-start.8 = (s32[16,8192]{1,0:T(8,128)S(1)}, s32[16,8192]{1,0:T(8,128)}, u32[]{:S(2)}) copy-start(s32[16,8192]{1,0:T(8,128)} %param.9) | copy-start | bytes 1572868
  121.2 10.8 %copy-start.9 = (f32[16]{0:T(128)S(1)}, f32[16]{0:T(128)}, u32[]{:S(2)}) copy-start(f32[16]{0:T(128)} %param.10) | copy-start | bytes 196
  121.2 38.8 %all-to-all-start.2 = ((f32[32,136,128]{2,1,0:T(8,128)}), f32[32,136,128]{2,1,0:T(8,128)S(1)}, u32[]{:S(2)}, u32[]{:S(2)}) async-start(f32[32,136,128]{2,1,0:T(8,128)} %shard_map.84), calls=%async_computation.2 | async-start | bytes 4456448 | tf_op jit(solution)/shard_map/all_to_all | solution.py:264
  132.0 0.8 copy-start.7
  160.0 1.0 copy-start.4

commit v6 on v4

--- a/solution.py
+++ b/solution.py
@@ -34,28 +34,69 @@
         out_ref[at : at + tile, :] = values.astype(jnp.bfloat16)
 
 
-def mask_half(ham, tile_mask, half):
+def mask_rows_of(ham, tile_mask):
     rows, cols = ham.shape
     mask_rows, mask_cols = tile_mask.shape
     return pl.pallas_call(
         mask_kernel,
-        grid=(4,),
+        grid=(cols // CHUNK,),
         in_specs=[
-            pl.BlockSpec((rows, cols // 8), lambda j: (0, half * 4 + j)),
-            pl.BlockSpec((mask_rows, mask_cols // 2), lambda j: (0, half)),
-        ],
-        out_specs=pl.BlockSpec((rows, cols // 8), lambda j: (0, j)),
-        out_shape=jax.ShapeDtypeStruct((rows, cols // 2), jnp.bfloat16),
+            pl.BlockSpec((rows, CHUNK), lambda j: (0, j)),
+            pl.BlockSpec((mask_rows, mask_cols), lambda j: (0, 0)),
+        ],
+        out_specs=pl.BlockSpec((rows, CHUNK), lambda j: (0, j)),
+        out_shape=jax.ShapeDtypeStruct((rows, cols), jnp.bfloat16),
         compiler_params=pltpu.CompilerParams(vmem_limit_bytes=8 * MIB),
+        cost_estimate=pl.CostEstimate(
+            flops=2 * rows * cols, bytes_accessed=4 * rows * cols, transcendentals=0
+        ),
+    )(ham, tile_mask)
+
+
+def part_kernel(place_ref, ham_ref, mask_ref, *out_refs):
+    rows = ham_ref.shape[0]
+    mask_rows, mask_cols = mask_ref.shape
+    tile = rows // mask_rows
+    mask = mask_ref[...].astype(jnp.float32).astype(jnp.bfloat16)
+    parts = [(place_ref[3] * 2, out_refs[0], 0), (place_ref[3] * 2 + 1, out_refs[1], 0)]
+    parts += [(4 + index, out_refs[2 + index // 2], index % 2 * CHUNK) for index in range(4)]
+    for chunk, out_ref, start in parts:
+        column = lax.broadcasted_iota(jnp.int32, (mask_cols, CHUNK), 1)
+        spread = (
+            column // tile + chunk * (CHUNK // tile)
+            == lax.broadcasted_iota(jnp.int32, (mask_cols, CHUNK), 0)
+        ).astype(jnp.bfloat16)
+        wide = jnp.dot(mask, spread, preferred_element_type=jnp.float32)
+        columns = pl.ds(chunk * CHUNK, CHUNK)
+        if not isinstance(chunk, int):
+            columns = pl.ds(pl.multiple_of(chunk * CHUNK, CHUNK), CHUNK)
+        for row in range(mask_rows):
+            at = row * tile
+            values = ham_ref[at : at + tile, columns].astype(jnp.float32) * wide[row : row + 1, :]
+            out_ref[at : at + tile, start : start + CHUNK] = values.astype(jnp.bfloat16)
+
+
+def mask_part(place, ham, tile_mask):
+    rows, cols = ham.shape
+    vmem = pl.BlockSpec(memory_space=pltpu.VMEM)
+    return pl.pallas_call(
+        part_kernel,
+        in_specs=[pl.BlockSpec(memory_space=pltpu.SMEM), vmem, vmem],
+        out_specs=[vmem] * 4,
+        out_shape=[
+            jax.ShapeDtypeStruct((rows, width), jnp.bfloat16)
+            for width in (CHUNK, CHUNK, 2 * CHUNK, 2 * CHUNK)
+        ],
+        compiler_params=pltpu.CompilerParams(vmem_limit_bytes=12 * MIB),
         cost_estimate=pl.CostEstimate(
             flops=rows * cols, bytes_accessed=2 * rows * cols, transcendentals=0
         ),
-    )(ham, tile_mask)
+    )(place, ham, tile_mask)
 
 
 def product_kernel(
     place_ref, c0, p1, p2, p3, m1, m2, m3, top, low,
-    own_a, own_b, pair_a, pair_b, far_a, far_b, cross_a, cross_b,
+    own, pair, f0, f2, g0, g2, fa, fb, x0, x2, w0, w2, xa, xb,
     turn_ref, home_ref, lhs, acc, local,
 ):
     xlo, z, core = place_ref[0], place_ref[1], place_ref[2]
@@ -71,27 +112,24 @@
         out[pl.ds(row, 16), :] = top[:, pl.ds(at, width)]
         out[pl.ds(pl.multiple_of(row + 16, 16), 16), :] = low[:, pl.ds(at, width)]
 
-    for start, panels in (
-        (0, (own_a, pair_a, far_a, cross_a)),
-        (strings // 2, (own_b, pair_b, far_b, cross_b)),
-    ):
-
-        def step(index, carry, start=start, panels=panels):
-            at = pl.multiple_of(index * CHUNK, CHUNK)
-            gather(pl.multiple_of(start + at, CHUNK), CHUNK, lhs)
-            for number, ref in enumerate(panels):
-                side = xlo if number < 2 else 1 - xlo
-                other = core if number % 2 == 0 else 1 - core
-                columns = pl.ds(pl.multiple_of((side * 2 + other) * 256, 256), 256)
-                acc[:, columns] += lax.dot_general(
-                    lhs[...],
-                    ref[:, pl.ds(at, CHUNK)],
-                    (((1,), (1,)), ((), ())),
-                    preferred_element_type=jnp.float32,
-                )
-            return carry
-
-        lax.fori_loop(0, strings // 2 // CHUNK, step, 0)
+    parity = place_ref[3]
+    steps = [
+        (2 * parity, f0, x0, 0), (2 * parity + 1, f2, x2, 0),
+        (2 - 2 * parity, g0, w0, 0), (3 - 2 * parity, g2, w2, 0),
+        (4, fa, xa, 0), (5, fa, xa, CHUNK), (6, fb, xb, 0), (7, fb, xb, CHUNK),
+    ]
+    for chunk, far, cross, start in steps:
+        at = pl.multiple_of(chunk * CHUNK, CHUNK)
+        gather(at, CHUNK, lhs)
+        part = slice(start, start + CHUNK)
+        here = pl.ds(at, CHUNK)
+        for number, panel in enumerate((own[:, here], pair[:, here], far[:, part], cross[:, part])):
+            side = xlo if number < 2 else 1 - xlo
+            other = core if number % 2 == 0 else 1 - core
+            columns = pl.ds(pl.multiple_of((side * 2 + other) * 256, 256), 256)
+            acc[:, columns] += lax.dot_general(
+                lhs[...], panel, (((1,), (1,)), ((), ())), preferred_element_type=jnp.float32
+            )
 
     for side in range(2):
         at = pl.multiple_of(side * (strings // 2) + z * 512, 512)
@@ -260,6 +298,11 @@
     return lax.ppermute(value, ("xlo", "xhi"), pairs)
 
 
+def shift_y(value, step):
+    count = lax.axis_size("y")
+    return lax.ppermute(value, "y", [(i, (i + step) % count) for i in range(count)])
+
+
 def exchange(value, axes):
     return lax.all_to_all(value, axes, split_axis=0, concat_axis=0, tiled=True)
 
@@ -273,28 +316,38 @@
     row_index = (xlo * 8 + z) * 2 + core
     col_index = lax.axis_index("xhi") * 4 + lax.axis_index("y")
 
-    place = jnp.stack([xlo, z, core]).astype(jnp.int32)
+    parity = lax.rem(lax.axis_index("y"), 2)
+    place = jnp.stack([xlo, z, core, parity]).astype(jnp.int32)
     ham, place = lax.optimization_barrier((ham, place))
     pair, pair_mask = swap(ham), swap(tile_mask)
-    own_a, own_b = mask_half(ham, tile_mask, 0), mask_half(ham, tile_mask, 1)
-    pair_a, pair_b = mask_half(pair, pair_mask, 0), mask_half(pair, pair_mask, 1)
+    s0, s2, sa, sb = mask_part(place, ham, tile_mask)
 
     block = exchange(coeff.reshape(32, 8, cols), PLANE)
     block = block.reshape(4, 8, 8, cols).transpose(0, 2, 1, 3).reshape(32, strings)
-    block, own_a, own_b, pair_a, pair_b = lax.optimization_barrier(
-        (block, own_a, own_b, pair_a, pair_b)
-    )
-    far_a, far_b = shift_x(own_a, 1), shift_x(own_b, -1)
-    p1, m1 = lax.optimization_barrier((shift(block, 1), shift(block, -1)))
-    p2, m2 = lax.optimization_barrier((shift(p1, 1), shift(m1, -1)))
-    p3, m3, far_a, far_b = lax.optimization_barrier((shift(p2, 1), shift(m2, -1), far_a, far_b))
-    cross_a, cross_b = swap(far_a), swap(far_b)
+    block, s0, s2, sa, sb, pair, pair_mask = lax.optimization_barrier(
+        (block, s0, s2, sa, sb, pair, pair_mask)
+    )
+    p1, m1, f0, f2, sa, sb, ham, pair, pair_mask = lax.optimization_barrier(
+        (
+            shift(block, 1), shift(block, -1), shift_x(s0, 1), shift_x(s2, -1),
+            sa, sb, ham, pair, pair_mask,
+        )
+    )
+    fa, fb = shift_x(sa, 1), shift_x(sb, -1)
+    own, pair = mask_rows_of(ham, tile_mask), mask_rows_of(pair, pair_mask)
+    p2, m2, g0, f2, own, pair = lax.optimization_barrier(
+        (shift(p1, 1), shift(m1, -1), shift_y(f0, 1), f2, own, pair)
+    )
+    p3, m3, g2, fa, fb, f0, f2, g0 = lax.optimization_barrier(
+        (shift(p2, 1), shift(m2, -1), shift_y(f2, -1), fa, fb, f0, f2, g0)
+    )
     top, low = shift(take_rows(p3, 0), 1), shift(take_rows(m3, 16), -1)
+    x0, x2, w0, w2, xa, xb = (swap(value) for value in (f0, f2, g0, g2, fa, fb))
 
     turn, home = multiply(
         place,
         (block, p1, p2, p3, m1, m2, m3, top, low),
-        (own_a, own_b, pair_a, pair_b, far_a, far_b, cross_a, cross_b),
+        (own, pair, f0, f2, g0, g2, fa, fb, x0, x2, w0, w2, xa, xb),
     )
 
     tiles = exchange(pack(exchange(turn, "z"), home), PLANE)

time: 196 us -> 188 us (0.959)
  waiting for transfers between devices: 66.1 us -> 58.1 us
  local copies, waits for them, and re-layouts: 13.4 us -> 7.48 us
  starting transfers between devices: 41.1 us -> 43.8 us
  blocking collectives: 50.9 us -> 53.5 us
    ppermute x8, waiting for transfers between devices: 37.8 us -> 22.9 us  [shift(): lax.ppermute(value, 'z', [(i, (i + step) % count) for i in range(count)])]
    ppermute x4 -> x8, starting transfers between devices: 4.88 us -> 11.1 us  [swap(): return lax.ppermute(value, 'core', [(0, 1), (1, 0)])]
    unnamed x28 -> x20, local copies, waits for them, and re-layouts: 12.9 us -> 6.97 us
    all_to_all x2, waiting for transfers between devices: 25.4 us -> 30.3 us  [exchange(): return lax.all_to_all(value, axes, split_axis=0, concat_axis=0, tiled=True)]
    all_to_all x2, starting transfers between devices: 16.6 us -> 12 us  [exchange(): return lax.all_to_all(value, axes, split_axis=0, concat_axis=0, tiled=True)]
    ppermute x8, starting transfers between devices: 16.9 us -> 12.5 us  [shift(): lax.ppermute(value, 'z', [(i, (i + step) % count) for i in range(count)])]
    ppermute x0 -> x2, starting transfers between devices: none -> 2.89 us  [shift_y(): lax.ppermute(value, 'y', [(i, (i + step) % count) for i in range(count)])]
    ppermute x2 -> x4, starting transfers between devices: 2.74 us -> 5.35 us  [shift_x(): return lax.ppermute(value, ('xlo', 'xhi'), pairs)]
  transfers between devices with their start and end apart: 16 -> 24, of which waited for: 7 -> 9; matrix products, arithmetic and copies ran while one was open for 1% -> 1% of each run, Pallas kernels for 5% -> 6%
where the time goes in v6:
time: 188 us; the launch traced here: 187 us
  waiting for transfers between devices  58.1 us (31%)
  blocking collectives  53.5 us (28%)
  starting transfers between devices  43.8 us (23%)
  Pallas kernels  20.6 us (11%)
  local copies, waits for them, and re-layouts  7.48 us (4%)
  matrix products  2.52 us (1%)
    all_to_all x2, blocking collectives, exchange(): return lax.all_to_all(value, axes, split_axis=0, concat_axis=0, tiled=True)  53.5 us
    all_to_all x2, waiting for transfers between devices, exchange(): return lax.all_to_all(value, axes, split_axis=0, concat_axis=0, tiled=True)  30.3 us
    ppermute x8, waiting for transfers between devices, shift(): lax.ppermute(value, 'z', [(i, (i + step) % count) for i in range(count)])  22.9 us
    ppermute x8, starting transfers between devices, shift(): lax.ppermute(value, 'z', [(i, (i + step) % count) for i in range(count)])  12.5 us
    all_to_all x2, starting transfers between devices, exchange(): return lax.all_to_all(value, axes, split_axis=0, concat_axis=0, tiled=True)  12 us
    ppermute x8, starting transfers between devices, swap(): return lax.ppermute(value, 'core', [(0, 1), (1, 0)])  11.1 us
    pallas_call x2, Pallas kernels, mask_rows_of(): pl.pallas_call(mask_kernel, grid=(cols // CHUNK,), in_specs=[pl.BlockSpec...  9.22 us
    unnamed x20, local copies, waits for them, and re-layouts  6.97 us
  transfers between devices with their start and end apart: 24, of which 9 were waited for; matrix products, arithmetic and copies ran while one was open for 1% of the time, Pallas kernels for 6%

profile of v6, /device:TPU:1, one launch (start us, length us, event | category | flops | bytes accessed | tf_op | source)
XLA Modules:
  0.0 186.9 jit_solution(6024940913015716493)
XLA Ops:
  0.7 3.3 %collective-permute-start = (bf16[256,8192]{1,0:T(8,128)(2,1)}, bf16[256,8192]{1,0:T(8,128)(2,1)}, u32[]{:S(2)}, u32[]{:S(2)}) collective-permute-start(bf16[256,8192]{1,0:T(8,128)(2,1)} %ham_ref.1), channel_id=1, source_target_pairs={{0,8},{8,0},{1,9},{9,1},{2,10},{10,2},{3,11},{11,3},{4,12},{12,4},... | collective-permute-start | bytes 12582920 | tf_op jit(solution)/shard_map/ppermute | solution.py:285
  4.0 5.5 %all-to-all-start = ((bf16[32,8,1024]{2,1,0:T(8,128)(2,1)}), bf16[32,8,1024]{2,1,0:T(8,128)(2,1)S(1)}, u32[]{:S(2)}, u32[]{:S(2)}) async-start(bf16[32,8,1024]{2,1,0:T(8,128)(2,1)} %bitcast.29), calls=%async_computation | async-start | bytes 1048576 | tf_op jit(solution)/shard_map/all_to_all | solution.py:307
  9.8 2.2 %copy-done.1 = bf16[256,8192]{1,0:T(8,128)(2,1)S(1)} copy-done((bf16[256,8192]{1,0:T(8,128)(2,1)S(1)}, bf16[256,8192]{1,0:T(8,128)(2,1)}, u32[]{:S(2)}) %copy-start.1) | copy-done | bytes 4194328
  12.7 1.5 shard_map.77
  15.0 5.0 %all-to-all-done = bf16[32,8,1024]{2,1,0:T(8,128)(2,1)S(1)} async-done(((bf16[32,8,1024]{2,1,0:T(8,128)(2,1)}), bf16[32,8,1024]{2,1,0:T(8,128)(2,1)S(1)}, u32[]{:S(2)}, u32[]{:S(2)}) %all-to-all-start) | async-done | bytes 524320 | tf_op jit(solution)/shard_map/all_to_all | solution.py:307
  20.0 1.6 collective-permute-start.2
  21.6 3.9 %collective-permute-start.3 = (bf16[32,8192]{1,0:T(8,128)(2,1)S(1)}, bf16[32,8192]{1,0:T(8,128)(2,1)S(1)}, u32[]{:S(2)}, u32[]{:S(2)}) collective-permute-start(bf16[32,8192]{1,0:T(8,128)(2,1)S(1)} %bitcast.27), channel_id=1, source_target_pairs={{0,112},{16,0},{32,16},{48,32},{64,48},{80,64},{96,80},{112,96},{1... | collective-permute-start | bytes 1572872 | tf_op jit(solution)/shard_map/ppermute | solution.py:290
  25.9 2.4 %collective-permute-start.5 = (bf16[256,1024]{1,0:T(8,128)(2,1)S(1)}, bf16[256,1024]{1,0:T(8,128)(2,1)S(1)}, u32[]{:S(2)}, u32[]{:S(2)}) collective-permute-start(bf16[256,1024]{1,0:T(8,128)(2,1)S(1)} %get-tuple-element.53), channel_id=1, source_target_pairs={{0,132},{128,0},{4,128},{132,4},{1,133},{129,1},{5,129},{133,5},{2... | collective-permute-start | bytes 1572872 | tf_op jit(solution)/shard_map/ppermute | solution.py:298
  28.2 7.8 %collective-permute-done.2.p1 = bf16[32,8192]{1,0:T(8,128)(2,1)S(1)} collective-permute-done((bf16[32,8192]{1,0:T(8,128)(2,1)S(1)}, bf16[32,8192]{1,0:T(8,128)(2,1)S(1)}, u32[]{:S(2)}, u32[]{:S(2)}) %collective-permute-start.2) | collective-permute-done | bytes 524320 | tf_op jit(solution)/shard_map/ppermute | solution.py:290
  36.0 2.3 %collective-permute-done.4.f0 = bf16[256,1024]{1,0:T(8,128)(2,1)S(1)} collective-permute-done((bf16[256,1024]{1,0:T(8,128)(2,1)}, bf16[256,1024]{1,0:T(8,128)(2,1)S(1)}, u32[]{:S(2)}, u32[]{:S(2)}) %collective-permute-start.4) | collective-permute-done | bytes 524320 | tf_op jit(solution)/shard_map/ppermute | solution.py:298
  38.3 2.7 %collective-permute-start.7 = (bf16[32,8192]{1,0:T(8,128)(2,1)S(1)}, bf16[32,8192]{1,0:T(8,128)(2,1)S(1)}, u32[]{:S(2)}, u32[]{:S(2)}) collective-permute-start(bf16[32,8192]{1,0:T(8,128)(2,1)S(1)} %collective-permute-done.3.m1), channel_id=1, source_target_pairs={{0,112},{16,0},{32,16},{48,32},{64,48},{80,64},{96,80},{112,96},{1... | collective-permute-start | bytes 1572872 | tf_op jit(solution)/shard_map/ppermute | solution.py:290
  41.0 2.8 %collective-permute-start.8 = (bf16[256,1024]{1,0:T(8,128)(2,1)S(1)}, bf16[256,1024]{1,0:T(8,128)(2,1)S(1)}, u32[]{:S(2)}, u32[]{:S(2)}) collective-permute-start(bf16[256,1024]{1,0:T(8,128)(2,1)S(1)} %collective-permute-done.4.f0), channel_id=1, source_target_pairs={{0,1},{1,2},{2,3},{3,0},{4,5},{5,6},{6,7},{7,4},{8,9},{9,10},{10,1... | collective-permute-start | bytes 1572872 | tf_op jit(solution)/shard_map/ppermute | solution.py:303
  43.8 2.7 %collective-permute-start.13 = (bf16[256,2048]{1,0:T(8,128)(2,1)S(1)}, bf16[256,2048]{1,0:T(8,128)(2,1)S(1)}, u32[]{:S(2)}, u32[]{:S(2)}) collective-permute-start(bf16[256,2048]{1,0:T(8,128)(2,1)S(1)} %get-tuple-element.69), channel_id=1, source_target_pairs={{0,132},{128,0},{4,128},{132,4},{1,133},{129,1},{5,129},{133,5},{2... | collective-permute-start | bytes 3145736 | tf_op jit(solution)/shard_map/ppermute | solution.py:298
  46.5 2.2 %copy-done.2 = bf16[256,8192]{1,0:T(8,128)(2,1)S(1)} copy-done((bf16[256,8192]{1,0:T(8,128)(2,1)S(1)}, bf16[256,8192]{1,0:T(8,128)(2,1)}, u32[]{:S(2)}) %copy-start.2) | copy-done | bytes 4194328
  48.7 3.2 %shard_map.78.own = bf16[256,8192]{1,0:T(8,128)(2,1)S(1)} custom-call(bf16[256,8192]{1,0:T(8,128)(2,1)S(1)} %copy-done.2, s32[8,256]{1,0:T(8,128)S(1)} %copy-done.5), custom_call_target="tpu_custom_call" | custom-call | flops 4194304 | bytes 8388608 | tf_op jit(solution)/shard_map/pallas_call | solution.py:40
  51.8 6.1 %shard_map.79.pair = bf16[256,8192]{1,0:T(8,128)(2,1)S(1)} custom-call(bf16[256,8192]{1,0:T(8,128)(2,1)} %collective-permute-done.ham_ref, s32[8,256]{1,0:T(8,128)S(1)} %collective-permute-done.1.mask_ref), custom_call_target="tpu_custom_call" | custom-call | flops 4194304 | bytes 8388608 | tf_op jit(solution)/shard_map/pallas_call | solution.py:40
  58.1 1.4 collective-permute-start.9
  59.5 8.8 %collective-permute-done.10.value_ref.m3 = bf16[32,8192]{1,0:T(8,128)(2,1)S(1)} collective-permute-done((bf16[32,8192]{1,0:T(8,128)(2,1)S(1)}, bf16[32,8192]{1,0:T(8,128)(2,1)S(1)}, u32[]{:S(2)}, u32[]{:S(2)}) %collective-permute-start.10) | collective-permute-done | bytes 524320 | tf_op jit(solution)/shard_map/ppermute | solution.py:290
  68.4 5.6 %collective-permute-start.16 = (bf16[256,1024]{1,0:T(8,128)(2,1)S(1)}, bf16[256,1024]{1,0:T(8,128)(2,1)S(1)}, u32[]{:S(2)}, u32[]{:S(2)}) collective-permute-start(bf16[256,1024]{1,0:T(8,128)(2,1)S(1)} %collective-permute-done.4.f0), channel_id=1, source_target_pairs={{0,8},{8,0},{1,9},{9,1},{2,10},{10,2},{3,11},{11,3},{4,12},{12,4},... | collective-permute-start | bytes 1572872 | tf_op jit(solution)/shard_map/ppermute | solution.py:285
  74.6 2.7 %collective-permute-start.15 = (bf16[16,8192]{1,0:T(8,128)(2,1)S(1)}, bf16[16,8192]{1,0:T(8,128)(2,1)S(1)}, u32[]{:S(2)}, u32[]{:S(2)}) collective-permute-start(bf16[16,8192]{1,0:T(8,128)(2,1)S(1)} %shard_map.81), channel_id=1, source_target_pairs={{0,112},{16,0},{32,16},{48,32},{64,48},{80,64},{96,80},{112,96},{1... | collective-permute-start | bytes 786440 | tf_op jit(solution)/shard_map/ppermute | solution.py:290
  77.3 6.3 %collective-permute-done.14.top = bf16[16,8192]{1,0:T(8,128)(2,1)S(1)} collective-permute-done((bf16[16,8192]{1,0:T(8,128)(2,1)S(1)}, bf16[16,8192]{1,0:T(8,128)(2,1)S(1)}, u32[]{:S(2)}, u32[]{:S(2)}) %collective-permute-start.14) | collective-permute-done | bytes 262176 | tf_op jit(solution)/shard_map/ppermute | solution.py:290
  83.6 0.9 collective-permute-start.17
  85.0 1.0 collective-permute-done.17.x2
  87.5 6.3 %shard_map.82 = (f32[8,264,128]{2,1,0:T(8,128)S(1)}, f32[32,64,128]{2,1,0:T(8,128)S(1)}) custom-call(s32[4]{0:T(128)S(1)} %pad_add_fusion.place_ref, bf16[32,8192]{1,0:T(8,128)(2,1)S(1)} %bitcast.28, bf16[32,8192]{1,0:T(8,128)(2,1)S(1)} %collective-permute-done.2.p1, bf16[32,8192]{1,0:T(8,128)(2,1)S(1)} %collective-permute-done.6.p2, ...), custom_call_target="tpu_custom_call" | custom-call | flops 4294967296 | bytes 25165824 | tf_op jit(solution)/shard_map/pallas_call | solution.py:165
  93.9 33.7 %all_to_all.26.turn_ref = f32[8,264,128]{2,1,0:T(8,128)S(1)} all-to-all(f32[8,264,128]{2,1,0:T(8,128)S(1)} %get-tuple-element.81), channel_id=1, replica_groups=mesh['xlo'=2,'z'=8,'core'=2,'xhi'=2,'y'=4] {'z'}, dimensions={0} | all-to-all | bytes 2162688 | tf_op jit(solution)/shard_map/all_to_all | solution.py:307
  127.5 1.5 shard_map.83
  129.1 6.5 %all-to-all-start.2 = ((f32[32,136,128]{2,1,0:T(8,128)}), f32[32,136,128]{2,1,0:T(8,128)S(1)}, u32[]{:S(2)}, u32[]{:S(2)}) async-start(f32[32,136,128]{2,1,0:T(8,128)} %shard_map.83), calls=%async_computation.2 | async-start | bytes 4456448 | tf_op jit(solution)/shard_map/all_to_all | solution.py:307
  136.4 1.8 convolution_add_fusion.diag_ref
  138.3 25.3 %all-to-all-done.2.tiles_ref = f32[32,136,128]{2,1,0:T(8,128)S(1)} async-done(((f32[32,136,128]{2,1,0:T(8,128)}), f32[32,136,128]{2,1,0:T(8,128)S(1)}, u32[]{:S(2)}, u32[]{:S(2)}) %all-to-all-start.2) | async-done | bytes 2228256 | tf_op jit(solution)/shard_map/all_to_all | solution.py:307
  163.6 1.0 copy-done.3
  165.4 19.8 %all_to_all.27 = f32[256,1,128]{2,1,0:T(1,128)S(1)} all-to-all(f32[256,1,128]{2,1,0:T(1,128)S(1)} %bitcast.31), channel_id=1, replica_groups=mesh['xlo'=2,'z'=8,'core'=2,'xhi'=2,'y'=4] {'xlo','z','core','xhi','y'}, dimensions={0} | all-to-all | bytes 262144 | tf_op jit(solution)/shard_map/all_to_all | solution.py:307
  185.2 1.2 shard_map.85
  (54 shorter events, 7.1 us)
Async XLA Ops:
  0.6 135.3 %copy-start = (f32[16,16]{1,0:T(8,128)S(1)}, f32[16,16]{1,0:T(8,128)}, u32[]{:S(2)}) copy-start(f32[16,16]{1,0:T(8,128)} %param.11) | copy-start | bytes 3076
  0.6 45.8 %copy-start.5 = (s32[8,256]{1,0:T(8,128)S(1)}, s32[8,256]{1,0:T(8,128)}, u32[]{:S(2)}) copy-start(s32[8,256]{1,0:T(8,128)} %mask_ref.3) | copy-start | bytes 24580
  0.7 19.2 %collective-permute-start = (bf16[256,8192]{1,0:T(8,128)(2,1)}, bf16[256,8192]{1,0:T(8,128)(2,1)}, u32[]{:S(2)}, u32[]{:S(2)}) collective-permute-start(bf16[256,8192]{1,0:T(8,128)(2,1)} %ham_ref.1), channel_id=1, source_target_pairs={{0,8},{8,0},{1,9},{9,1},{2,10},{10,2},{3,11},{11,3},{4,12},{12,4},... | collective-permute-start | bytes 12582920 | tf_op jit(solution)/shard_map/ppermute | solution.py:285
  4.0 16.0 %all-to-all-start = ((bf16[32,8,1024]{2,1,0:T(8,128)(2,1)}), bf16[32,8,1024]{2,1,0:T(8,128)(2,1)S(1)}, u32[]{:S(2)}, u32[]{:S(2)}) async-start(bf16[32,8,1024]{2,1,0:T(8,128)(2,1)} %bitcast.29), calls=%async_computation | async-start | bytes 1048576 | tf_op jit(solution)/shard_map/all_to_all | solution.py:307
  9.5 5.5 %collective-permute-start.1 = (s32[8,256]{1,0:T(8,128)}, s32[8,256]{1,0:T(8,128)S(1)}, u32[]{:S(2)}, u32[]{:S(2)}) collective-permute-start(s32[8,256]{1,0:T(8,128)} %mask_ref.3), channel_id=1, source_target_pairs={{0,8},{8,0},{1,9},{9,1},{2,10},{10,2},{3,11},{11,3},{4,12},{12,4},... | collective-permute-start | bytes 24584 | tf_op jit(solution)/shard_map/ppermute | solution.py:285
  9.8 2.2 %copy-start.1 = (bf16[256,8192]{1,0:T(8,128)(2,1)S(1)}, bf16[256,8192]{1,0:T(8,128)(2,1)}, u32[]{:S(2)}) copy-start(bf16[256,8192]{1,0:T(8,128)(2,1)} %ham_ref.1) | copy-start | bytes 12582916
  20.0 16.0 %collective-permute-start.2 = (bf16[32,8192]{1,0:T(8,128)(2,1)S(1)}, bf16[32,8192]{1,0:T(8,128)(2,1)S(1)}, u32[]{:S(2)}, u32[]{:S(2)}) collective-permute-start(bf16[32,8192]{1,0:T(8,128)(2,1)S(1)} %bitcast.26), channel_id=1, source_target_pairs={{0,16},{16,32},{32,48},{48,64},{64,80},{80,96},{96,112},{112,0},{1... | collective-permute-start | bytes 1572872 | tf_op jit(solution)/shard_map/ppermute | solution.py:290
  21.6 14.4 %collective-permute-start.3 = (bf16[32,8192]{1,0:T(8,128)(2,1)S(1)}, bf16[32,8192]{1,0:T(8,128)(2,1)S(1)}, u32[]{:S(2)}, u32[]{:S(2)}) collective-permute-start(bf16[32,8192]{1,0:T(8,128)(2,1)S(1)} %bitcast.27), channel_id=1, source_target_pairs={{0,112},{16,0},{32,16},{48,32},{64,48},{80,64},{96,80},{112,96},{1... | collective-permute-start | bytes 1572872 | tf_op jit(solution)/shard_map/ppermute | solution.py:290
  25.6 12.8 %collective-permute-start.4 = (bf16[256,1024]{1,0:T(8,128)(2,1)}, bf16[256,1024]{1,0:T(8,128)(2,1)S(1)}, u32[]{:S(2)}, u32[]{:S(2)}) collective-permute-start(bf16[256,1024]{1,0:T(8,128)(2,1)} %copy-done.6), channel_id=1, source_target_pairs={{0,128},{128,4},{4,132},{132,0},{1,129},{129,5},{5,133},{133,1},{2... | collective-permute-start | bytes 1572872 | tf_op jit(solution)/shard_map/ppermute | solution.py:298
  25.9 12.5 %collective-permute-start.5 = (bf16[256,1024]{1,0:T(8,128)(2,1)S(1)}, bf16[256,1024]{1,0:T(8,128)(2,1)S(1)}, u32[]{:S(2)}, u32[]{:S(2)}) collective-permute-start(bf16[256,1024]{1,0:T(8,128)(2,1)S(1)} %get-tuple-element.53), channel_id=1, source_target_pairs={{0,132},{128,0},{4,128},{132,4},{1,133},{129,1},{5,129},{133,5},{2... | collective-permute-start | bytes 1572872 | tf_op jit(solution)/shard_map/ppermute | solution.py:298
  38.3 19.6 %collective-permute-start.6 = (bf16[32,8192]{1,0:T(8,128)(2,1)S(1)}, bf16[32,8192]{1,0:T(8,128)(2,1)S(1)}, u32[]{:S(2)}, u32[]{:S(2)}) collective-permute-start(bf16[32,8192]{1,0:T(8,128)(2,1)S(1)} %collective-permute-done.2.p1), channel_id=1, source_target_pairs={{0,16},{16,32},{32,48},{48,64},{64,80},{80,96},{96,112},{112,0},{1... | collective-permute-start | bytes 1572872 | tf_op jit(solution)/shard_map/ppermute | solution.py:290
  38.3 19.6 %collective-permute-start.7 = (bf16[32,8192]{1,0:T(8,128)(2,1)S(1)}, bf16[32,8192]{1,0:T(8,128)(2,1)S(1)}, u32[]{:S(2)}, u32[]{:S(2)}) collective-permute-start(bf16[32,8192]{1,0:T(8,128)(2,1)S(1)} %collective-permute-done.3.m1), channel_id=1, source_target_pairs={{0,112},{16,0},{32,16},{48,32},{64,48},{80,64},{96,80},{112,96},{1... | collective-permute-start | bytes 1572872 | tf_op jit(solution)/shard_map/ppermute | solution.py:290
  41.0 16.9 %collective-permute-start.8 = (bf16[256,1024]{1,0:T(8,128)(2,1)S(1)}, bf16[256,1024]{1,0:T(8,128)(2,1)S(1)}, u32[]{:S(2)}, u32[]{:S(2)}) collective-permute-start(bf16[256,1024]{1,0:T(8,128)(2,1)S(1)} %collective-permute-done.4.f0), channel_id=1, source_target_pairs={{0,1},{1,2},{2,3},{3,0},{4,5},{5,6},{6,7},{7,4},{8,9},{9,10},{10,1... | collective-permute-start | bytes 1572872 | tf_op jit(solution)/shard_map/ppermute | solution.py:303
  43.8 24.5 %collective-permute-start.12 = (bf16[256,2048]{1,0:T(8,128)(2,1)S(1)}, bf16[256,2048]{1,0:T(8,128)(2,1)S(1)}, u32[]{:S(2)}, u32[]{:S(2)}) collective-permute-start(bf16[256,2048]{1,0:T(8,128)(2,1)S(1)} %get-tuple-element.68), channel_id=1, source_target_pairs={{0,128},{128,4},{4,132},{132,0},{1,129},{129,5},{5,133},{133,1},{2... | collective-permute-start | bytes 3145736 | tf_op jit(solution)/shard_map/ppermute | solution.py:298
  43.8 24.5 %collective-permute-start.13 = (bf16[256,2048]{1,0:T(8,128)(2,1)S(1)}, bf16[256,2048]{1,0:T(8,128)(2,1)S(1)}, u32[]{:S(2)}, u32[]{:S(2)}) collective-permute-start(bf16[256,2048]{1,0:T(8,128)(2,1)S(1)} %get-tuple-element.69), channel_id=1, source_target_pairs={{0,132},{128,0},{4,128},{132,4},{1,133},{129,1},{5,129},{133,5},{2... | collective-permute-start | bytes 3145736 | tf_op jit(solution)/shard_map/ppermute | solution.py:298
  46.5 2.2 %copy-start.2 = (bf16[256,8192]{1,0:T(8,128)(2,1)S(1)}, bf16[256,8192]{1,0:T(8,128)(2,1)}, u32[]{:S(2)}) copy-start(bf16[256,8192]{1,0:T(8,128)(2,1)} %ham_ref.1) | copy-start | bytes 12582916
  57.9 10.4 %collective-permute-start.10 = (bf16[32,8192]{1,0:T(8,128)(2,1)S(1)}, bf16[32,8192]{1,0:T(8,128)(2,1)S(1)}, u32[]{:S(2)}, u32[]{:S(2)}) collective-permute-start(bf16[32,8192]{1,0:T(8,128)(2,1)S(1)} %collective-permute-done.7.m2), channel_id=1, source_target_pairs={{0,112},{16,0},{32,16},{48,32},{64,48},{80,64},{96,80},{112,96},{1... | collective-permute-start | bytes 1572872 | tf_op jit(solution)/shard_map/ppermute | solution.py:290
  58.0 10.3 %collective-permute-start.11 = (bf16[256,1024]{1,0:T(8,128)(2,1)S(1)}, bf16[256,1024]{1,0:T(8,128)(2,1)S(1)}, u32[]{:S(2)}, u32[]{:S(2)}) collective-permute-start(bf16[256,1024]{1,0:T(8,128)(2,1)S(1)} %collective-permute-done.5.f2), channel_id=1, source_target_pairs={{0,3},{1,0},{2,1},{3,2},{4,7},{5,4},{6,5},{7,6},{8,11},{9,8},{10,9... | collective-permute-start | bytes 1572872 | tf_op jit(solution)/shard_map/ppermute | solution.py:303
  58.1 10.2 %collective-permute-start.9 = (bf16[32,8192]{1,0:T(8,128)(2,1)S(1)}, bf16[32,8192]{1,0:T(8,128)(2,1)S(1)}, u32[]{:S(2)}, u32[]{:S(2)}) collective-permute-start(bf16[32,8192]{1,0:T(8,128)(2,1)S(1)} %collective-permute-done.6.p2), channel_id=1, source_target_pairs={{0,16},{16,32},{32,48},{48,64},{64,80},{80,96},{96,112},{112,0},{1... | collective-permute-start | bytes 1572872 | tf_op jit(solution)/shard_map/ppermute | solution.py:290
  68.4 16.1 %collective-permute-start.16 = (bf16[256,1024]{1,0:T(8,128)(2,1)S(1)}, bf16[256,1024]{1,0:T(8,128)(2,1)S(1)}, u32[]{:S(2)}, u32[]{:S(2)}) collective-permute-start(bf16[256,1024]{1,0:T(8,128)(2,1)S(1)} %collective-permute-done.4.f0), channel_id=1, source_target_pairs={{0,8},{8,0},{1,9},{9,1},{2,10},{10,2},{3,11},{11,3},{4,12},{12,4},... | collective-permute-start | bytes 1572872 | tf_op jit(solution)/shard_map/ppermute | solution.py:285
  73.9 13.6 %collective-permute-start.20 = (bf16[256,2048]{1,0:T(8,128)(2,1)S(1)}, bf16[256,2048]{1,0:T(8,128)(2,1)S(1)}, u32[]{:S(2)}, u32[]{:S(2)}) collective-permute-start(bf16[256,2048]{1,0:T(8,128)(2,1)S(1)} %collective-permute-done.12.fa), channel_id=1, source_target_pairs={{0,8},{8,0},{1,9},{9,1},{2,10},{10,2},{3,11},{11,3},{4,12},{12,4},... | collective-permute-start | bytes 3145736 | tf_op jit(solution)/shard_map/ppermute | solution.py:285
  74.0 13.5 %collective-permute-start.21 = (bf16[256,2048]{1,0:T(8,128)(2,1)S(1)}, bf16[256,2048]{1,0:T(8,128)(2,1)S(1)}, u32[]{:S(2)}, u32[]{:S(2)}) collective-permute-start(bf16[256,2048]{1,0:T(8,128)(2,1)S(1)} %collective-permute-done.13.fb), channel_id=1, source_target_pairs={{0,8},{8,0},{1,9},{9,1},{2,10},{10,2},{3,11},{11,3},{4,12},{12,4},... | collective-permute-start | bytes 3145736 | tf_op jit(solution)/shard_map/ppermute | solution.py:285
  74.5 9.2 %collective-permute-start.14 = (bf16[16,8192]{1,0:T(8,128)(2,1)S(1)}, bf16[16,8192]{1,0:T(8,128)(2,1)S(1)}, u32[]{:S(2)}, u32[]{:S(2)}) collective-permute-start(bf16[16,8192]{1,0:T(8,128)(2,1)S(1)} %shard_map.80), channel_id=1, source_target_pairs={{0,16},{16,32},{32,48},{48,64},{64,80},{80,96},{96,112},{112,0},{1... | collective-permute-start | bytes 786440 | tf_op jit(solution)/shard_map/ppermute | solution.py:290
  74.6 9.9 %collective-permute-start.15 = (bf16[16,8192]{1,0:T(8,128)(2,1)S(1)}, bf16[16,8192]{1,0:T(8,128)(2,1)S(1)}, u32[]{:S(2)}, u32[]{:S(2)}) collective-permute-start(bf16[16,8192]{1,0:T(8,128)(2,1)S(1)} %shard_map.81), channel_id=1, source_target_pairs={{0,112},{16,0},{32,16},{48,32},{64,48},{80,64},{96,80},{112,96},{1... | collective-permute-start | bytes 786440 | tf_op jit(solution)/shard_map/ppermute | solution.py:290
  83.6 2.4 %collective-permute-start.17 = (bf16[256,1024]{1,0:T(8,128)(2,1)S(1)}, bf16[256,1024]{1,0:T(8,128)(2,1)S(1)}, u32[]{:S(2)}, u32[]{:S(2)}) collective-permute-start(bf16[256,1024]{1,0:T(8,128)(2,1)S(1)} %collective-permute-done.5.f2), channel_id=1, source_target_pairs={{0,8},{8,0},{1,9},{9,1},{2,10},{10,2},{3,11},{11,3},{4,12},{12,4},... | collective-permute-start | bytes 1572872 | tf_op jit(solution)/shard_map/ppermute | solution.py:285
  84.5 2.3 %collective-permute-start.18 = (bf16[256,1024]{1,0:T(8,128)(2,1)S(1)}, bf16[256,1024]{1,0:T(8,128)(2,1)S(1)}, u32[]{:S(2)}, u32[]{:S(2)}) collective-permute-start(bf16[256,1024]{1,0:T(8,128)(2,1)S(1)} %collective-permute-done.8.g0), channel_id=1, source_target_pairs={{0,8},{8,0},{1,9},{9,1},{2,10},{10,2},{3,11},{11,3},{4,12},{12,4},... | collective-permute-start | bytes 1572872 | tf_op jit(solution)/shard_map/ppermute | solution.py:285
  84.5 3.0 %collective-permute-start.19 = (bf16[256,1024]{1,0:T(8,128)(2,1)S(1)}, bf16[256,1024]{1,0:T(8,128)(2,1)S(1)}, u32[]{:S(2)}, u32[]{:S(2)}) collective-permute-start(bf16[256,1024]{1,0:T(8,128)(2,1)S(1)} %collective-permute-done.11.g2), channel_id=1, source_target_pairs={{0,8},{8,0},{1,9},{9,1},{2,10},{10,2},{3,11},{11,3},{4,12},{12,4},... | collective-permute-start | bytes 1572872 | tf_op jit(solution)/shard_map/ppermute | solution.py:285
  127.5 8.1 %copy-start.8 = (s32[16,8192]{1,0:T(8,128)S(1)}, s32[16,8192]{1,0:T(8,128)}, u32[]{:S(2)}) copy-start(s32[16,8192]{1,0:T(8,128)} %param.9) | copy-start | bytes 1572868
  127.5 8.1 %copy-start.9 = (f32[16]{0:T(128)S(1)}, f32[16]{0:T(128)}, u32[]{:S(2)}) copy-start(f32[16]{0:T(128)} %param.10) | copy-start | bytes 196
  129.1 34.5 %all-to-all-start.2 = ((f32[32,136,128]{2,1,0:T(8,128)}), f32[32,136,128]{2,1,0:T(8,128)S(1)}, u32[]{:S(2)}, u32[]{:S(2)}) async-start(f32[32,136,128]{2,1,0:T(8,128)} %shard_map.83), calls=%async_computation.2 | async-start | bytes 4456448 | tf_op jit(solution)/shard_map/all_to_all | solution.py:307
  135.6 0.8 copy-start.7
  163.6 1.0 copy-start.3
  (2 other events, 1.5 us)

commit v7 on v5

--- a/solution.py
+++ b/solution.py
@@ -53,49 +53,51 @@
     )(ham, tile_mask)
 
 
-def product_kernel(
-    place_ref, c0, p1, p2, p3, m1, m2, m3, top, low,
-    own_a, own_b, pair_a, pair_b, far_a, far_b, cross_a, cross_b,
-    turn_ref, home_ref, lhs, acc, local,
-):
-    xlo, z, core = place_ref[0], place_ref[1], place_ref[2]
-    strings = c0.shape[1]
-    blocks = ((0, c0), (-1, p1), (-2, p2), (-3, p3), (1, m1), (2, m2), (3, m3))
+def collect(z, blocks, at, width, out_ref):
+    c0, p1, p2, p3, m1, m2, m3, top, low = blocks
+    for offset, ref in ((0, c0), (-1, p1), (-2, p2), (-3, p3), (1, m1), (2, m2), (3, m3)):
+        row = pl.multiple_of(lax.rem(z + offset + 8, 8) * 32, 32)
+        out_ref[pl.ds(row, 32), :] = ref[:, pl.ds(at, width)]
+    row = pl.multiple_of(lax.rem(z + 4, 8) * 32, 32)
+    out_ref[pl.ds(row, 16), :] = top[:, pl.ds(at, width)]
+    out_ref[pl.ds(pl.multiple_of(row + 16, 16), 16), :] = low[:, pl.ds(at, width)]
+
+
+def accumulate(z, core, blocks, panels, lhs, acc):
+    width = panels[0].shape[1]
     acc[...] = jnp.zeros_like(acc)
-
-    def gather(at, width, out):
-        for offset, ref in blocks:
-            row = pl.multiple_of(lax.rem(z + offset + 8, 8) * 32, 32)
-            out[pl.ds(row, 32), :] = ref[:, pl.ds(at, width)]
-        row = pl.multiple_of(lax.rem(z + 4, 8) * 32, 32)
-        out[pl.ds(row, 16), :] = top[:, pl.ds(at, width)]
-        out[pl.ds(pl.multiple_of(row + 16, 16), 16), :] = low[:, pl.ds(at, width)]
-
-    for start, panels in (
-        (0, (own_a, pair_a, far_a, cross_a)),
-        (strings // 2, (own_b, pair_b, far_b, cross_b)),
-    ):
-
-        def step(index, carry, start=start, panels=panels):
-            at = pl.multiple_of(index * CHUNK, CHUNK)
-            gather(pl.multiple_of(start + at, CHUNK), CHUNK, lhs)
-            for number, ref in enumerate(panels):
-                side = xlo if number < 2 else 1 - xlo
-                other = core if number % 2 == 0 else 1 - core
-                columns = pl.ds(pl.multiple_of((side * 2 + other) * 256, 256), 256)
+    for half in range(2):
+        for at in range(0, width, CHUNK):
+            collect(z, blocks, half * width + at, CHUNK, lhs)
+            for number in range(2):
+                ref = panels[2 * number + half]
+                other = core if number == 0 else 1 - core
+                columns = pl.ds(pl.multiple_of(other * 256, 256), 256)
                 acc[:, columns] += lax.dot_general(
                     lhs[...],
-                    ref[:, pl.ds(at, CHUNK)],
+                    ref[:, at : at + CHUNK],
                     (((1,), (1,)), ((), ())),
                     preferred_element_type=jnp.float32,
                 )
-            return carry
-
-        lax.fori_loop(0, strings // 2 // CHUNK, step, 0)
+
+
+def near_kernel(place_ref, *refs):
+    blocks, panels, (out_ref, lhs) = refs[:9], refs[9:13], refs[13:]
+    accumulate(place_ref[1], place_ref[2], blocks, panels, lhs, out_ref)
+
+
+def product_kernel(place_ref, *refs):
+    blocks, panels, near_ref = refs[:9], refs[9:13], refs[13]
+    turn_ref, home_ref, lhs, far, acc, local = refs[14:]
+    xlo, z, core = place_ref[0], place_ref[1], place_ref[2]
+    strings = blocks[0].shape[1]
+    accumulate(z, core, blocks, panels, lhs, far)
+    acc[:, pl.ds(pl.multiple_of(xlo * 512, 512), 512)] = near_ref[...]
+    acc[:, pl.ds(pl.multiple_of((1 - xlo) * 512, 512), 512)] = far[...]
 
     for side in range(2):
         at = pl.multiple_of(side * (strings // 2) + z * 512, 512)
-        gather(at, 512, local.at[:, side * 512 : side * 512 + 512])
+        collect(z, blocks, at, 512, local.at[:, side * 512 : side * 512 + 512])
 
     coeff = local[...].astype(jnp.float32)
     projection = jnp.sum(2.0 * coeff * acc[...])
@@ -121,15 +123,30 @@
                 ]
 
 
-def multiply(place, blocks, halves):
-    strings = blocks[0].shape[1]
+def multiply_near(place, blocks, panels):
     vmem = pl.BlockSpec(memory_space=pltpu.VMEM)
     return pl.pallas_call(
+        near_kernel,
+        in_specs=[pl.BlockSpec(memory_space=pltpu.SMEM)] + [vmem] * (len(blocks) + len(panels)),
+        out_specs=vmem,
+        scratch_shapes=[pltpu.VMEM((256, CHUNK), jnp.bfloat16)],
+        out_shape=jax.ShapeDtypeStruct((256, 512), jnp.float32),
+        compiler_params=pltpu.CompilerParams(vmem_limit_bytes=20 * MIB),
+        cost_estimate=pl.CostEstimate(
+            flops=2 * 256 * 512 * NS, bytes_accessed=12 * MIB, transcendentals=0
+        ),
+    )(place, *blocks, *panels)
+
+
+def multiply(place, blocks, panels, near):
+    vmem = pl.BlockSpec(memory_space=pltpu.VMEM)
+    return pl.pallas_call(
         product_kernel,
-        in_specs=[pl.BlockSpec(memory_space=pltpu.SMEM)] + [vmem] * (len(blocks) + len(halves)),
+        in_specs=[pl.BlockSpec(memory_space=pltpu.SMEM)] + [vmem] * (len(blocks) + len(panels) + 1),
         out_specs=[vmem, vmem],
         scratch_shapes=[
             pltpu.VMEM((256, CHUNK), jnp.bfloat16),
+            pltpu.VMEM((256, 512), jnp.float32),
             pltpu.VMEM((256, 1024), jnp.float32),
             pltpu.VMEM((256, 1024), jnp.bfloat16),
         ],
@@ -137,11 +154,11 @@
             jax.ShapeDtypeStruct((8, 264, LANES), jnp.float32),
             jax.ShapeDtypeStruct((32, 64, LANES), jnp.float32),
         ],
-        compiler_params=pltpu.CompilerParams(vmem_limit_bytes=30 * MIB),
+        compiler_params=pltpu.CompilerParams(vmem_limit_bytes=24 * MIB),
         cost_estimate=pl.CostEstimate(
-            flops=2 * 256 * 1024 * strings, bytes_accessed=24 * MIB, transcendentals=0
+            flops=2 * 256 * 512 * NS, bytes_accessed=16 * MIB, transcendentals=0
         ),
-    )(place, *blocks, *halves)
+    )(place, *blocks, *panels, near)
 
 
 def split_kernel(value_ref, out_ref, start):
@@ -287,21 +304,20 @@
     p1, m1, pair, pair_mask = lax.optimization_barrier(
         (shift(block, 1), shift(block, -1), pair, pair_mask)
     )
-    pair_a, pair_b = mask_half(pair, pair_mask, 0), mask_half(pair, pair_mask, 1)
-    p2, m2, pair_a, pair_b = lax.optimization_barrier(
-        (shift(p1, 1), shift(m1, -1), pair_a, pair_b)
-    )
+    pair_a = mask_half(pair, pair_mask, 0)
+    p2, m2, pair_a = lax.optimization_barrier((shift(p1, 1), shift(m1, -1), pair_a))
     p3, m3 = shift(p2, 1), shift(m2, -1)
     top, low = take_rows(p3, 0), take_rows(m3, 16)
-    _, _, far_a, far_b = lax.optimization_barrier((top, low, far_a, far_b))
-    top, low = shift(top, 1), shift(low, -1)
+    top, low, pair, pair_mask = lax.optimization_barrier((top, low, pair, pair_mask))
+    pair_b = mask_half(pair, pair_mask, 1)
+    top, low, pair_b, far_a, far_b = lax.optimization_barrier(
+        (shift(top, 1), shift(low, -1), pair_b, far_a, far_b)
+    )
     cross_a, cross_b = swap(far_a), swap(far_b)
 
-    turn, home = multiply(
-        place,
-        (block, p1, p2, p3, m1, m2, m3, top, low),
-        (own_a, own_b, pair_a, pair_b, far_a, far_b, cross_a, cross_b),
-    )
+    blocks = (block, p1, p2, p3, m1, m2, m3, top, low)
+    near = multiply_near(place, blocks, (own_a, own_b, pair_a, pair_b))
+    turn, home = multiply(place, blocks, (far_a, far_b, cross_a, cross_b), near)
 
     tiles = exchange(pack(exchange(turn, "z"), home), PLANE)
 

time: 184 us -> 180 us (0.978)
  waiting for transfers between devices: 61.3 us -> 57.1 us
  blocking collectives: 50.8 us -> 53.4 us
    ppermute x2, waiting for transfers between devices: 6.01 us -> 0.01 us  [shift_x(): return lax.ppermute(value, ('xlo', 'xhi'), pairs)]
    pallas_call x1, Pallas kernels: 7.56 us -> 3.66 us  [multiply(): pl.pallas_call(product_kernel, in_specs=[pl.BlockSpec(memory_space=pltpu....]
    ppermute x4, starting transfers between devices: 6.31 us -> 10.2 us  [swap(): return lax.ppermute(value, 'core', [(0, 1), (1, 0)])]
    ppermute x4, waiting for transfers between devices: 0.01 us -> 3.4 us  [swap(): return lax.ppermute(value, 'core', [(0, 1), (1, 0)])]
    pallas_call x0 -> x1, Pallas kernels: none -> 3.11 us  [multiply_near(): pl.pallas_call(near_kernel, in_specs=[pl.BlockSpec(memory_space=pltpu.SME...]
    ppermute x8, starting transfers between devices: 16.5 us -> 13.7 us  [shift(): lax.ppermute(value, 'z', [(i, (i + step) % count) for i in range(count)])]
    all_to_all x2, blocking collectives: 50.8 us -> 53.4 us  [exchange(): return lax.all_to_all(value, axes, split_axis=0, concat_axis=0, tiled=True)]
    all_to_all x2, starting transfers between devices: 16.2 us -> 14.3 us  [exchange(): return lax.all_to_all(value, axes, split_axis=0, concat_axis=0, tiled=True)]
  transfers between devices with their start and end apart: 16 -> 16, of which waited for: 7 -> 8; matrix products, arithmetic and copies ran while one was open for 1% -> 1% of each run, Pallas kernels for 5% -> 7%
where the time goes in v7:
time: 180 us
  waiting for transfers between devices  57.1 us (32%)
  blocking collectives  53.4 us (30%)
  starting transfers between devices  40.8 us (23%)
  Pallas kernels  19.2 us (11%)
  local copies, waits for them, and re-layouts  5.86 us (3%)
  matrix products  2.52 us (1%)
    all_to_all x2, blocking collectives, exchange(): return lax.all_to_all(value, axes, split_axis=0, concat_axis=0, tiled=True)  53.4 us
    all_to_all x2, waiting for transfers between devices, exchange(): return lax.all_to_all(value, axes, split_axis=0, concat_axis=0, tiled=True)  28.5 us
    ppermute x8, waiting for transfers between devices, shift(): lax.ppermute(value, 'z', [(i, (i + step) % count) for i in range(count)])  25.2 us
    all_to_all x2, starting transfers between devices, exchange(): return lax.all_to_all(value, axes, split_axis=0, concat_axis=0, tiled=True)  14.3 us
    ppermute x8, starting transfers between devices, shift(): lax.ppermute(value, 'z', [(i, (i + step) % count) for i in range(count)])  13.7 us
    ppermute x4, starting transfers between devices, swap(): return lax.ppermute(value, 'core', [(0, 1), (1, 0)])  10.2 us
    pallas_call x4, Pallas kernels, mask_half(): pl.pallas_call(mask_kernel, grid=(4,), in_specs=[pl.BlockSpec((rows, cols...  8.86 us
    unnamed x20, local copies, waits for them, and re-layouts  5.35 us
  transfers between devices with their start and end apart: 16, of which 8 were waited for; matrix products, arithmetic and copies ran while one was open for 1% of the time, Pallas kernels for 7%

profile of v7, /device:TPU:1, one launch (start us, length us, event | category | flops | bytes accessed | tf_op | source)
XLA Modules:
  0.0 179.8 jit_solution(1191601358312530270)
XLA Ops:
  0.7 3.3 %collective-permute-start = (bf16[256,8192]{1,0:T(8,128)(2,1)}, bf16[256,8192]{1,0:T(8,128)(2,1)}, u32[]{:S(2)}, u32[]{:S(2)}) collective-permute-start(bf16[256,8192]{1,0:T(8,128)(2,1)} %ham_ref.1), channel_id=1, source_target_pairs={{0,8},{8,0},{1,9},{9,1},{2,10},{10,2},{3,11},{11,3},{4,12},{12,4},... | collective-permute-start | bytes 12582920 | tf_op jit(solution)/shard_map/ppermute | solution.py:264
  4.0 5.5 %all-to-all-start = ((bf16[32,8,1024]{2,1,0:T(8,128)(2,1)}), bf16[32,8,1024]{2,1,0:T(8,128)(2,1)S(1)}, u32[]{:S(2)}, u32[]{:S(2)}) async-start(bf16[32,8,1024]{2,1,0:T(8,128)(2,1)} %bitcast.29), calls=%async_computation | async-start | bytes 1048576 | tf_op jit(solution)/shard_map/all_to_all | solution.py:281
  9.8 2.2 %copy-done.1 = bf16[256,8192]{1,0:T(8,128)(2,1)S(1)} copy-done((bf16[256,8192]{1,0:T(8,128)(2,1)S(1)}, bf16[256,8192]{1,0:T(8,128)(2,1)}, u32[]{:S(2)}) %copy-start.1) | copy-done | bytes 4194328
  12.7 1.4 shard_map.77.refs_9_
  14.1 1.4 shard_map.78.refs_10_
  15.5 1.4 copy-done.2
  16.8 3.1 %all-to-all-done = bf16[32,8,1024]{2,1,0:T(8,128)(2,1)S(1)} async-done(((bf16[32,8,1024]{2,1,0:T(8,128)(2,1)}), bf16[32,8,1024]{2,1,0:T(8,128)(2,1)S(1)}, u32[]{:S(2)}, u32[]{:S(2)}) %all-to-all-start) | async-done | bytes 524320 | tf_op jit(solution)/shard_map/all_to_all | solution.py:281
  20.3 2.4 %collective-permute-start.11 = (bf16[256,4096]{1,0:T(8,128)(2,1)}, bf16[256,4096]{1,0:T(8,128)(2,1)S(1)}, u32[]{:S(2)}, u32[]{:S(2)}) collective-permute-start(bf16[256,4096]{1,0:T(8,128)(2,1)} %copy-done.2), channel_id=1, source_target_pairs={{0,132},{128,0},{4,128},{132,4},{1,133},{129,1},{5,129},{133,5},{2... | collective-permute-start | bytes 6291464 | tf_op jit(solution)/shard_map/ppermute | solution.py:277
  22.6 1.6 collective-permute-start.2
  24.3 3.9 %collective-permute-start.3 = (bf16[32,8192]{1,0:T(8,128)(2,1)S(1)}, bf16[32,8192]{1,0:T(8,128)(2,1)S(1)}, u32[]{:S(2)}, u32[]{:S(2)}) collective-permute-start(bf16[32,8192]{1,0:T(8,128)(2,1)S(1)} %bitcast.26), channel_id=1, source_target_pairs={{0,112},{16,0},{32,16},{48,32},{64,48},{80,64},{96,80},{112,96},{1... | collective-permute-start | bytes 1572872 | tf_op jit(solution)/shard_map/ppermute | solution.py:269
  28.2 9.9 %collective-permute-done.2.refs_1_ = bf16[32,8192]{1,0:T(8,128)(2,1)S(1)} collective-permute-done((bf16[32,8192]{1,0:T(8,128)(2,1)S(1)}, bf16[32,8192]{1,0:T(8,128)(2,1)S(1)}, u32[]{:S(2)}, u32[]{:S(2)}) %collective-permute-start.2) | collective-permute-done | bytes 524320 | tf_op jit(solution)/shard_map/ppermute | solution.py:269
  38.1 2.7 %collective-permute-start.5 = (bf16[32,8192]{1,0:T(8,128)(2,1)S(1)}, bf16[32,8192]{1,0:T(8,128)(2,1)S(1)}, u32[]{:S(2)}, u32[]{:S(2)}) collective-permute-start(bf16[32,8192]{1,0:T(8,128)(2,1)S(1)} %collective-permute-done.3.refs_4_), channel_id=1, source_target_pairs={{0,112},{16,0},{32,16},{48,32},{64,48},{80,64},{96,80},{112,96},{1... | collective-permute-start | bytes 1572872 | tf_op jit(solution)/shard_map/ppermute | solution.py:269
  40.8 3.0 %shard_map.79.refs_11_ = bf16[256,4096]{1,0:T(8,128)(2,1)S(1)} custom-call(bf16[256,8192]{1,0:T(8,128)(2,1)} %collective-permute-done.ham_ref, s32[8,256]{1,0:T(8,128)S(1)} %collective-permute-done.1.mask_ref), custom_call_target="tpu_custom_call" | custom-call | flops 2097152 | bytes 4194304 | tf_op jit(solution)/shard_map/pallas_call | solution.py:40
  43.8 5.9 %collective-permute-done.4.refs_2_ = bf16[32,8192]{1,0:T(8,128)(2,1)S(1)} collective-permute-done((bf16[32,8192]{1,0:T(8,128)(2,1)S(1)}, bf16[32,8192]{1,0:T(8,128)(2,1)S(1)}, u32[]{:S(2)}, u32[]{:S(2)}) %collective-permute-start.4) | collective-permute-done | bytes 524320 | tf_op jit(solution)/shard_map/ppermute | solution.py:269
  49.7 1.1 collective-permute-start.6
  50.8 1.6 collective-permute-start.7
  52.4 8.0 %collective-permute-done.6.value_ref.refs_3_ = bf16[32,8192]{1,0:T(8,128)(2,1)S(1)} collective-permute-done((bf16[32,8192]{1,0:T(8,128)(2,1)S(1)}, bf16[32,8192]{1,0:T(8,128)(2,1)S(1)}, u32[]{:S(2)}, u32[]{:S(2)}) %collective-permute-start.6) | collective-permute-done | bytes 524320 | tf_op jit(solution)/shard_map/ppermute | solution.py:269
  61.1 2.2 %collective-permute-start.9 = (bf16[16,8192]{1,0:T(8,128)(2,1)S(1)}, bf16[16,8192]{1,0:T(8,128)(2,1)S(1)}, u32[]{:S(2)}, u32[]{:S(2)}) collective-permute-start(bf16[16,8192]{1,0:T(8,128)(2,1)S(1)} %shard_map.81), channel_id=1, source_target_pairs={{0,112},{16,0},{32,16},{48,32},{64,48},{80,64},{96,80},{112,96},{1... | collective-permute-start | bytes 786440 | tf_op jit(solution)/shard_map/ppermute | solution.py:269
  63.3 3.0 %shard_map.82.refs_12_ = bf16[256,4096]{1,0:T(8,128)(2,1)S(1)} custom-call(bf16[256,8192]{1,0:T(8,128)(2,1)} %collective-permute-done.ham_ref, s32[8,256]{1,0:T(8,128)S(1)} %collective-permute-done.1.mask_ref), custom_call_target="tpu_custom_call" | custom-call | flops 2097152 | bytes 4194304 | tf_op jit(solution)/shard_map/pallas_call | solution.py:40
  66.3 1.4 collective-permute-done.8.refs_7_
  67.7 6.3 %collective-permute-start.12 = (bf16[256,4096]{1,0:T(8,128)(2,1)S(1)}, bf16[256,4096]{1,0:T(8,128)(2,1)S(1)}, u32[]{:S(2)}, u32[]{:S(2)}) collective-permute-start(bf16[256,4096]{1,0:T(8,128)(2,1)S(1)} %collective-permute-done.10.refs_9_), channel_id=1, source_target_pairs={{0,8},{8,0},{1,9},{9,1},{2,10},{10,2},{3,11},{11,3},{4,12},{12,4},... | collective-permute-start | bytes 6291464 | tf_op jit(solution)/shard_map/ppermute | solution.py:264
  74.3 3.1 %shard_map.83.refs_13_ = f32[256,512]{1,0:T(8,128)S(1)} custom-call(s32[3]{0:T(128)S(1)} %pad_add_fusion.place_ref, bf16[32,8192]{1,0:T(8,128)(2,1)S(1)} %bitcast.27, bf16[32,8192]{1,0:T(8,128)(2,1)S(1)} %collective-permute-done.2.refs_1_, bf16[32,8192]{1,0:T(8,128)(2,1)S(1)} %collective-permute-done.4.refs_2_, ...), custom_call_target="tpu_custom_call" | custom-call | flops 2147483648 | bytes 12582912 | tf_op jit(solution)/shard_map/pallas_call | solution.py:128
  77.8 3.0 %collective-permute-done.13.refs_12_ = bf16[256,4096]{1,0:T(8,128)(2,1)S(1)} collective-permute-done((bf16[256,4096]{1,0:T(8,128)(2,1)S(1)}, bf16[256,4096]{1,0:T(8,128)(2,1)S(1)}, u32[]{:S(2)}, u32[]{:S(2)}) %collective-permute-start.13) | collective-permute-done | bytes 2097184 | tf_op jit(solution)/shard_map/ppermute | solution.py:264
  80.8 3.7 %shard_map.84 = (f32[8,264,128]{2,1,0:T(8,128)S(1)}, f32[32,64,128]{2,1,0:T(8,128)S(1)}) custom-call(s32[3]{0:T(128)S(1)} %pad_add_fusion.place_ref, bf16[32,8192]{1,0:T(8,128)(2,1)S(1)} %bitcast.28, bf16[32,8192]{1,0:T(8,128)(2,1)S(1)} %collective-permute-done.2.refs_1_, bf16[32,8192]{1,0:T(8,128)(2,1)S(1)} %collective-permute-done.4.refs_2_, ...), custom_call_target="tpu_custom_call" | custom-call | flops 2147483648 | bytes 16777216 | tf_op jit(solution)/shard_map/pallas_call | solution.py:143
  84.5 33.7 %all_to_all.26.turn_ref = f32[8,264,128]{2,1,0:T(8,128)S(1)} all-to-all(f32[8,264,128]{2,1,0:T(8,128)S(1)} %get-tuple-element.55), channel_id=1, replica_groups=mesh['xlo'=2,'z'=8,'core'=2,'xhi'=2,'y'=4] {'z'}, dimensions={0} | all-to-all | bytes 2162688 | tf_op jit(solution)/shard_map/all_to_all | solution.py:281
  118.2 1.6 shard_map.85
  119.7 8.8 %all-to-all-start.2 = ((f32[32,136,128]{2,1,0:T(8,128)}), f32[32,136,128]{2,1,0:T(8,128)S(1)}, u32[]{:S(2)}, u32[]{:S(2)}) async-start(f32[32,136,128]{2,1,0:T(8,128)} %shard_map.85), calls=%async_computation.2 | async-start | bytes 4456448 | tf_op jit(solution)/shard_map/all_to_all | solution.py:281
  129.4 1.8 %convolution_add_fusion.diag_ref = f32[256,1024]{1,0:T(8,128)S(1)} fusion(f32[256,16]{1,0:T(8,128)S(1)} %fusion.3, f32[1024]{0:T(1024)S(1)} %bitcast.32, f32[256]{0:T(256)S(1)} %bitcast.33, f32[16,8192]{1,0:T(8,128)} %copy-done.7, s32[]{:T(128)S(6)} %select_n.7), kind=kOutput, calls=%fused_computation | convolution fusion | flops 50855936 | bytes 1135620 | tf_op jit(solution)/shard_map/dot_general | solution.py:329
  131.3 25.3 %all-to-all-done.2.tiles_ref = f32[32,136,128]{2,1,0:T(8,128)S(1)} async-done(((f32[32,136,128]{2,1,0:T(8,128)}), f32[32,136,128]{2,1,0:T(8,128)S(1)}, u32[]{:S(2)}, u32[]{:S(2)}) %all-to-all-start.2) | async-done | bytes 2228256 | tf_op jit(solution)/shard_map/all_to_all | solution.py:281
  156.6 1.0 copy-done.4
  158.4 19.7 %all_to_all.27 = f32[256,1,128]{2,1,0:T(1,128)S(1)} all-to-all(f32[256,1,128]{2,1,0:T(1,128)S(1)} %bitcast.31), channel_id=1, replica_groups=mesh['xlo'=2,'z'=8,'core'=2,'xhi'=2,'y'=4] {'xlo','z','core','xhi','y'}, dimensions={0} | all-to-all | bytes 262144 | tf_op jit(solution)/shard_map/all_to_all | solution.py:281
  178.1 1.2 shard_map.87
  (40 shorter events, 4.8 us)
Async XLA Ops:
  0.6 128.4 %copy-start = (f32[16,16]{1,0:T(8,128)S(1)}, f32[16,16]{1,0:T(8,128)}, u32[]{:S(2)}) copy-start(f32[16,16]{1,0:T(8,128)} %param.11) | copy-start | bytes 3076
  0.7 19.2 %collective-permute-start = (bf16[256,8192]{1,0:T(8,128)(2,1)}, bf16[256,8192]{1,0:T(8,128)(2,1)}, u32[]{:S(2)}, u32[]{:S(2)}) collective-permute-start(bf16[256,8192]{1,0:T(8,128)(2,1)} %ham_ref.1), channel_id=1, source_target_pairs={{0,8},{8,0},{1,9},{9,1},{2,10},{10,2},{3,11},{11,3},{4,12},{12,4},... | collective-permute-start | bytes 12582920 | tf_op jit(solution)/shard_map/ppermute | solution.py:264
  4.0 16.0 %all-to-all-start = ((bf16[32,8,1024]{2,1,0:T(8,128)(2,1)}), bf16[32,8,1024]{2,1,0:T(8,128)(2,1)S(1)}, u32[]{:S(2)}, u32[]{:S(2)}) async-start(bf16[32,8,1024]{2,1,0:T(8,128)(2,1)} %bitcast.29), calls=%async_computation | async-start | bytes 1048576 | tf_op jit(solution)/shard_map/all_to_all | solution.py:281
  9.5 7.4 %collective-permute-start.1 = (s32[8,256]{1,0:T(8,128)}, s32[8,256]{1,0:T(8,128)S(1)}, u32[]{:S(2)}, u32[]{:S(2)}) collective-permute-start(s32[8,256]{1,0:T(8,128)} %mask_ref.3), channel_id=1, source_target_pairs={{0,8},{8,0},{1,9},{9,1},{2,10},{10,2},{3,11},{11,3},{4,12},{12,4},... | collective-permute-start | bytes 24584 | tf_op jit(solution)/shard_map/ppermute | solution.py:264
  9.8 2.2 %copy-start.1 = (bf16[256,8192]{1,0:T(8,128)(2,1)S(1)}, bf16[256,8192]{1,0:T(8,128)(2,1)}, u32[]{:S(2)}) copy-start(bf16[256,8192]{1,0:T(8,128)(2,1)} %ham_ref.1) | copy-start | bytes 12582916
  12.0 0.7 copy-start.5
  12.7 1.4 copy-start.6
  15.5 1.4 copy-start.2
  20.0 47.7 %collective-permute-start.10 = (bf16[256,4096]{1,0:T(8,128)(2,1)S(1)}, bf16[256,4096]{1,0:T(8,128)(2,1)S(1)}, u32[]{:S(2)}, u32[]{:S(2)}) collective-permute-start(bf16[256,4096]{1,0:T(8,128)(2,1)S(1)} %shard_map.77.refs_9_), channel_id=1, source_target_pairs={{0,128},{128,4},{4,132},{132,0},{1,129},{129,5},{5,133},{133,1},{2... | collective-permute-start | bytes 6291464 | tf_op jit(solution)/shard_map/ppermute | solution.py:277
  20.3 47.4 %collective-permute-start.11 = (bf16[256,4096]{1,0:T(8,128)(2,1)}, bf16[256,4096]{1,0:T(8,128)(2,1)S(1)}, u32[]{:S(2)}, u32[]{:S(2)}) collective-permute-start(bf16[256,4096]{1,0:T(8,128)(2,1)} %copy-done.2), channel_id=1, source_target_pairs={{0,132},{128,0},{4,128},{132,4},{1,133},{129,1},{5,129},{133,5},{2... | collective-permute-start | bytes 6291464 | tf_op jit(solution)/shard_map/ppermute | solution.py:277
  22.6 15.5 %collective-permute-start.2 = (bf16[32,8192]{1,0:T(8,128)(2,1)S(1)}, bf16[32,8192]{1,0:T(8,128)(2,1)S(1)}, u32[]{:S(2)}, u32[]{:S(2)}) collective-permute-start(bf16[32,8192]{1,0:T(8,128)(2,1)S(1)} %bitcast.25), channel_id=1, source_target_pairs={{0,16},{16,32},{32,48},{48,64},{64,80},{80,96},{96,112},{112,0},{1... | collective-permute-start | bytes 1572872 | tf_op jit(solution)/shard_map/ppermute | solution.py:269
  24.3 13.8 %collective-permute-start.3 = (bf16[32,8192]{1,0:T(8,128)(2,1)S(1)}, bf16[32,8192]{1,0:T(8,128)(2,1)S(1)}, u32[]{:S(2)}, u32[]{:S(2)}) collective-permute-start(bf16[32,8192]{1,0:T(8,128)(2,1)S(1)} %bitcast.26), channel_id=1, source_target_pairs={{0,112},{16,0},{32,16},{48,32},{64,48},{80,64},{96,80},{112,96},{1... | collective-permute-start | bytes 1572872 | tf_op jit(solution)/shard_map/ppermute | solution.py:269
  38.1 11.6 %collective-permute-start.4 = (bf16[32,8192]{1,0:T(8,128)(2,1)S(1)}, bf16[32,8192]{1,0:T(8,128)(2,1)S(1)}, u32[]{:S(2)}, u32[]{:S(2)}) collective-permute-start(bf16[32,8192]{1,0:T(8,128)(2,1)S(1)} %collective-permute-done.2.refs_1_), channel_id=1, source_target_pairs={{0,16},{16,32},{32,48},{48,64},{64,80},{80,96},{96,112},{112,0},{1... | collective-permute-start | bytes 1572872 | tf_op jit(solution)/shard_map/ppermute | solution.py:269
  38.1 11.6 %collective-permute-start.5 = (bf16[32,8192]{1,0:T(8,128)(2,1)S(1)}, bf16[32,8192]{1,0:T(8,128)(2,1)S(1)}, u32[]{:S(2)}, u32[]{:S(2)}) collective-permute-start(bf16[32,8192]{1,0:T(8,128)(2,1)S(1)} %collective-permute-done.3.refs_4_), channel_id=1, source_target_pairs={{0,112},{16,0},{32,16},{48,32},{64,48},{80,64},{96,80},{112,96},{1... | collective-permute-start | bytes 1572872 | tf_op jit(solution)/shard_map/ppermute | solution.py:269
  49.7 10.7 %collective-permute-start.6 = (bf16[32,8192]{1,0:T(8,128)(2,1)S(1)}, bf16[32,8192]{1,0:T(8,128)(2,1)S(1)}, u32[]{:S(2)}, u32[]{:S(2)}) collective-permute-start(bf16[32,8192]{1,0:T(8,128)(2,1)S(1)} %collective-permute-done.4.refs_2_), channel_id=1, source_target_pairs={{0,16},{16,32},{32,48},{48,64},{64,80},{80,96},{96,112},{112,0},{1... | collective-permute-start | bytes 1572872 | tf_op jit(solution)/shard_map/ppermute | solution.py:269
  50.8 9.7 %collective-permute-start.7 = (bf16[32,8192]{1,0:T(8,128)(2,1)S(1)}, bf16[32,8192]{1,0:T(8,128)(2,1)S(1)}, u32[]{:S(2)}, u32[]{:S(2)}) collective-permute-start(bf16[32,8192]{1,0:T(8,128)(2,1)S(1)} %collective-permute-done.5.refs_5_), channel_id=1, source_target_pairs={{0,112},{16,0},{32,16},{48,32},{64,48},{80,64},{96,80},{112,96},{1... | collective-permute-start | bytes 1572872 | tf_op jit(solution)/shard_map/ppermute | solution.py:269
  60.5 13.8 %copy-start.3 = (bf16[256,4096]{1,0:T(8,128)(2,1)S(1)}, bf16[256,4096]{1,0:T(8,128)(2,1)}, u32[]{:S(2)}) copy-start(bf16[256,4096]{1,0:T(8,128)(2,1)} %copy-done.2) | copy-start | bytes 6291460
  60.5 7.2 %collective-permute-start.8 = (bf16[16,8192]{1,0:T(8,128)(2,1)S(1)}, bf16[16,8192]{1,0:T(8,128)(2,1)S(1)}, u32[]{:S(2)}, u32[]{:S(2)}) collective-permute-start(bf16[16,8192]{1,0:T(8,128)(2,1)S(1)} %shard_map.80), channel_id=1, source_target_pairs={{0,16},{16,32},{32,48},{48,64},{64,80},{80,96},{96,112},{112,0},{1... | collective-permute-start | bytes 786440 | tf_op jit(solution)/shard_map/ppermute | solution.py:269
  61.1 6.6 %collective-permute-start.9 = (bf16[16,8192]{1,0:T(8,128)(2,1)S(1)}, bf16[16,8192]{1,0:T(8,128)(2,1)S(1)}, u32[]{:S(2)}, u32[]{:S(2)}) collective-permute-start(bf16[16,8192]{1,0:T(8,128)(2,1)S(1)} %shard_map.81), channel_id=1, source_target_pairs={{0,112},{16,0},{32,16},{48,32},{64,48},{80,64},{96,80},{112,96},{1... | collective-permute-start | bytes 786440 | tf_op jit(solution)/shard_map/ppermute | solution.py:269
  67.7 10.1 %collective-permute-start.12 = (bf16[256,4096]{1,0:T(8,128)(2,1)S(1)}, bf16[256,4096]{1,0:T(8,128)(2,1)S(1)}, u32[]{:S(2)}, u32[]{:S(2)}) collective-permute-start(bf16[256,4096]{1,0:T(8,128)(2,1)S(1)} %collective-permute-done.10.refs_9_), channel_id=1, source_target_pairs={{0,8},{8,0},{1,9},{9,1},{2,10},{10,2},{3,11},{11,3},{4,12},{12,4},... | collective-permute-start | bytes 6291464 | tf_op jit(solution)/shard_map/ppermute | solution.py:264
  74.0 6.8 %collective-permute-start.13 = (bf16[256,4096]{1,0:T(8,128)(2,1)S(1)}, bf16[256,4096]{1,0:T(8,128)(2,1)S(1)}, u32[]{:S(2)}, u32[]{:S(2)}) collective-permute-start(bf16[256,4096]{1,0:T(8,128)(2,1)S(1)} %collective-permute-done.11.refs_10_), channel_id=1, source_target_pairs={{0,8},{8,0},{1,9},{9,1},{2,10},{10,2},{3,11},{11,3},{4,12},{12,4},... | collective-permute-start | bytes 6291464 | tf_op jit(solution)/shard_map/ppermute | solution.py:264
  119.7 8.9 %copy-start.8 = (s32[16,8192]{1,0:T(8,128)S(1)}, s32[16,8192]{1,0:T(8,128)}, u32[]{:S(2)}) copy-start(s32[16,8192]{1,0:T(8,128)} %param.9) | copy-start | bytes 1572868
  119.7 8.9 %copy-start.9 = (f32[16]{0:T(128)S(1)}, f32[16]{0:T(128)}, u32[]{:S(2)}) copy-start(f32[16]{0:T(128)} %param.10) | copy-start | bytes 196
  119.7 36.9 %all-to-all-start.2 = ((f32[32,136,128]{2,1,0:T(8,128)}), f32[32,136,128]{2,1,0:T(8,128)S(1)}, u32[]{:S(2)}, u32[]{:S(2)}) async-start(f32[32,136,128]{2,1,0:T(8,128)} %shard_map.85), calls=%async_computation.2 | async-start | bytes 4456448 | tf_op jit(solution)/shard_map/all_to_all | solution.py:281
  128.6 0.8 copy-start.7
  156.6 1.0 copy-start.4

commit v8 on v7

--- a/solution.py
+++ b/solution.py
@@ -63,37 +63,39 @@
     out_ref[pl.ds(pl.multiple_of(row + 16, 16), 16), :] = low[:, pl.ds(at, width)]
 
 
-def accumulate(z, core, blocks, panels, lhs, acc):
+def accumulate(z, blocks, panels, columns, lhs, acc):
     width = panels[0].shape[1]
     acc[...] = jnp.zeros_like(acc)
     for half in range(2):
         for at in range(0, width, CHUNK):
             collect(z, blocks, half * width + at, CHUNK, lhs)
-            for number in range(2):
-                ref = panels[2 * number + half]
-                other = core if number == 0 else 1 - core
-                columns = pl.ds(pl.multiple_of(other * 256, 256), 256)
-                acc[:, columns] += lax.dot_general(
+            for number, column in enumerate(columns):
+                place = pl.ds(pl.multiple_of(column * 256, 256), 256)
+                acc[:, place] += lax.dot_general(
                     lhs[...],
-                    ref[:, at : at + CHUNK],
+                    panels[2 * number + half][:, at : at + CHUNK],
                     (((1,), (1,)), ((), ())),
                     preferred_element_type=jnp.float32,
                 )
 
 
 def near_kernel(place_ref, *refs):
-    blocks, panels, (out_ref, lhs) = refs[:9], refs[9:13], refs[13:]
-    accumulate(place_ref[1], place_ref[2], blocks, panels, lhs, out_ref)
+    blocks, panels, (out_ref, lhs, acc) = refs[:9], refs[9:15], refs[15:]
+    core = place_ref[2]
+    accumulate(place_ref[1], blocks, panels, (core, 1 - core, jnp.int32(2)), lhs, acc)
+    out_ref[...] = acc[...]
 
 
 def product_kernel(place_ref, *refs):
-    blocks, panels, near_ref = refs[:9], refs[9:13], refs[13]
-    turn_ref, home_ref, lhs, far, acc, local = refs[14:]
+    blocks, panels, near_ref = refs[:9], refs[9:11], refs[11]
+    turn_ref, home_ref, lhs, cross, acc, local = refs[12:]
     xlo, z, core = place_ref[0], place_ref[1], place_ref[2]
     strings = blocks[0].shape[1]
-    accumulate(z, core, blocks, panels, lhs, far)
-    acc[:, pl.ds(pl.multiple_of(xlo * 512, 512), 512)] = near_ref[...]
-    acc[:, pl.ds(pl.multiple_of((1 - xlo) * 512, 512), 512)] = far[...]
+    accumulate(z, blocks, panels, (jnp.int32(0),), lhs, cross)
+    acc[:, pl.ds(pl.multiple_of(xlo * 512, 512), 512)] = near_ref[:, 0:512]
+    far = (1 - xlo) * 2
+    acc[:, pl.ds(pl.multiple_of((far + core) * 256, 256), 256)] = near_ref[:, 512:768]
+    acc[:, pl.ds(pl.multiple_of((far + 1 - core) * 256, 256), 256)] = cross[...]
 
     for side in range(2):
         at = pl.multiple_of(side * (strings // 2) + z * 512, 512)
@@ -129,11 +131,14 @@
         near_kernel,
         in_specs=[pl.BlockSpec(memory_space=pltpu.SMEM)] + [vmem] * (len(blocks) + len(panels)),
         out_specs=vmem,
-        scratch_shapes=[pltpu.VMEM((256, CHUNK), jnp.bfloat16)],
-        out_shape=jax.ShapeDtypeStruct((256, 512), jnp.float32),
+        scratch_shapes=[
+            pltpu.VMEM((256, CHUNK), jnp.bfloat16),
+            pltpu.VMEM((256, 768), jnp.float32),
+        ],
+        out_shape=jax.ShapeDtypeStruct((256, 768), jnp.float32),
         compiler_params=pltpu.CompilerParams(vmem_limit_bytes=20 * MIB),
         cost_estimate=pl.CostEstimate(
-            flops=2 * 256 * 512 * NS, bytes_accessed=12 * MIB, transcendentals=0
+            flops=2 * 256 * 768 * NS, bytes_accessed=16 * MIB, transcendentals=0
         ),
     )(place, *blocks, *panels)
 
@@ -146,7 +151,7 @@
         out_specs=[vmem, vmem],
         scratch_shapes=[
             pltpu.VMEM((256, CHUNK), jnp.bfloat16),
-            pltpu.VMEM((256, 512), jnp.float32),
+            pltpu.VMEM((256, 256), jnp.float32),
             pltpu.VMEM((256, 1024), jnp.float32),
             pltpu.VMEM((256, 1024), jnp.bfloat16),
         ],
@@ -156,7 +161,7 @@
         ],
         compiler_params=pltpu.CompilerParams(vmem_limit_bytes=24 * MIB),
         cost_estimate=pl.CostEstimate(
-            flops=2 * 256 * 512 * NS, bytes_accessed=16 * MIB, transcendentals=0
+            flops=2 * 256 * 256 * NS, bytes_accessed=12 * MIB, transcendentals=0
         ),
     )(place, *blocks, *panels, near)
 
@@ -316,8 +321,8 @@
     cross_a, cross_b = swap(far_a), swap(far_b)
 
     blocks = (block, p1, p2, p3, m1, m2, m3, top, low)
-    near = multiply_near(place, blocks, (own_a, own_b, pair_a, pair_b))
-    turn, home = multiply(place, blocks, (far_a, far_b, cross_a, cross_b), near)
+    near = multiply_near(place, blocks, (own_a, own_b, pair_a, pair_b, far_a, far_b))
+    turn, home = multiply(place, blocks, (cross_a, cross_b), near)
 
     tiles = exchange(pack(exchange(turn, "z"), home), PLANE)
 

time: 180 us -> 179 us (level)
  transfers between devices with their start and end apart: 16 -> 16, of which waited for: 8 -> 7; matrix products, arithmetic and copies ran while one was open for 1% -> 1% of each run, Pallas kernels for 7% -> 7%
where the time goes in v8:
time: 179 us
  waiting for transfers between devices  55.7 us (31%)
  blocking collectives  53.4 us (30%)
  starting transfers between devices  40.9 us (23%)
  Pallas kernels  19.4 us (11%)
  local copies, waits for them, and re-layouts  5.86 us (3%)
  matrix products  2.52 us (1%)
    all_to_all x2, blocking collectives, exchange(): return lax.all_to_all(value, axes, split_axis=0, concat_axis=0, tiled=True)  53.4 us
    all_to_all x2, waiting for transfers between devices, exchange(): return lax.all_to_all(value, axes, split_axis=0, concat_axis=0, tiled=True)  28.5 us
    ppermute x8, waiting for transfers between devices, shift(): lax.ppermute(value, 'z', [(i, (i + step) % count) for i in range(count)])  25.2 us
    all_to_all x2, starting transfers between devices, exchange(): return lax.all_to_all(value, axes, split_axis=0, concat_axis=0, tiled=True)  14.3 us
    ppermute x8, starting transfers between devices, shift(): lax.ppermute(value, 'z', [(i, (i + step) % count) for i in range(count)])  13.7 us
    ppermute x4, starting transfers between devices, swap(): return lax.ppermute(value, 'core', [(0, 1), (1, 0)])  10.2 us
    pallas_call x4, Pallas kernels, mask_half(): pl.pallas_call(mask_kernel, grid=(4,), in_specs=[pl.BlockSpec((rows, cols...  8.86 us
    unnamed x20, local copies, waits for them, and re-layouts  5.35 us
  transfers between devices with their start and end apart: 16, of which 7 were waited for; matrix products, arithmetic and copies ran while one was open for 1% of the time, Pallas kernels for 7%

profile of v8, /device:TPU:1, one launch (start us, length us, event | category | flops | bytes accessed | tf_op | source)
XLA Modules:
  0.0 178.8 jit_solution(3304411956712101161)
XLA Ops:
  0.7 3.3 %collective-permute-start = (bf16[256,8192]{1,0:T(8,128)(2,1)}, bf16[256,8192]{1,0:T(8,128)(2,1)}, u32[]{:S(2)}, u32[]{:S(2)}) collective-permute-start(bf16[256,8192]{1,0:T(8,128)(2,1)} %ham_ref.1), channel_id=1, source_target_pairs={{0,8},{8,0},{1,9},{9,1},{2,10},{10,2},{3,11},{11,3},{4,12},{12,4},... | collective-permute-start | bytes 12582920 | tf_op jit(solution)/shard_map/ppermute | solution.py:269
  4.0 5.5 %all-to-all-start = ((bf16[32,8,1024]{2,1,0:T(8,128)(2,1)}), bf16[32,8,1024]{2,1,0:T(8,128)(2,1)S(1)}, u32[]{:S(2)}, u32[]{:S(2)}) async-start(bf16[32,8,1024]{2,1,0:T(8,128)(2,1)} %bitcast.29), calls=%async_computation | async-start | bytes 1048576 | tf_op jit(solution)/shard_map/all_to_all | solution.py:286
  9.8 2.2 %copy-done.1 = bf16[256,8192]{1,0:T(8,128)(2,1)S(1)} copy-done((bf16[256,8192]{1,0:T(8,128)(2,1)S(1)}, bf16[256,8192]{1,0:T(8,128)(2,1)}, u32[]{:S(2)}) %copy-start.1) | copy-done | bytes 4194328
  12.7 1.4 shard_map.77.refs_9_
  14.1 1.4 shard_map.78.refs_10_
  15.5 1.4 copy-done.2
  16.8 3.1 %all-to-all-done = bf16[32,8,1024]{2,1,0:T(8,128)(2,1)S(1)} async-done(((bf16[32,8,1024]{2,1,0:T(8,128)(2,1)}), bf16[32,8,1024]{2,1,0:T(8,128)(2,1)S(1)}, u32[]{:S(2)}, u32[]{:S(2)}) %all-to-all-start) | async-done | bytes 524320 | tf_op jit(solution)/shard_map/all_to_all | solution.py:286
  20.3 2.4 %collective-permute-start.11 = (bf16[256,4096]{1,0:T(8,128)(2,1)}, bf16[256,4096]{1,0:T(8,128)(2,1)S(1)}, u32[]{:S(2)}, u32[]{:S(2)}) collective-permute-start(bf16[256,4096]{1,0:T(8,128)(2,1)} %copy-done.2), channel_id=1, source_target_pairs={{0,132},{128,0},{4,128},{132,4},{1,133},{129,1},{5,129},{133,5},{2... | collective-permute-start | bytes 6291464 | tf_op jit(solution)/shard_map/ppermute | solution.py:282
  22.6 1.6 collective-permute-start.2
  24.3 3.9 %collective-permute-start.3 = (bf16[32,8192]{1,0:T(8,128)(2,1)S(1)}, bf16[32,8192]{1,0:T(8,128)(2,1)S(1)}, u32[]{:S(2)}, u32[]{:S(2)}) collective-permute-start(bf16[32,8192]{1,0:T(8,128)(2,1)S(1)} %bitcast.26), channel_id=1, source_target_pairs={{0,112},{16,0},{32,16},{48,32},{64,48},{80,64},{96,80},{112,96},{1... | collective-permute-start | bytes 1572872 | tf_op jit(solution)/shard_map/ppermute | solution.py:274
  28.2 9.9 %collective-permute-done.2.refs_1_ = bf16[32,8192]{1,0:T(8,128)(2,1)S(1)} collective-permute-done((bf16[32,8192]{1,0:T(8,128)(2,1)S(1)}, bf16[32,8192]{1,0:T(8,128)(2,1)S(1)}, u32[]{:S(2)}, u32[]{:S(2)}) %collective-permute-start.2) | collective-permute-done | bytes 524320 | tf_op jit(solution)/shard_map/ppermute | solution.py:274
  38.1 2.7 %collective-permute-start.5 = (bf16[32,8192]{1,0:T(8,128)(2,1)S(1)}, bf16[32,8192]{1,0:T(8,128)(2,1)S(1)}, u32[]{:S(2)}, u32[]{:S(2)}) collective-permute-start(bf16[32,8192]{1,0:T(8,128)(2,1)S(1)} %collective-permute-done.3.refs_4_), channel_id=1, source_target_pairs={{0,112},{16,0},{32,16},{48,32},{64,48},{80,64},{96,80},{112,96},{1... | collective-permute-start | bytes 1572872 | tf_op jit(solution)/shard_map/ppermute | solution.py:274
  40.8 3.0 %shard_map.79.refs_11_ = bf16[256,4096]{1,0:T(8,128)(2,1)S(1)} custom-call(bf16[256,8192]{1,0:T(8,128)(2,1)} %collective-permute-done.ham_ref, s32[8,256]{1,0:T(8,128)S(1)} %collective-permute-done.1.mask_ref), custom_call_target="tpu_custom_call" | custom-call | flops 2097152 | bytes 4194304 | tf_op jit(solution)/shard_map/pallas_call | solution.py:40
  43.8 5.9 %collective-permute-done.4.refs_2_ = bf16[32,8192]{1,0:T(8,128)(2,1)S(1)} collective-permute-done((bf16[32,8192]{1,0:T(8,128)(2,1)S(1)}, bf16[32,8192]{1,0:T(8,128)(2,1)S(1)}, u32[]{:S(2)}, u32[]{:S(2)}) %collective-permute-start.4) | collective-permute-done | bytes 524320 | tf_op jit(solution)/shard_map/ppermute | solution.py:274
  49.7 1.1 collective-permute-start.6
  50.8 1.6 collective-permute-start.7
  52.4 8.0 %collective-permute-done.6.value_ref.refs_3_ = bf16[32,8192]{1,0:T(8,128)(2,1)S(1)} collective-permute-done((bf16[32,8192]{1,0:T(8,128)(2,1)S(1)}, bf16[32,8192]{1,0:T(8,128)(2,1)S(1)}, u32[]{:S(2)}, u32[]{:S(2)}) %collective-permute-start.6) | collective-permute-done | bytes 524320 | tf_op jit(solution)/shard_map/ppermute | solution.py:274
  61.1 2.2 %collective-permute-start.9 = (bf16[16,8192]{1,0:T(8,128)(2,1)S(1)}, bf16[16,8192]{1,0:T(8,128)(2,1)S(1)}, u32[]{:S(2)}, u32[]{:S(2)}) collective-permute-start(bf16[16,8192]{1,0:T(8,128)(2,1)S(1)} %shard_map.81), channel_id=1, source_target_pairs={{0,112},{16,0},{32,16},{48,32},{64,48},{80,64},{96,80},{112,96},{1... | collective-permute-start | bytes 786440 | tf_op jit(solution)/shard_map/ppermute | solution.py:274
  63.3 3.0 %shard_map.82.refs_12_ = bf16[256,4096]{1,0:T(8,128)(2,1)S(1)} custom-call(bf16[256,8192]{1,0:T(8,128)(2,1)} %collective-permute-done.ham_ref, s32[8,256]{1,0:T(8,128)S(1)} %collective-permute-done.1.mask_ref), custom_call_target="tpu_custom_call" | custom-call | flops 2097152 | bytes 4194304 | tf_op jit(solution)/shard_map/pallas_call | solution.py:40
  66.3 1.4 collective-permute-done.8.refs_7_
  67.7 6.3 %collective-permute-start.12 = (bf16[256,4096]{1,0:T(8,128)(2,1)S(1)}, bf16[256,4096]{1,0:T(8,128)(2,1)S(1)}, u32[]{:S(2)}, u32[]{:S(2)}) collective-permute-start(bf16[256,4096]{1,0:T(8,128)(2,1)S(1)} %collective-permute-done.10.refs_13_), channel_id=1, source_target_pairs={{0,8},{8,0},{1,9},{9,1},{2,10},{10,2},{3,11},{11,3},{4,12},{12,4},... | collective-permute-start | bytes 6291464 | tf_op jit(solution)/shard_map/ppermute | solution.py:269
  74.3 4.4 %shard_map.83.refs_11_ = f32[256,768]{1,0:T(8,128)S(1)} custom-call(s32[3]{0:T(128)S(1)} %pad_add_fusion.place_ref, bf16[32,8192]{1,0:T(8,128)(2,1)S(1)} %bitcast.27, bf16[32,8192]{1,0:T(8,128)(2,1)S(1)} %collective-permute-done.2.refs_1_, bf16[32,8192]{1,0:T(8,128)(2,1)S(1)} %collective-permute-done.4.refs_2_, ...), custom_call_target="tpu_custom_call" | custom-call | flops 3221225472 | bytes 16777216 | tf_op jit(solution)/shard_map/pallas_call | solution.py:130
  78.7 2.1 %collective-permute-done.13.refs_10_ = bf16[256,4096]{1,0:T(8,128)(2,1)S(1)} collective-permute-done((bf16[256,4096]{1,0:T(8,128)(2,1)S(1)}, bf16[256,4096]{1,0:T(8,128)(2,1)S(1)}, u32[]{:S(2)}, u32[]{:S(2)}) %collective-permute-start.13) | collective-permute-done | bytes 2097184 | tf_op jit(solution)/shard_map/ppermute | solution.py:269
  80.8 2.6 %shard_map.84 = (f32[8,264,128]{2,1,0:T(8,128)S(1)}, f32[32,64,128]{2,1,0:T(8,128)S(1)}) custom-call(s32[3]{0:T(128)S(1)} %pad_add_fusion.place_ref, bf16[32,8192]{1,0:T(8,128)(2,1)S(1)} %bitcast.28, bf16[32,8192]{1,0:T(8,128)(2,1)S(1)} %collective-permute-done.2.refs_1_, bf16[32,8192]{1,0:T(8,128)(2,1)S(1)} %collective-permute-done.4.refs_2_, ...), custom_call_target="tpu_custom_call" | custom-call | flops 1073741824 | bytes 12582912 | tf_op jit(solution)/shard_map/pallas_call | solution.py:148
  83.4 33.6 %all_to_all.26.turn_ref = f32[8,264,128]{2,1,0:T(8,128)S(1)} all-to-all(f32[8,264,128]{2,1,0:T(8,128)S(1)} %get-tuple-element.55), channel_id=1, replica_groups=mesh['xlo'=2,'z'=8,'core'=2,'xhi'=2,'y'=4] {'z'}, dimensions={0} | all-to-all | bytes 2162688 | tf_op jit(solution)/shard_map/all_to_all | solution.py:286
  117.1 1.6 shard_map.85
  118.6 8.9 %all-to-all-start.2 = ((f32[32,136,128]{2,1,0:T(8,128)}), f32[32,136,128]{2,1,0:T(8,128)S(1)}, u32[]{:S(2)}, u32[]{:S(2)}) async-start(f32[32,136,128]{2,1,0:T(8,128)} %shard_map.85), calls=%async_computation.2 | async-start | bytes 4456448 | tf_op jit(solution)/shard_map/all_to_all | solution.py:286
  128.4 1.8 %convolution_add_fusion.diag_ref = f32[256,1024]{1,0:T(8,128)S(1)} fusion(f32[256,16]{1,0:T(8,128)S(1)} %fusion.3, f32[1024]{0:T(1024)S(1)} %bitcast.32, f32[256]{0:T(256)S(1)} %bitcast.33, f32[16,8192]{1,0:T(8,128)} %copy-done.7, s32[]{:T(128)S(6)} %select_n.7), kind=kOutput, calls=%fused_computation | convolution fusion | flops 50855936 | bytes 1135620 | tf_op jit(solution)/shard_map/dot_general | solution.py:334
  130.2 25.4 %all-to-all-done.2.tiles_ref = f32[32,136,128]{2,1,0:T(8,128)S(1)} async-done(((f32[32,136,128]{2,1,0:T(8,128)}), f32[32,136,128]{2,1,0:T(8,128)S(1)}, u32[]{:S(2)}, u32[]{:S(2)}) %all-to-all-start.2) | async-done | bytes 2228256 | tf_op jit(solution)/shard_map/all_to_all | solution.py:286
  155.6 1.0 copy-done.4
  157.4 19.7 %all_to_all.27 = f32[256,1,128]{2,1,0:T(1,128)S(1)} all-to-all(f32[256,1,128]{2,1,0:T(1,128)S(1)} %bitcast.31), channel_id=1, replica_groups=mesh['xlo'=2,'z'=8,'core'=2,'xhi'=2,'y'=4] {'xlo','z','core','xhi','y'}, dimensions={0} | all-to-all | bytes 262144 | tf_op jit(solution)/shard_map/all_to_all | solution.py:286
  177.1 1.2 shard_map.87
  (40 shorter events, 4.4 us)
Async XLA Ops:
  0.6 127.3 %copy-start = (f32[16,16]{1,0:T(8,128)S(1)}, f32[16,16]{1,0:T(8,128)}, u32[]{:S(2)}) copy-start(f32[16,16]{1,0:T(8,128)} %param.11) | copy-start | bytes 3076
  0.7 19.2 %collective-permute-start = (bf16[256,8192]{1,0:T(8,128)(2,1)}, bf16[256,8192]{1,0:T(8,128)(2,1)}, u32[]{:S(2)}, u32[]{:S(2)}) collective-permute-start(bf16[256,8192]{1,0:T(8,128)(2,1)} %ham_ref.1), channel_id=1, source_target_pairs={{0,8},{8,0},{1,9},{9,1},{2,10},{10,2},{3,11},{11,3},{4,12},{12,4},... | collective-permute-start | bytes 12582920 | tf_op jit(solution)/shard_map/ppermute | solution.py:269
  4.0 16.0 %all-to-all-start = ((bf16[32,8,1024]{2,1,0:T(8,128)(2,1)}), bf16[32,8,1024]{2,1,0:T(8,128)(2,1)S(1)}, u32[]{:S(2)}, u32[]{:S(2)}) async-start(bf16[32,8,1024]{2,1,0:T(8,128)(2,1)} %bitcast.29), calls=%async_computation | async-start | bytes 1048576 | tf_op jit(solution)/shard_map/all_to_all | solution.py:286
  9.5 7.4 %collective-permute-start.1 = (s32[8,256]{1,0:T(8,128)}, s32[8,256]{1,0:T(8,128)S(1)}, u32[]{:S(2)}, u32[]{:S(2)}) collective-permute-start(s32[8,256]{1,0:T(8,128)} %mask_ref.3), channel_id=1, source_target_pairs={{0,8},{8,0},{1,9},{9,1},{2,10},{10,2},{3,11},{11,3},{4,12},{12,4},... | collective-permute-start | bytes 24584 | tf_op jit(solution)/shard_map/ppermute | solution.py:269
  9.8 2.2 %copy-start.1 = (bf16[256,8192]{1,0:T(8,128)(2,1)S(1)}, bf16[256,8192]{1,0:T(8,128)(2,1)}, u32[]{:S(2)}) copy-start(bf16[256,8192]{1,0:T(8,128)(2,1)} %ham_ref.1) | copy-start | bytes 12582916
  12.0 0.7 copy-start.5
  12.7 1.4 copy-start.6
  15.5 1.4 copy-start.2
  20.0 47.7 %collective-permute-start.10 = (bf16[256,4096]{1,0:T(8,128)(2,1)S(1)}, bf16[256,4096]{1,0:T(8,128)(2,1)S(1)}, u32[]{:S(2)}, u32[]{:S(2)}) collective-permute-start(bf16[256,4096]{1,0:T(8,128)(2,1)S(1)} %shard_map.77.refs_9_), channel_id=1, source_target_pairs={{0,128},{128,4},{4,132},{132,0},{1,129},{129,5},{5,133},{133,1},{2... | collective-permute-start | bytes 6291464 | tf_op jit(solution)/shard_map/ppermute | solution.py:282
  20.3 47.4 %collective-permute-start.11 = (bf16[256,4096]{1,0:T(8,128)(2,1)}, bf16[256,4096]{1,0:T(8,128)(2,1)S(1)}, u32[]{:S(2)}, u32[]{:S(2)}) collective-permute-start(bf16[256,4096]{1,0:T(8,128)(2,1)} %copy-done.2), channel_id=1, source_target_pairs={{0,132},{128,0},{4,128},{132,4},{1,133},{129,1},{5,129},{133,5},{2... | collective-permute-start | bytes 6291464 | tf_op jit(solution)/shard_map/ppermute | solution.py:282
  22.6 15.5 %collective-permute-start.2 = (bf16[32,8192]{1,0:T(8,128)(2,1)S(1)}, bf16[32,8192]{1,0:T(8,128)(2,1)S(1)}, u32[]{:S(2)}, u32[]{:S(2)}) collective-permute-start(bf16[32,8192]{1,0:T(8,128)(2,1)S(1)} %bitcast.25), channel_id=1, source_target_pairs={{0,16},{16,32},{32,48},{48,64},{64,80},{80,96},{96,112},{112,0},{1... | collective-permute-start | bytes 1572872 | tf_op jit(solution)/shard_map/ppermute | solution.py:274
  24.3 13.8 %collective-permute-start.3 = (bf16[32,8192]{1,0:T(8,128)(2,1)S(1)}, bf16[32,8192]{1,0:T(8,128)(2,1)S(1)}, u32[]{:S(2)}, u32[]{:S(2)}) collective-permute-start(bf16[32,8192]{1,0:T(8,128)(2,1)S(1)} %bitcast.26), channel_id=1, source_target_pairs={{0,112},{16,0},{32,16},{48,32},{64,48},{80,64},{96,80},{112,96},{1... | collective-permute-start | bytes 1572872 | tf_op jit(solution)/shard_map/ppermute | solution.py:274
  38.1 11.6 %collective-permute-start.4 = (bf16[32,8192]{1,0:T(8,128)(2,1)S(1)}, bf16[32,8192]{1,0:T(8,128)(2,1)S(1)}, u32[]{:S(2)}, u32[]{:S(2)}) collective-permute-start(bf16[32,8192]{1,0:T(8,128)(2,1)S(1)} %collective-permute-done.2.refs_1_), channel_id=1, source_target_pairs={{0,16},{16,32},{32,48},{48,64},{64,80},{80,96},{96,112},{112,0},{1... | collective-permute-start | bytes 1572872 | tf_op jit(solution)/shard_map/ppermute | solution.py:274
  38.1 11.6 %collective-permute-start.5 = (bf16[32,8192]{1,0:T(8,128)(2,1)S(1)}, bf16[32,8192]{1,0:T(8,128)(2,1)S(1)}, u32[]{:S(2)}, u32[]{:S(2)}) collective-permute-start(bf16[32,8192]{1,0:T(8,128)(2,1)S(1)} %collective-permute-done.3.refs_4_), channel_id=1, source_target_pairs={{0,112},{16,0},{32,16},{48,32},{64,48},{80,64},{96,80},{112,96},{1... | collective-permute-start | bytes 1572872 | tf_op jit(solution)/shard_map/ppermute | solution.py:274
  49.7 10.7 %collective-permute-start.6 = (bf16[32,8192]{1,0:T(8,128)(2,1)S(1)}, bf16[32,8192]{1,0:T(8,128)(2,1)S(1)}, u32[]{:S(2)}, u32[]{:S(2)}) collective-permute-start(bf16[32,8192]{1,0:T(8,128)(2,1)S(1)} %collective-permute-done.4.refs_2_), channel_id=1, source_target_pairs={{0,16},{16,32},{32,48},{48,64},{64,80},{80,96},{96,112},{112,0},{1... | collective-permute-start | bytes 1572872 | tf_op jit(solution)/shard_map/ppermute | solution.py:274
  50.8 9.7 %collective-permute-start.7 = (bf16[32,8192]{1,0:T(8,128)(2,1)S(1)}, bf16[32,8192]{1,0:T(8,128)(2,1)S(1)}, u32[]{:S(2)}, u32[]{:S(2)}) collective-permute-start(bf16[32,8192]{1,0:T(8,128)(2,1)S(1)} %collective-permute-done.5.refs_5_), channel_id=1, source_target_pairs={{0,112},{16,0},{32,16},{48,32},{64,48},{80,64},{96,80},{112,96},{1... | collective-permute-start | bytes 1572872 | tf_op jit(solution)/shard_map/ppermute | solution.py:274
  60.5 13.8 %copy-start.3 = (bf16[256,4096]{1,0:T(8,128)(2,1)S(1)}, bf16[256,4096]{1,0:T(8,128)(2,1)}, u32[]{:S(2)}) copy-start(bf16[256,4096]{1,0:T(8,128)(2,1)} %copy-done.2) | copy-start | bytes 6291460
  60.5 7.2 %collective-permute-start.8 = (bf16[16,8192]{1,0:T(8,128)(2,1)S(1)}, bf16[16,8192]{1,0:T(8,128)(2,1)S(1)}, u32[]{:S(2)}, u32[]{:S(2)}) collective-permute-start(bf16[16,8192]{1,0:T(8,128)(2,1)S(1)} %shard_map.80), channel_id=1, source_target_pairs={{0,16},{16,32},{32,48},{48,64},{64,80},{80,96},{96,112},{112,0},{1... | collective-permute-start | bytes 786440 | tf_op jit(solution)/shard_map/ppermute | solution.py:274
  61.1 6.6 %collective-permute-start.9 = (bf16[16,8192]{1,0:T(8,128)(2,1)S(1)}, bf16[16,8192]{1,0:T(8,128)(2,1)S(1)}, u32[]{:S(2)}, u32[]{:S(2)}) collective-permute-start(bf16[16,8192]{1,0:T(8,128)(2,1)S(1)} %shard_map.81), channel_id=1, source_target_pairs={{0,112},{16,0},{32,16},{48,32},{64,48},{80,64},{96,80},{112,96},{1... | collective-permute-start | bytes 786440 | tf_op jit(solution)/shard_map/ppermute | solution.py:274
  67.7 11.0 %collective-permute-start.12 = (bf16[256,4096]{1,0:T(8,128)(2,1)S(1)}, bf16[256,4096]{1,0:T(8,128)(2,1)S(1)}, u32[]{:S(2)}, u32[]{:S(2)}) collective-permute-start(bf16[256,4096]{1,0:T(8,128)(2,1)S(1)} %collective-permute-done.10.refs_13_), channel_id=1, source_target_pairs={{0,8},{8,0},{1,9},{9,1},{2,10},{10,2},{3,11},{11,3},{4,12},{12,4},... | collective-permute-start | bytes 6291464 | tf_op jit(solution)/shard_map/ppermute | solution.py:269
  74.0 6.8 %collective-permute-start.13 = (bf16[256,4096]{1,0:T(8,128)(2,1)S(1)}, bf16[256,4096]{1,0:T(8,128)(2,1)S(1)}, u32[]{:S(2)}, u32[]{:S(2)}) collective-permute-start(bf16[256,4096]{1,0:T(8,128)(2,1)S(1)} %collective-permute-done.11.refs_14_), channel_id=1, source_target_pairs={{0,8},{8,0},{1,9},{9,1},{2,10},{10,2},{3,11},{11,3},{4,12},{12,4},... | collective-permute-start | bytes 6291464 | tf_op jit(solution)/shard_map/ppermute | solution.py:269
  118.6 8.9 %copy-start.8 = (s32[16,8192]{1,0:T(8,128)S(1)}, s32[16,8192]{1,0:T(8,128)}, u32[]{:S(2)}) copy-start(s32[16,8192]{1,0:T(8,128)} %param.9) | copy-start | bytes 1572868
  118.6 9.0 %copy-start.9 = (f32[16]{0:T(128)S(1)}, f32[16]{0:T(128)}, u32[]{:S(2)}) copy-start(f32[16]{0:T(128)} %param.10) | copy-start | bytes 196
  118.6 36.9 %all-to-all-start.2 = ((f32[32,136,128]{2,1,0:T(8,128)}), f32[32,136,128]{2,1,0:T(8,128)S(1)}, u32[]{:S(2)}, u32[]{:S(2)}) async-start(f32[32,136,128]{2,1,0:T(8,128)} %shard_map.85), calls=%async_computation.2 | async-start | bytes 4456448 | tf_op jit(solution)/shard_map/all_to_all | solution.py:286
  127.6 0.8 copy-start.7
  155.6 1.0 copy-start.4

commit v9 on v8

--- a/solution.py
+++ b/solution.py
@@ -306,11 +306,11 @@
         (block, own_a, own_b, pair, pair_mask)
     )
     far_a, far_b = shift_x(own_a, 1), shift_x(own_b, -1)
-    p1, m1, pair, pair_mask = lax.optimization_barrier(
-        (shift(block, 1), shift(block, -1), pair, pair_mask)
-    )
+    p1, pair, pair_mask = lax.optimization_barrier((shift(block, 1), pair, pair_mask))
+    m1 = shift(block, -1)
     pair_a = mask_half(pair, pair_mask, 0)
-    p2, m2, pair_a = lax.optimization_barrier((shift(p1, 1), shift(m1, -1), pair_a))
+    p2, pair_a = lax.optimization_barrier((shift(p1, 1), pair_a))
+    m2 = shift(m1, -1)
     p3, m3 = shift(p2, 1), shift(m2, -1)
     top, low = take_rows(p3, 0), take_rows(m3, 16)
     top, low, pair, pair_mask = lax.optimization_barrier((top, low, pair, pair_mask))

time: 179 us -> 179 us (level)
  no operation moved by 1% of the time
where the time goes in v9:
time: 179 us
  waiting for transfers between devices  55.7 us (31%)
  blocking collectives  53.9 us (30%)
  starting transfers between devices  40.3 us (23%)
  Pallas kernels  19.4 us (11%)
  local copies, waits for them, and re-layouts  5.86 us (3%)
  matrix products  2.52 us (1%)
    all_to_all x2, blocking collectives, exchange(): return lax.all_to_all(value, axes, split_axis=0, concat_axis=0, tiled=True)  53.9 us
    all_to_all x2, waiting for transfers between devices, exchange(): return lax.all_to_all(value, axes, split_axis=0, concat_axis=0, tiled=True)  28.5 us
    ppermute x8, waiting for transfers between devices, shift(): lax.ppermute(value, 'z', [(i, (i + step) % count) for i in range(count)])  25.2 us
    all_to_all x2, starting transfers between devices, exchange(): return lax.all_to_all(value, axes, split_axis=0, concat_axis=0, tiled=True)  14.3 us
    ppermute x8, starting transfers between devices, shift(): lax.ppermute(value, 'z', [(i, (i + step) % count) for i in range(count)])  13.7 us
    ppermute x4, starting transfers between devices, swap(): return lax.ppermute(value, 'core', [(0, 1), (1, 0)])  9.58 us
    pallas_call x4, Pallas kernels, mask_half(): pl.pallas_call(mask_kernel, grid=(4,), in_specs=[pl.BlockSpec((rows, cols...  8.86 us
    unnamed x20, local copies, waits for them, and re-layouts  5.35 us
  transfers between devices with their start and end apart: 16, of which 7 were waited for; matrix products, arithmetic and copies ran while one was open for 1% of the time, Pallas kernels for 7%

profile of v9, /device:TPU:1, one launch (start us, length us, event | category | flops | bytes accessed | tf_op | source)
XLA Modules:
  0.0 178.8 jit_solution(12643363538421273751)
XLA Ops:
  0.7 3.3 %collective-permute-start = (bf16[256,8192]{1,0:T(8,128)(2,1)}, bf16[256,8192]{1,0:T(8,128)(2,1)}, u32[]{:S(2)}, u32[]{:S(2)}) collective-permute-start(bf16[256,8192]{1,0:T(8,128)(2,1)} %ham_ref.1), channel_id=1, source_target_pairs={{0,8},{8,0},{1,9},{9,1},{2,10},{10,2},{3,11},{11,3},{4,12},{12,4},... | collective-permute-start | bytes 12582920 | tf_op jit(solution)/shard_map/ppermute | solution.py:269
  4.0 5.5 %all-to-all-start = ((bf16[32,8,1024]{2,1,0:T(8,128)(2,1)}), bf16[32,8,1024]{2,1,0:T(8,128)(2,1)S(1)}, u32[]{:S(2)}, u32[]{:S(2)}) async-start(bf16[32,8,1024]{2,1,0:T(8,128)(2,1)} %bitcast.29), calls=%async_computation | async-start | bytes 1048576 | tf_op jit(solution)/shard_map/all_to_all | solution.py:286
  9.8 2.2 %copy-done.1 = bf16[256,8192]{1,0:T(8,128)(2,1)S(1)} copy-done((bf16[256,8192]{1,0:T(8,128)(2,1)S(1)}, bf16[256,8192]{1,0:T(8,128)(2,1)}, u32[]{:S(2)}) %copy-start.1) | copy-done | bytes 4194328
  12.7 1.4 shard_map.77.refs_9_
  14.1 1.4 shard_map.78.refs_10_
  15.5 1.4 copy-done.2
  16.8 3.1 %all-to-all-done = bf16[32,8,1024]{2,1,0:T(8,128)(2,1)S(1)} async-done(((bf16[32,8,1024]{2,1,0:T(8,128)(2,1)}), bf16[32,8,1024]{2,1,0:T(8,128)(2,1)S(1)}, u32[]{:S(2)}, u32[]{:S(2)}) %all-to-all-start) | async-done | bytes 524320 | tf_op jit(solution)/shard_map/all_to_all | solution.py:286
  20.3 2.4 %collective-permute-start.11 = (bf16[256,4096]{1,0:T(8,128)(2,1)}, bf16[256,4096]{1,0:T(8,128)(2,1)S(1)}, u32[]{:S(2)}, u32[]{:S(2)}) collective-permute-start(bf16[256,4096]{1,0:T(8,128)(2,1)} %copy-done.2), channel_id=1, source_target_pairs={{0,132},{128,0},{4,128},{132,4},{1,133},{129,1},{5,129},{133,5},{2... | collective-permute-start | bytes 6291464 | tf_op jit(solution)/shard_map/ppermute | solution.py:282
  22.6 1.6 collective-permute-start.2
  24.3 3.9 %collective-permute-start.5 = (bf16[32,8192]{1,0:T(8,128)(2,1)S(1)}, bf16[32,8192]{1,0:T(8,128)(2,1)S(1)}, u32[]{:S(2)}, u32[]{:S(2)}) collective-permute-start(bf16[32,8192]{1,0:T(8,128)(2,1)S(1)} %bitcast.26), channel_id=1, source_target_pairs={{0,112},{16,0},{32,16},{48,32},{64,48},{80,64},{96,80},{112,96},{1... | collective-permute-start | bytes 1572872 | tf_op jit(solution)/shard_map/ppermute | solution.py:274
  28.2 9.9 %collective-permute-done.2.refs_1_ = bf16[32,8192]{1,0:T(8,128)(2,1)S(1)} collective-permute-done((bf16[32,8192]{1,0:T(8,128)(2,1)S(1)}, bf16[32,8192]{1,0:T(8,128)(2,1)S(1)}, u32[]{:S(2)}, u32[]{:S(2)}) %collective-permute-start.2) | collective-permute-done | bytes 524320 | tf_op jit(solution)/shard_map/ppermute | solution.py:274
  38.1 2.7 %collective-permute-start.6 = (bf16[32,8192]{1,0:T(8,128)(2,1)S(1)}, bf16[32,8192]{1,0:T(8,128)(2,1)S(1)}, u32[]{:S(2)}, u32[]{:S(2)}) collective-permute-start(bf16[32,8192]{1,0:T(8,128)(2,1)S(1)} %collective-permute-done.5.refs_4_), channel_id=1, source_target_pairs={{0,112},{16,0},{32,16},{48,32},{64,48},{80,64},{96,80},{112,96},{1... | collective-permute-start | bytes 1572872 | tf_op jit(solution)/shard_map/ppermute | solution.py:274
  40.8 3.0 %shard_map.79.refs_11_ = bf16[256,4096]{1,0:T(8,128)(2,1)S(1)} custom-call(bf16[256,8192]{1,0:T(8,128)(2,1)} %collective-permute-done.ham_ref, s32[8,256]{1,0:T(8,128)S(1)} %collective-permute-done.1.mask_ref), custom_call_target="tpu_custom_call" | custom-call | flops 2097152 | bytes 4194304 | tf_op jit(solution)/shard_map/pallas_call | solution.py:40
  43.8 5.9 %collective-permute-done.3.refs_2_ = bf16[32,8192]{1,0:T(8,128)(2,1)S(1)} collective-permute-done((bf16[32,8192]{1,0:T(8,128)(2,1)S(1)}, bf16[32,8192]{1,0:T(8,128)(2,1)S(1)}, u32[]{:S(2)}, u32[]{:S(2)}) %collective-permute-start.3) | collective-permute-done | bytes 524320 | tf_op jit(solution)/shard_map/ppermute | solution.py:274
  49.7 2.7 %collective-permute-start.7 = (bf16[32,8192]{1,0:T(8,128)(2,1)S(1)}, bf16[32,8192]{1,0:T(8,128)(2,1)S(1)}, u32[]{:S(2)}, u32[]{:S(2)}) collective-permute-start(bf16[32,8192]{1,0:T(8,128)(2,1)S(1)} %collective-permute-done.6.refs_5_), channel_id=1, source_target_pairs={{0,112},{16,0},{32,16},{48,32},{64,48},{80,64},{96,80},{112,96},{1... | collective-permute-start | bytes 1572872 | tf_op jit(solution)/shard_map/ppermute | solution.py:274
  52.4 8.0 %collective-permute-done.4.value_ref.refs_3_ = bf16[32,8192]{1,0:T(8,128)(2,1)S(1)} collective-permute-done((bf16[32,8192]{1,0:T(8,128)(2,1)S(1)}, bf16[32,8192]{1,0:T(8,128)(2,1)S(1)}, u32[]{:S(2)}, u32[]{:S(2)}) %collective-permute-start.4) | collective-permute-done | bytes 524320 | tf_op jit(solution)/shard_map/ppermute | solution.py:274
  60.6 2.7 %collective-permute-start.9 = (bf16[16,8192]{1,0:T(8,128)(2,1)S(1)}, bf16[16,8192]{1,0:T(8,128)(2,1)S(1)}, u32[]{:S(2)}, u32[]{:S(2)}) collective-permute-start(bf16[16,8192]{1,0:T(8,128)(2,1)S(1)} %shard_map.81), channel_id=1, source_target_pairs={{0,112},{16,0},{32,16},{48,32},{64,48},{80,64},{96,80},{112,96},{1... | collective-permute-start | bytes 786440 | tf_op jit(solution)/shard_map/ppermute | solution.py:274
  63.3 3.0 %shard_map.82.refs_12_ = bf16[256,4096]{1,0:T(8,128)(2,1)S(1)} custom-call(bf16[256,8192]{1,0:T(8,128)(2,1)} %collective-permute-done.ham_ref, s32[8,256]{1,0:T(8,128)S(1)} %collective-permute-done.1.mask_ref), custom_call_target="tpu_custom_call" | custom-call | flops 2097152 | bytes 4194304 | tf_op jit(solution)/shard_map/pallas_call | solution.py:40
  66.3 1.4 collective-permute-done.8.refs_7_
  67.7 5.7 %collective-permute-start.12 = (bf16[256,4096]{1,0:T(8,128)(2,1)S(1)}, bf16[256,4096]{1,0:T(8,128)(2,1)S(1)}, u32[]{:S(2)}, u32[]{:S(2)}) collective-permute-start(bf16[256,4096]{1,0:T(8,128)(2,1)S(1)} %collective-permute-done.10.refs_13_), channel_id=1, source_target_pairs={{0,8},{8,0},{1,9},{9,1},{2,10},{10,2},{3,11},{11,3},{4,12},{12,4},... | collective-permute-start | bytes 6291464 | tf_op jit(solution)/shard_map/ppermute | solution.py:269
  73.7 4.4 %shard_map.83.refs_11_ = f32[256,768]{1,0:T(8,128)S(1)} custom-call(s32[3]{0:T(128)S(1)} %pad_add_fusion.place_ref, bf16[32,8192]{1,0:T(8,128)(2,1)S(1)} %bitcast.27, bf16[32,8192]{1,0:T(8,128)(2,1)S(1)} %collective-permute-done.2.refs_1_, bf16[32,8192]{1,0:T(8,128)(2,1)S(1)} %collective-permute-done.3.refs_2_, ...), custom_call_target="tpu_custom_call" | custom-call | flops 3221225472 | bytes 16777216 | tf_op jit(solution)/shard_map/pallas_call | solution.py:130
  78.1 2.1 %collective-permute-done.13.refs_10_ = bf16[256,4096]{1,0:T(8,128)(2,1)S(1)} collective-permute-done((bf16[256,4096]{1,0:T(8,128)(2,1)S(1)}, bf16[256,4096]{1,0:T(8,128)(2,1)S(1)}, u32[]{:S(2)}, u32[]{:S(2)}) %collective-permute-start.13) | collective-permute-done | bytes 2097184 | tf_op jit(solution)/shard_map/ppermute | solution.py:269
  80.2 2.6 %shard_map.84 = (f32[8,264,128]{2,1,0:T(8,128)S(1)}, f32[32,64,128]{2,1,0:T(8,128)S(1)}) custom-call(s32[3]{0:T(128)S(1)} %pad_add_fusion.place_ref, bf16[32,8192]{1,0:T(8,128)(2,1)S(1)} %bitcast.28, bf16[32,8192]{1,0:T(8,128)(2,1)S(1)} %collective-permute-done.2.refs_1_, bf16[32,8192]{1,0:T(8,128)(2,1)S(1)} %collective-permute-done.3.refs_2_, ...), custom_call_target="tpu_custom_call" | custom-call | flops 1073741824 | bytes 12582912 | tf_op jit(solution)/shard_map/pallas_call | solution.py:148
  82.8 34.2 %all_to_all.26.turn_ref = f32[8,264,128]{2,1,0:T(8,128)S(1)} all-to-all(f32[8,264,128]{2,1,0:T(8,128)S(1)} %get-tuple-element.51), channel_id=1, replica_groups=mesh['xlo'=2,'z'=8,'core'=2,'xhi'=2,'y'=4] {'z'}, dimensions={0} | all-to-all | bytes 2162688 | tf_op jit(solution)/shard_map/all_to_all | solution.py:286
  117.1 1.6 shard_map.85
  118.6 8.9 %all-to-all-start.2 = ((f32[32,136,128]{2,1,0:T(8,128)}), f32[32,136,128]{2,1,0:T(8,128)S(1)}, u32[]{:S(2)}, u32[]{:S(2)}) async-start(f32[32,136,128]{2,1,0:T(8,128)} %shard_map.85), calls=%async_computation.2 | async-start | bytes 4456448 | tf_op jit(solution)/shard_map/all_to_all | solution.py:286
  128.4 1.8 %convolution_add_fusion.diag_ref = f32[256,1024]{1,0:T(8,128)S(1)} fusion(f32[256,16]{1,0:T(8,128)S(1)} %fusion.3, f32[1024]{0:T(1024)S(1)} %bitcast.32, f32[256]{0:T(256)S(1)} %bitcast.33, f32[16,8192]{1,0:T(8,128)} %copy-done.7, s32[]{:T(128)S(6)} %select_n.7), kind=kOutput, calls=%fused_computation | convolution fusion | flops 50855936 | bytes 1135620 | tf_op jit(solution)/shard_map/dot_general | solution.py:334
  130.2 25.4 %all-to-all-done.2.tiles_ref = f32[32,136,128]{2,1,0:T(8,128)S(1)} async-done(((f32[32,136,128]{2,1,0:T(8,128)}), f32[32,136,128]{2,1,0:T(8,128)S(1)}, u32[]{:S(2)}, u32[]{:S(2)}) %all-to-all-start.2) | async-done | bytes 2228256 | tf_op jit(solution)/shard_map/all_to_all | solution.py:286
  155.6 1.0 copy-done.4
  156.6 0.8 shard_map.86
  157.4 19.7 %all_to_all.27 = f32[256,1,128]{2,1,0:T(1,128)S(1)} all-to-all(f32[256,1,128]{2,1,0:T(1,128)S(1)} %bitcast.31), channel_id=1, replica_groups=mesh['xlo'=2,'z'=8,'core'=2,'xhi'=2,'y'=4] {'xlo','z','core','xhi','y'}, dimensions={0} | all-to-all | bytes 262144 | tf_op jit(solution)/shard_map/all_to_all | solution.py:286
  177.1 1.2 shard_map.87
  (40 shorter events, 3.1 us)
Async XLA Ops:
  0.6 127.3 %copy-start = (f32[16,16]{1,0:T(8,128)S(1)}, f32[16,16]{1,0:T(8,128)}, u32[]{:S(2)}) copy-start(f32[16,16]{1,0:T(8,128)} %param.11) | copy-start | bytes 3076
  0.7 19.2 %collective-permute-start = (bf16[256,8192]{1,0:T(8,128)(2,1)}, bf16[256,8192]{1,0:T(8,128)(2,1)}, u32[]{:S(2)}, u32[]{:S(2)}) collective-permute-start(bf16[256,8192]{1,0:T(8,128)(2,1)} %ham_ref.1), channel_id=1, source_target_pairs={{0,8},{8,0},{1,9},{9,1},{2,10},{10,2},{3,11},{11,3},{4,12},{12,4},... | collective-permute-start | bytes 12582920 | tf_op jit(solution)/shard_map/ppermute | solution.py:269
  4.0 16.0 %all-to-all-start = ((bf16[32,8,1024]{2,1,0:T(8,128)(2,1)}), bf16[32,8,1024]{2,1,0:T(8,128)(2,1)S(1)}, u32[]{:S(2)}, u32[]{:S(2)}) async-start(bf16[32,8,1024]{2,1,0:T(8,128)(2,1)} %bitcast.29), calls=%async_computation | async-start | bytes 1048576 | tf_op jit(solution)/shard_map/all_to_all | solution.py:286
  9.5 7.4 %collective-permute-start.1 = (s32[8,256]{1,0:T(8,128)}, s32[8,256]{1,0:T(8,128)S(1)}, u32[]{:S(2)}, u32[]{:S(2)}) collective-permute-start(s32[8,256]{1,0:T(8,128)} %mask_ref.3), channel_id=1, source_target_pairs={{0,8},{8,0},{1,9},{9,1},{2,10},{10,2},{3,11},{11,3},{4,12},{12,4},... | collective-permute-start | bytes 24584 | tf_op jit(solution)/shard_map/ppermute | solution.py:269
  9.8 2.2 %copy-start.1 = (bf16[256,8192]{1,0:T(8,128)(2,1)S(1)}, bf16[256,8192]{1,0:T(8,128)(2,1)}, u32[]{:S(2)}) copy-start(bf16[256,8192]{1,0:T(8,128)(2,1)} %ham_ref.1) | copy-start | bytes 12582916
  12.0 0.7 copy-start.5
  12.7 1.4 copy-start.6
  15.5 1.4 copy-start.2
  20.0 47.7 %collective-permute-start.10 = (bf16[256,4096]{1,0:T(8,128)(2,1)S(1)}, bf16[256,4096]{1,0:T(8,128)(2,1)S(1)}, u32[]{:S(2)}, u32[]{:S(2)}) collective-permute-start(bf16[256,4096]{1,0:T(8,128)(2,1)S(1)} %shard_map.77.refs_9_), channel_id=1, source_target_pairs={{0,128},{128,4},{4,132},{132,0},{1,129},{129,5},{5,133},{133,1},{2... | collective-permute-start | bytes 6291464 | tf_op jit(solution)/shard_map/ppermute | solution.py:282
  20.3 47.4 %collective-permute-start.11 = (bf16[256,4096]{1,0:T(8,128)(2,1)}, bf16[256,4096]{1,0:T(8,128)(2,1)S(1)}, u32[]{:S(2)}, u32[]{:S(2)}) collective-permute-start(bf16[256,4096]{1,0:T(8,128)(2,1)} %copy-done.2), channel_id=1, source_target_pairs={{0,132},{128,0},{4,128},{132,4},{1,133},{129,1},{5,129},{133,5},{2... | collective-permute-start | bytes 6291464 | tf_op jit(solution)/shard_map/ppermute | solution.py:282
  22.6 15.5 %collective-permute-start.2 = (bf16[32,8192]{1,0:T(8,128)(2,1)S(1)}, bf16[32,8192]{1,0:T(8,128)(2,1)S(1)}, u32[]{:S(2)}, u32[]{:S(2)}) collective-permute-start(bf16[32,8192]{1,0:T(8,128)(2,1)S(1)} %bitcast.25), channel_id=1, source_target_pairs={{0,16},{16,32},{32,48},{48,64},{64,80},{80,96},{96,112},{112,0},{1... | collective-permute-start | bytes 1572872 | tf_op jit(solution)/shard_map/ppermute | solution.py:274
  24.3 13.8 %collective-permute-start.5 = (bf16[32,8192]{1,0:T(8,128)(2,1)S(1)}, bf16[32,8192]{1,0:T(8,128)(2,1)S(1)}, u32[]{:S(2)}, u32[]{:S(2)}) collective-permute-start(bf16[32,8192]{1,0:T(8,128)(2,1)S(1)} %bitcast.26), channel_id=1, source_target_pairs={{0,112},{16,0},{32,16},{48,32},{64,48},{80,64},{96,80},{112,96},{1... | collective-permute-start | bytes 1572872 | tf_op jit(solution)/shard_map/ppermute | solution.py:274
  38.1 11.6 %collective-permute-start.3 = (bf16[32,8192]{1,0:T(8,128)(2,1)S(1)}, bf16[32,8192]{1,0:T(8,128)(2,1)S(1)}, u32[]{:S(2)}, u32[]{:S(2)}) collective-permute-start(bf16[32,8192]{1,0:T(8,128)(2,1)S(1)} %collective-permute-done.2.refs_1_), channel_id=1, source_target_pairs={{0,16},{16,32},{32,48},{48,64},{64,80},{80,96},{96,112},{112,0},{1... | collective-permute-start | bytes 1572872 | tf_op jit(solution)/shard_map/ppermute | solution.py:274
  38.1 11.6 %collective-permute-start.6 = (bf16[32,8192]{1,0:T(8,128)(2,1)S(1)}, bf16[32,8192]{1,0:T(8,128)(2,1)S(1)}, u32[]{:S(2)}, u32[]{:S(2)}) collective-permute-start(bf16[32,8192]{1,0:T(8,128)(2,1)S(1)} %collective-permute-done.5.refs_4_), channel_id=1, source_target_pairs={{0,112},{16,0},{32,16},{48,32},{64,48},{80,64},{96,80},{112,96},{1... | collective-permute-start | bytes 1572872 | tf_op jit(solution)/shard_map/ppermute | solution.py:274
  49.7 10.7 %collective-permute-start.4 = (bf16[32,8192]{1,0:T(8,128)(2,1)S(1)}, bf16[32,8192]{1,0:T(8,128)(2,1)S(1)}, u32[]{:S(2)}, u32[]{:S(2)}) collective-permute-start(bf16[32,8192]{1,0:T(8,128)(2,1)S(1)} %collective-permute-done.3.refs_2_), channel_id=1, source_target_pairs={{0,16},{16,32},{32,48},{48,64},{64,80},{80,96},{96,112},{112,0},{1... | collective-permute-start | bytes 1572872 | tf_op jit(solution)/shard_map/ppermute | solution.py:274
  49.7 10.7 %collective-permute-start.7 = (bf16[32,8192]{1,0:T(8,128)(2,1)S(1)}, bf16[32,8192]{1,0:T(8,128)(2,1)S(1)}, u32[]{:S(2)}, u32[]{:S(2)}) collective-permute-start(bf16[32,8192]{1,0:T(8,128)(2,1)S(1)} %collective-permute-done.6.refs_5_), channel_id=1, source_target_pairs={{0,112},{16,0},{32,16},{48,32},{64,48},{80,64},{96,80},{112,96},{1... | collective-permute-start | bytes 1572872 | tf_op jit(solution)/shard_map/ppermute | solution.py:274
  60.5 13.2 %copy-start.3 = (bf16[256,4096]{1,0:T(8,128)(2,1)S(1)}, bf16[256,4096]{1,0:T(8,128)(2,1)}, u32[]{:S(2)}) copy-start(bf16[256,4096]{1,0:T(8,128)(2,1)} %copy-done.2) | copy-start | bytes 6291460
  60.5 7.2 %collective-permute-start.8 = (bf16[16,8192]{1,0:T(8,128)(2,1)S(1)}, bf16[16,8192]{1,0:T(8,128)(2,1)S(1)}, u32[]{:S(2)}, u32[]{:S(2)}) collective-permute-start(bf16[16,8192]{1,0:T(8,128)(2,1)S(1)} %shard_map.80), channel_id=1, source_target_pairs={{0,16},{16,32},{32,48},{48,64},{64,80},{80,96},{96,112},{112,0},{1... | collective-permute-start | bytes 786440 | tf_op jit(solution)/shard_map/ppermute | solution.py:274
  60.6 7.1 %collective-permute-start.9 = (bf16[16,8192]{1,0:T(8,128)(2,1)S(1)}, bf16[16,8192]{1,0:T(8,128)(2,1)S(1)}, u32[]{:S(2)}, u32[]{:S(2)}) collective-permute-start(bf16[16,8192]{1,0:T(8,128)(2,1)S(1)} %shard_map.81), channel_id=1, source_target_pairs={{0,112},{16,0},{32,16},{48,32},{64,48},{80,64},{96,80},{112,96},{1... | collective-permute-start | bytes 786440 | tf_op jit(solution)/shard_map/ppermute | solution.py:274
  67.7 10.4 %collective-permute-start.12 = (bf16[256,4096]{1,0:T(8,128)(2,1)S(1)}, bf16[256,4096]{1,0:T(8,128)(2,1)S(1)}, u32[]{:S(2)}, u32[]{:S(2)}) collective-permute-start(bf16[256,4096]{1,0:T(8,128)(2,1)S(1)} %collective-permute-done.10.refs_13_), channel_id=1, source_target_pairs={{0,8},{8,0},{1,9},{9,1},{2,10},{10,2},{3,11},{11,3},{4,12},{12,4},... | collective-permute-start | bytes 6291464 | tf_op jit(solution)/shard_map/ppermute | solution.py:269
  73.4 6.8 %collective-permute-start.13 = (bf16[256,4096]{1,0:T(8,128)(2,1)S(1)}, bf16[256,4096]{1,0:T(8,128)(2,1)S(1)}, u32[]{:S(2)}, u32[]{:S(2)}) collective-permute-start(bf16[256,4096]{1,0:T(8,128)(2,1)S(1)} %collective-permute-done.11.refs_14_), channel_id=1, source_target_pairs={{0,8},{8,0},{1,9},{9,1},{2,10},{10,2},{3,11},{11,3},{4,12},{12,4},... | collective-permute-start | bytes 6291464 | tf_op jit(solution)/shard_map/ppermute | solution.py:269
  118.6 8.9 %copy-start.8 = (s32[16,8192]{1,0:T(8,128)S(1)}, s32[16,8192]{1,0:T(8,128)}, u32[]{:S(2)}) copy-start(s32[16,8192]{1,0:T(8,128)} %param.9) | copy-start | bytes 1572868
  118.6 9.0 %copy-start.9 = (f32[16]{0:T(128)S(1)}, f32[16]{0:T(128)}, u32[]{:S(2)}) copy-start(f32[16]{0:T(128)} %param.10) | copy-start | bytes 196
  118.6 36.9 %all-to-all-start.2 = ((f32[32,136,128]{2,1,0:T(8,128)}), f32[32,136,128]{2,1,0:T(8,128)S(1)}, u32[]{:S(2)}, u32[]{:S(2)}) async-start(f32[32,136,128]{2,1,0:T(8,128)} %shard_map.85), calls=%async_computation.2 | async-start | bytes 4456448 | tf_op jit(solution)/shard_map/all_to_all | solution.py:286
  127.6 0.8 copy-start.7
  155.6 1.0 copy-start.4

commit v10 on v9

--- a/solution.py
+++ b/solution.py
@@ -324,7 +324,8 @@
     near = multiply_near(place, blocks, (own_a, own_b, pair_a, pair_b, far_a, far_b))
     turn, home = multiply(place, blocks, (cross_a, cross_b), near)
 
-    tiles = exchange(pack(exchange(turn, "z"), home), PLANE)
+    turn, home, occupation = lax.optimization_barrier((turn, home, occupation))
+    turn = exchange(turn, "z")
 
     occ_float = occupation.astype(jnp.float32)
     occ_alpha = lax.dynamic_slice_in_dim(occ_float, row_index * rows, rows, 1)
@@ -338,6 +339,8 @@
     )
     diagonal = energy_alpha[:, None] + energy_beta[None, :] + coupling
 
+    turn, diagonal, coeff = lax.optimization_barrier((turn, diagonal, coeff))
+    tiles = exchange(pack(turn, home), PLANE)
     update, sums, theta = make_update(tiles, coeff, diagonal)
     correction, stats = finish(update, exchange(sums, AXES), theta)
     return (correction, stats[0, :2])

time: 179 us -> 181 us (1.011)
  waiting for transfers between devices: 55.7 us -> 60.9 us
  starting transfers between devices: 40.3 us -> 37.7 us
    all_to_all x2, starting transfers between devices: 14.3 us -> 11.2 us  [exchange(): return lax.all_to_all(value, axes, split_axis=0, concat_axis=0, tiled=True)]
    all_to_all x2, waiting for transfers between devices: 28.5 us -> 31.3 us  [exchange(): return lax.all_to_all(value, axes, split_axis=0, concat_axis=0, tiled=True)]
    ppermute x8, waiting for transfers between devices: 25.2 us -> 27.6 us  [shift(): lax.ppermute(value, 'z', [(i, (i + step) % count) for i in range(count)])]
    unnamed x20 -> x18, local copies, waits for them, and re-layouts: 5.35 us -> 4.27 us
  transfers between devices with their start and end apart: 16 -> 16, of which waited for: 7 -> 8; matrix products, arithmetic and copies ran while one was open for 1% -> 1% of each run, Pallas kernels for 7% -> 7%
where the time goes in v10:
time: 181 us; the launch traced here: 180 us
  waiting for transfers between devices  60.9 us (34%)
  blocking collectives  55.5 us (31%)
  starting transfers between devices  37.7 us (21%)
  Pallas kernels  19 us (10%)
  local copies, waits for them, and re-layouts  4.78 us (3%)
    all_to_all x2, blocking collectives, exchange(): return lax.all_to_all(value, axes, split_axis=0, concat_axis=0, tiled=True)  55.5 us
    all_to_all x2, waiting for transfers between devices, exchange(): return lax.all_to_all(value, axes, split_axis=0, concat_axis=0, tiled=True)  31.3 us
    ppermute x8, waiting for transfers between devices, shift(): lax.ppermute(value, 'z', [(i, (i + step) % count) for i in range(count)])  27.6 us
    ppermute x8, starting transfers between devices, shift(): lax.ppermute(value, 'z', [(i, (i + step) % count) for i in range(count)])  13.4 us
    all_to_all x2, starting transfers between devices, exchange(): return lax.all_to_all(value, axes, split_axis=0, concat_axis=0, tiled=True)  11.2 us
    ppermute x4, starting transfers between devices, swap(): return lax.ppermute(value, 'core', [(0, 1), (1, 0)])  10.4 us
    pallas_call x4, Pallas kernels, mask_half(): pl.pallas_call(mask_kernel, grid=(4,), in_specs=[pl.BlockSpec((rows, cols...  8.86 us
    pallas_call x1, Pallas kernels, multiply_near(): pl.pallas_call(near_kernel, in_specs=[pl.BlockSpec(memory_space=pltpu.SME...  4.42 us
  transfers between devices with their start and end apart: 16, of which 8 were waited for; matrix products, arithmetic and copies ran while one was open for 1% of the time, Pallas kernels for 7%

profile of v10, /device:TPU:1, one launch (start us, length us, event | category | flops | bytes accessed | tf_op | source)
XLA Modules:
  0.0 180.5 jit_solution(15546042899470865587)
XLA Ops:
  0.7 3.3 %collective-permute-start = (bf16[256,8192]{1,0:T(8,128)(2,1)}, bf16[256,8192]{1,0:T(8,128)(2,1)}, u32[]{:S(2)}, u32[]{:S(2)}) collective-permute-start(bf16[256,8192]{1,0:T(8,128)(2,1)} %ham_ref.1), channel_id=1, source_target_pairs={{0,8},{8,0},{1,9},{9,1},{2,10},{10,2},{3,11},{11,3},{4,12},{12,4},... | collective-permute-start | bytes 12582920 | tf_op jit(solution)/shard_map/ppermute | solution.py:269
  4.0 5.5 %all-to-all-start = ((bf16[32,8,1024]{2,1,0:T(8,128)(2,1)}), bf16[32,8,1024]{2,1,0:T(8,128)(2,1)S(1)}, u32[]{:S(2)}, u32[]{:S(2)}) async-start(bf16[32,8,1024]{2,1,0:T(8,128)(2,1)} %bitcast.29), calls=%async_computation | async-start | bytes 1048576 | tf_op jit(solution)/shard_map/all_to_all | solution.py:286
  9.8 2.2 %copy-done.1 = bf16[256,8192]{1,0:T(8,128)(2,1)S(1)} copy-done((bf16[256,8192]{1,0:T(8,128)(2,1)S(1)}, bf16[256,8192]{1,0:T(8,128)(2,1)}, u32[]{:S(2)}) %copy-start.1) | copy-done | bytes 4194328
  12.0 0.7 copy-done.5
  12.7 1.4 shard_map.78.refs_10_
  14.1 1.4 shard_map.77.refs_9_
  15.5 1.4 copy-done.2
  16.9 3.1 %all-to-all-done = bf16[32,8,1024]{2,1,0:T(8,128)(2,1)S(1)} async-done(((bf16[32,8,1024]{2,1,0:T(8,128)(2,1)}), bf16[32,8,1024]{2,1,0:T(8,128)(2,1)S(1)}, u32[]{:S(2)}, u32[]{:S(2)}) %all-to-all-start) | async-done | bytes 524320 | tf_op jit(solution)/shard_map/all_to_all | solution.py:286
  20.3 2.4 %collective-permute-start.11 = (bf16[256,4096]{1,0:T(8,128)(2,1)S(1)}, bf16[256,4096]{1,0:T(8,128)(2,1)S(1)}, u32[]{:S(2)}, u32[]{:S(2)}) collective-permute-start(bf16[256,4096]{1,0:T(8,128)(2,1)S(1)} %shard_map.78.refs_10_), channel_id=1, source_target_pairs={{0,132},{128,0},{4,128},{132,4},{1,133},{129,1},{5,129},{133,5},{2... | collective-permute-start | bytes 6291464 | tf_op jit(solution)/shard_map/ppermute | solution.py:282
  22.6 1.6 collective-permute-start.2
  24.3 3.9 %collective-permute-start.5 = (bf16[32,8192]{1,0:T(8,128)(2,1)S(1)}, bf16[32,8192]{1,0:T(8,128)(2,1)S(1)}, u32[]{:S(2)}, u32[]{:S(2)}) collective-permute-start(bf16[32,8192]{1,0:T(8,128)(2,1)S(1)} %bitcast.26), channel_id=1, source_target_pairs={{0,112},{16,0},{32,16},{48,32},{64,48},{80,64},{96,80},{112,96},{1... | collective-permute-start | bytes 1572872 | tf_op jit(solution)/shard_map/ppermute | solution.py:274
  28.2 9.9 %collective-permute-done.2.refs_1_ = bf16[32,8192]{1,0:T(8,128)(2,1)S(1)} collective-permute-done((bf16[32,8192]{1,0:T(8,128)(2,1)S(1)}, bf16[32,8192]{1,0:T(8,128)(2,1)S(1)}, u32[]{:S(2)}, u32[]{:S(2)}) %collective-permute-start.2) | collective-permute-done | bytes 524320 | tf_op jit(solution)/shard_map/ppermute | solution.py:274
  38.1 2.7 %collective-permute-start.6 = (bf16[32,8192]{1,0:T(8,128)(2,1)S(1)}, bf16[32,8192]{1,0:T(8,128)(2,1)S(1)}, u32[]{:S(2)}, u32[]{:S(2)}) collective-permute-start(bf16[32,8192]{1,0:T(8,128)(2,1)S(1)} %collective-permute-done.5.refs_4_), channel_id=1, source_target_pairs={{0,112},{16,0},{32,16},{48,32},{64,48},{80,64},{96,80},{112,96},{1... | collective-permute-start | bytes 1572872 | tf_op jit(solution)/shard_map/ppermute | solution.py:274
  40.8 3.0 %shard_map.79.refs_11_ = bf16[256,4096]{1,0:T(8,128)(2,1)S(1)} custom-call(bf16[256,8192]{1,0:T(8,128)(2,1)} %collective-permute-done.ham_ref, s32[8,256]{1,0:T(8,128)S(1)} %collective-permute-done.1.mask_ref), custom_call_target="tpu_custom_call" | custom-call | flops 2097152 | bytes 4194304 | tf_op jit(solution)/shard_map/pallas_call | solution.py:40
  43.8 5.9 %collective-permute-done.3.refs_2_ = bf16[32,8192]{1,0:T(8,128)(2,1)S(1)} collective-permute-done((bf16[32,8192]{1,0:T(8,128)(2,1)S(1)}, bf16[32,8192]{1,0:T(8,128)(2,1)S(1)}, u32[]{:S(2)}, u32[]{:S(2)}) %collective-permute-start.3) | collective-permute-done | bytes 524320 | tf_op jit(solution)/shard_map/ppermute | solution.py:274
  49.7 2.4 %collective-permute-start.7 = (bf16[32,8192]{1,0:T(8,128)(2,1)S(1)}, bf16[32,8192]{1,0:T(8,128)(2,1)S(1)}, u32[]{:S(2)}, u32[]{:S(2)}) collective-permute-start(bf16[32,8192]{1,0:T(8,128)(2,1)S(1)} %collective-permute-done.6.refs_5_), channel_id=1, source_target_pairs={{0,112},{16,0},{32,16},{48,32},{64,48},{80,64},{96,80},{112,96},{1... | collective-permute-start | bytes 1572872 | tf_op jit(solution)/shard_map/ppermute | solution.py:274
  52.1 7.1 %collective-permute-done.7.value_ref.refs_6_ = bf16[32,8192]{1,0:T(8,128)(2,1)S(1)} collective-permute-done((bf16[32,8192]{1,0:T(8,128)(2,1)S(1)}, bf16[32,8192]{1,0:T(8,128)(2,1)S(1)}, u32[]{:S(2)}, u32[]{:S(2)}) %collective-permute-start.7) | collective-permute-done | bytes 524320 | tf_op jit(solution)/shard_map/ppermute | solution.py:274
  59.2 3.0 %collective-permute-done.4.value_ref.refs_3_ = bf16[32,8192]{1,0:T(8,128)(2,1)S(1)} collective-permute-done((bf16[32,8192]{1,0:T(8,128)(2,1)S(1)}, bf16[32,8192]{1,0:T(8,128)(2,1)S(1)}, u32[]{:S(2)}, u32[]{:S(2)}) %collective-permute-start.4) | collective-permute-done | bytes 524320 | tf_op jit(solution)/shard_map/ppermute | solution.py:274
  62.4 2.7 %collective-permute-start.9 = (bf16[16,8192]{1,0:T(8,128)(2,1)S(1)}, bf16[16,8192]{1,0:T(8,128)(2,1)S(1)}, u32[]{:S(2)}, u32[]{:S(2)}) collective-permute-start(bf16[16,8192]{1,0:T(8,128)(2,1)S(1)} %shard_map.81), channel_id=1, source_target_pairs={{0,112},{16,0},{32,16},{48,32},{64,48},{80,64},{96,80},{112,96},{1... | collective-permute-start | bytes 786440 | tf_op jit(solution)/shard_map/ppermute | solution.py:274
  65.1 3.0 %shard_map.82.refs_12_ = bf16[256,4096]{1,0:T(8,128)(2,1)S(1)} custom-call(bf16[256,8192]{1,0:T(8,128)(2,1)} %collective-permute-done.ham_ref, s32[8,256]{1,0:T(8,128)S(1)} %collective-permute-done.1.mask_ref), custom_call_target="tpu_custom_call" | custom-call | flops 2097152 | bytes 4194304 | tf_op jit(solution)/shard_map/pallas_call | solution.py:40
  68.1 1.7 collective-permute-done.8.refs_7_
  69.8 6.6 %collective-permute-start.12 = (bf16[256,4096]{1,0:T(8,128)(2,1)S(1)}, bf16[256,4096]{1,0:T(8,128)(2,1)S(1)}, u32[]{:S(2)}, u32[]{:S(2)}) collective-permute-start(bf16[256,4096]{1,0:T(8,128)(2,1)S(1)} %collective-permute-done.10.refs_13_), channel_id=1, source_target_pairs={{0,8},{8,0},{1,9},{9,1},{2,10},{10,2},{3,11},{11,3},{4,12},{12,4},... | collective-permute-start | bytes 6291464 | tf_op jit(solution)/shard_map/ppermute | solution.py:269
  76.7 4.4 %shard_map.83.refs_11_ = f32[256,768]{1,0:T(8,128)S(1)} custom-call(s32[3]{0:T(128)S(1)} %pad_add_fusion.place_ref, bf16[32,8192]{1,0:T(8,128)(2,1)S(1)} %bitcast.27, bf16[32,8192]{1,0:T(8,128)(2,1)S(1)} %collective-permute-done.2.refs_1_, bf16[32,8192]{1,0:T(8,128)(2,1)S(1)} %collective-permute-done.3.refs_2_, ...), custom_call_target="tpu_custom_call" | custom-call | flops 3221225472 | bytes 16777216 | tf_op jit(solution)/shard_map/pallas_call | solution.py:130
  81.1 2.1 %collective-permute-done.13.refs_10_ = bf16[256,4096]{1,0:T(8,128)(2,1)S(1)} collective-permute-done((bf16[256,4096]{1,0:T(8,128)(2,1)S(1)}, bf16[256,4096]{1,0:T(8,128)(2,1)S(1)}, u32[]{:S(2)}, u32[]{:S(2)}) %collective-permute-start.13) | collective-permute-done | bytes 2097184 | tf_op jit(solution)/shard_map/ppermute | solution.py:269
  83.2 3.6 %shard_map.84 = (f32[8,264,128]{2,1,0:T(8,128)}, f32[32,64,128]{2,1,0:T(8,128)S(1)}) custom-call(s32[3]{0:T(128)S(1)} %pad_add_fusion.place_ref, bf16[32,8192]{1,0:T(8,128)(2,1)S(1)} %bitcast.28, bf16[32,8192]{1,0:T(8,128)(2,1)S(1)} %collective-permute-done.2.refs_1_, bf16[32,8192]{1,0:T(8,128)(2,1)S(1)} %collective-permute-done.3.refs_2_, ...), custom_call_target="tpu_custom_call" | custom-call | flops 1073741824 | bytes 12582912 | tf_op jit(solution)/shard_map/pallas_call | solution.py:148
  86.8 5.7 %all-to-all-start.1 = ((f32[8,264,128]{2,1,0:T(8,128)}), f32[8,264,128]{2,1,0:T(8,128)S(1)}, u32[]{:S(2)}, u32[]{:S(2)}) async-start(f32[8,264,128]{2,1,0:T(8,128)} %get-tuple-element.59), calls=%async_computation.1 | async-start | bytes 2162688 | tf_op jit(solution)/shard_map/all_to_all | solution.py:286
  93.3 1.0 convolution_add_fusion.diag_ref
  94.3 28.2 %all-to-all-done.1.turn_ref = f32[8,264,128]{2,1,0:T(8,128)S(1)} async-done(((f32[8,264,128]{2,1,0:T(8,128)}), f32[8,264,128]{2,1,0:T(8,128)S(1)}, u32[]{:S(2)}, u32[]{:S(2)}) %all-to-all-start.1) | async-done | bytes 1081376 | tf_op jit(solution)/shard_map/all_to_all | solution.py:286
  122.6 37.0 %all_to_all.26.tiles_ref = f32[32,136,128]{2,1,0:T(8,128)S(1)} all-to-all(f32[32,136,128]{2,1,0:T(8,128)S(1)} %shard_map.85), channel_id=1, replica_groups=mesh['xlo'=2,'z'=8,'core'=2,'xhi'=2,'y'=4] {'xlo','core','xhi','y'}, dimensions={0} | all-to-all | bytes 4456448 | tf_op jit(solution)/shard_map/all_to_all | solution.py:286
  159.6 0.8 shard_map.86
  160.3 18.5 %all_to_all.27 = f32[256,1,128]{2,1,0:T(1,128)S(1)} all-to-all(f32[256,1,128]{2,1,0:T(1,128)S(1)} %bitcast.31), channel_id=1, replica_groups=mesh['xlo'=2,'z'=8,'core'=2,'xhi'=2,'y'=4] {'xlo','z','core','xhi','y'}, dimensions={0} | all-to-all | bytes 262144 | tf_op jit(solution)/shard_map/all_to_all | solution.py:286
  178.8 1.2 shard_map.87
  (38 shorter events, 2.6 us)
Async XLA Ops:
  0.6 92.2 %copy-start = (f32[16,16]{1,0:T(8,128)S(1)}, f32[16,16]{1,0:T(8,128)}, u32[]{:S(2)}) copy-start(f32[16,16]{1,0:T(8,128)} %param.11) | copy-start | bytes 3076
  0.7 19.2 %collective-permute-start = (bf16[256,8192]{1,0:T(8,128)(2,1)}, bf16[256,8192]{1,0:T(8,128)(2,1)}, u32[]{:S(2)}, u32[]{:S(2)}) collective-permute-start(bf16[256,8192]{1,0:T(8,128)(2,1)} %ham_ref.1), channel_id=1, source_target_pairs={{0,8},{8,0},{1,9},{9,1},{2,10},{10,2},{3,11},{11,3},{4,12},{12,4},... | collective-permute-start | bytes 12582920 | tf_op jit(solution)/shard_map/ppermute | solution.py:269
  4.0 16.0 %all-to-all-start = ((bf16[32,8,1024]{2,1,0:T(8,128)(2,1)}), bf16[32,8,1024]{2,1,0:T(8,128)(2,1)S(1)}, u32[]{:S(2)}, u32[]{:S(2)}) async-start(bf16[32,8,1024]{2,1,0:T(8,128)(2,1)} %bitcast.29), calls=%async_computation | async-start | bytes 1048576 | tf_op jit(solution)/shard_map/all_to_all | solution.py:286
  9.5 7.4 %collective-permute-start.1 = (s32[8,256]{1,0:T(8,128)}, s32[8,256]{1,0:T(8,128)S(1)}, u32[]{:S(2)}, u32[]{:S(2)}) collective-permute-start(s32[8,256]{1,0:T(8,128)} %mask_ref.3), channel_id=1, source_target_pairs={{0,8},{8,0},{1,9},{9,1},{2,10},{10,2},{3,11},{11,3},{4,12},{12,4},... | collective-permute-start | bytes 24584 | tf_op jit(solution)/shard_map/ppermute | solution.py:269
  9.8 2.2 %copy-start.1 = (bf16[256,8192]{1,0:T(8,128)(2,1)S(1)}, bf16[256,8192]{1,0:T(8,128)(2,1)}, u32[]{:S(2)}) copy-start(bf16[256,8192]{1,0:T(8,128)(2,1)} %ham_ref.1) | copy-start | bytes 12582916
  12.0 0.7 copy-start.5
  12.7 1.4 copy-start.6
  15.5 1.4 copy-start.2
  20.0 49.8 %collective-permute-start.10 = (bf16[256,4096]{1,0:T(8,128)(2,1)}, bf16[256,4096]{1,0:T(8,128)(2,1)S(1)}, u32[]{:S(2)}, u32[]{:S(2)}) collective-permute-start(bf16[256,4096]{1,0:T(8,128)(2,1)} %copy-done.2), channel_id=1, source_target_pairs={{0,128},{128,4},{4,132},{132,0},{1,129},{129,5},{5,133},{133,1},{2... | collective-permute-start | bytes 6291464 | tf_op jit(solution)/shard_map/ppermute | solution.py:282
  20.3 49.5 %collective-permute-start.11 = (bf16[256,4096]{1,0:T(8,128)(2,1)S(1)}, bf16[256,4096]{1,0:T(8,128)(2,1)S(1)}, u32[]{:S(2)}, u32[]{:S(2)}) collective-permute-start(bf16[256,4096]{1,0:T(8,128)(2,1)S(1)} %shard_map.78.refs_10_), channel_id=1, source_target_pairs={{0,132},{128,0},{4,128},{132,4},{1,133},{129,1},{5,129},{133,5},{2... | collective-permute-start | bytes 6291464 | tf_op jit(solution)/shard_map/ppermute | solution.py:282
  22.6 15.5 %collective-permute-start.2 = (bf16[32,8192]{1,0:T(8,128)(2,1)S(1)}, bf16[32,8192]{1,0:T(8,128)(2,1)S(1)}, u32[]{:S(2)}, u32[]{:S(2)}) collective-permute-start(bf16[32,8192]{1,0:T(8,128)(2,1)S(1)} %bitcast.25), channel_id=1, source_target_pairs={{0,16},{16,32},{32,48},{48,64},{64,80},{80,96},{96,112},{112,0},{1... | collective-permute-start | bytes 1572872 | tf_op jit(solution)/shard_map/ppermute | solution.py:274
  24.3 13.8 %collective-permute-start.5 = (bf16[32,8192]{1,0:T(8,128)(2,1)S(1)}, bf16[32,8192]{1,0:T(8,128)(2,1)S(1)}, u32[]{:S(2)}, u32[]{:S(2)}) collective-permute-start(bf16[32,8192]{1,0:T(8,128)(2,1)S(1)} %bitcast.26), channel_id=1, source_target_pairs={{0,112},{16,0},{32,16},{48,32},{64,48},{80,64},{96,80},{112,96},{1... | collective-permute-start | bytes 1572872 | tf_op jit(solution)/shard_map/ppermute | solution.py:274
  38.1 11.6 %collective-permute-start.3 = (bf16[32,8192]{1,0:T(8,128)(2,1)S(1)}, bf16[32,8192]{1,0:T(8,128)(2,1)S(1)}, u32[]{:S(2)}, u32[]{:S(2)}) collective-permute-start(bf16[32,8192]{1,0:T(8,128)(2,1)S(1)} %collective-permute-done.2.refs_1_), channel_id=1, source_target_pairs={{0,16},{16,32},{32,48},{48,64},{64,80},{80,96},{96,112},{112,0},{1... | collective-permute-start | bytes 1572872 | tf_op jit(solution)/shard_map/ppermute | solution.py:274
  38.1 11.6 %collective-permute-start.6 = (bf16[32,8192]{1,0:T(8,128)(2,1)S(1)}, bf16[32,8192]{1,0:T(8,128)(2,1)S(1)}, u32[]{:S(2)}, u32[]{:S(2)}) collective-permute-start(bf16[32,8192]{1,0:T(8,128)(2,1)S(1)} %collective-permute-done.5.refs_4_), channel_id=1, source_target_pairs={{0,112},{16,0},{32,16},{48,32},{64,48},{80,64},{96,80},{112,96},{1... | collective-permute-start | bytes 1572872 | tf_op jit(solution)/shard_map/ppermute | solution.py:274
  49.7 9.5 %collective-permute-start.7 = (bf16[32,8192]{1,0:T(8,128)(2,1)S(1)}, bf16[32,8192]{1,0:T(8,128)(2,1)S(1)}, u32[]{:S(2)}, u32[]{:S(2)}) collective-permute-start(bf16[32,8192]{1,0:T(8,128)(2,1)S(1)} %collective-permute-done.6.refs_5_), channel_id=1, source_target_pairs={{0,112},{16,0},{32,16},{48,32},{64,48},{80,64},{96,80},{112,96},{1... | collective-permute-start | bytes 1572872 | tf_op jit(solution)/shard_map/ppermute | solution.py:274
  52.1 10.1 %collective-permute-start.4 = (bf16[32,8192]{1,0:T(8,128)(2,1)S(1)}, bf16[32,8192]{1,0:T(8,128)(2,1)S(1)}, u32[]{:S(2)}, u32[]{:S(2)}) collective-permute-start(bf16[32,8192]{1,0:T(8,128)(2,1)S(1)} %collective-permute-done.3.refs_2_), channel_id=1, source_target_pairs={{0,16},{16,32},{32,48},{48,64},{64,80},{80,96},{96,112},{112,0},{1... | collective-permute-start | bytes 1572872 | tf_op jit(solution)/shard_map/ppermute | solution.py:274
  62.3 14.4 %copy-start.3 = (bf16[256,4096]{1,0:T(8,128)(2,1)S(1)}, bf16[256,4096]{1,0:T(8,128)(2,1)}, u32[]{:S(2)}) copy-start(bf16[256,4096]{1,0:T(8,128)(2,1)} %copy-done.2) | copy-start | bytes 6291460
  62.3 7.5 %collective-permute-start.8 = (bf16[16,8192]{1,0:T(8,128)(2,1)S(1)}, bf16[16,8192]{1,0:T(8,128)(2,1)S(1)}, u32[]{:S(2)}, u32[]{:S(2)}) collective-permute-start(bf16[16,8192]{1,0:T(8,128)(2,1)S(1)} %shard_map.80), channel_id=1, source_target_pairs={{0,16},{16,32},{32,48},{48,64},{64,80},{80,96},{96,112},{112,0},{1... | collective-permute-start | bytes 786440 | tf_op jit(solution)/shard_map/ppermute | solution.py:274
  62.4 7.4 %collective-permute-start.9 = (bf16[16,8192]{1,0:T(8,128)(2,1)S(1)}, bf16[16,8192]{1,0:T(8,128)(2,1)S(1)}, u32[]{:S(2)}, u32[]{:S(2)}) collective-permute-start(bf16[16,8192]{1,0:T(8,128)(2,1)S(1)} %shard_map.81), channel_id=1, source_target_pairs={{0,112},{16,0},{32,16},{48,32},{64,48},{80,64},{96,80},{112,96},{1... | collective-permute-start | bytes 786440 | tf_op jit(solution)/shard_map/ppermute | solution.py:274
  69.8 11.3 %collective-permute-start.12 = (bf16[256,4096]{1,0:T(8,128)(2,1)S(1)}, bf16[256,4096]{1,0:T(8,128)(2,1)S(1)}, u32[]{:S(2)}, u32[]{:S(2)}) collective-permute-start(bf16[256,4096]{1,0:T(8,128)(2,1)S(1)} %collective-permute-done.10.refs_13_), channel_id=1, source_target_pairs={{0,8},{8,0},{1,9},{9,1},{2,10},{10,2},{3,11},{11,3},{4,12},{12,4},... | collective-permute-start | bytes 6291464 | tf_op jit(solution)/shard_map/ppermute | solution.py:269
  76.4 6.8 %collective-permute-start.13 = (bf16[256,4096]{1,0:T(8,128)(2,1)S(1)}, bf16[256,4096]{1,0:T(8,128)(2,1)S(1)}, u32[]{:S(2)}, u32[]{:S(2)}) collective-permute-start(bf16[256,4096]{1,0:T(8,128)(2,1)S(1)} %collective-permute-done.11.refs_14_), channel_id=1, source_target_pairs={{0,8},{8,0},{1,9},{9,1},{2,10},{10,2},{3,11},{11,3},{4,12},{12,4},... | collective-permute-start | bytes 6291464 | tf_op jit(solution)/shard_map/ppermute | solution.py:269
  86.8 5.7 %copy-start.7 = (s32[16,8192]{1,0:T(8,128)S(1)}, s32[16,8192]{1,0:T(8,128)}, u32[]{:S(2)}) copy-start(s32[16,8192]{1,0:T(8,128)} %param.9) | copy-start | bytes 1572868
  86.8 5.8 %copy-start.8 = (f32[16]{0:T(128)S(1)}, f32[16]{0:T(128)}, u32[]{:S(2)}) copy-start(f32[16]{0:T(128)} %param.10) | copy-start | bytes 196
  86.8 35.7 %all-to-all-start.1 = ((f32[8,264,128]{2,1,0:T(8,128)}), f32[8,264,128]{2,1,0:T(8,128)S(1)}, u32[]{:S(2)}, u32[]{:S(2)}) async-start(f32[8,264,128]{2,1,0:T(8,128)} %get-tuple-element.59), calls=%async_computation.1 | async-start | bytes 2162688 | tf_op jit(solution)/shard_map/all_to_all | solution.py:286
  122.6 37.0 %copy-start.4 = (bf16[256,1024]{1,0:T(8,128)(2,1)S(1)}, bf16[256,1024]{1,0:T(8,128)(2,1)}, u32[]{:S(2)}) copy-start(bf16[256,1024]{1,0:T(8,128)(2,1)} %coeff_ref) | copy-start | bytes 1572868
